TPU v7x, 32 devices: a whole 2x2x4 slice. The times are simulated.
32 devices in a mesh: gx: 8 (over z, x), gy: 4 (over y, core).
Axes of the slice: x: 2, y: 2, z: 4, core: 2. Of those that a mesh axis runs over, the one named last changes fastest.
Arguments:
- point_counts: int32 [128, 64, 128], P('gx', 'gy'), may hold values from 0 to 16
- face_counts: int32 [3, 128, 64, 128], P(None, 'gx', 'gy'), may hold values from -12 to 12, as said below
Outputs:
- solution: float32 [128, 64, 128], P('gx', 'gy')
- residual: float32 [128, 64, 128], P('gx', 'gy')
Inputs may be any that keep to these rules, and one draw needn't show every extreme that they name: `face_counts`: signed count of oriented points splatted onto each upper face.
All inputs are finite; a program needn't handle non-finite values.
Results may differ from a plain program's by a relative error of at most 0.0003.
Values may be sent and summed in bfloat16 or wider, within the bound.
No kernel may reach another device: no remote copies, remote signals or barrier semaphores. Data moves between devices by JAX's collectives and lax.ppermute only.
A program may use at most 64 MiB of HBM per device.

v0:
```python
import jax
import jax.numpy as jnp
from jax import lax
from jax.sharding import PartitionSpec as P

LEVELS = 3
CYCLES = 2
COARSE_ITERS = 6


screen_weight = 0.25
flux_scale = 0.125
low_edge = 0.3
high_edge = 2.0


def padded_2(block, sides, width):
    for axis, dim in sides:
        count = lax.axis_size(axis)
        forward = [(i, i + 1) for i in range(count - 1)]
        backward = [(target, source) for source, target in forward]
        low = lax.ppermute(
            lax.slice_in_dim(block, block.shape[dim] - width, None, axis=dim), axis, forward
        )
        high = lax.ppermute(lax.slice_in_dim(block, 0, width, axis=dim), axis, backward)
        block = jnp.concatenate([low, block, high], axis=dim)
    return block


def shifted(value, axis, steps):
    count = lax.axis_size(axis)
    first, last = (max(0, -steps), min(count, count - steps))
    return lax.ppermute(value, axis, [(source, source + steps) for source in range(first, last)])


def neighbour_sum(padded):
    total = padded[2:, 1:-1, 1:-1] + padded[:-2, 1:-1, 1:-1]
    total = total + padded[1:-1, 2:, 1:-1] + padded[1:-1, :-2, 1:-1]
    total = total + padded[1:-1, 1:-1, 2:] + padded[1:-1, 1:-1, :-2]
    return total


def extend(field, level_index):
    if level_index == 0:
        padded = padded_2(field, (("gx", 0), ("gy", 1)), 1)
    else:
        padded = padded_2(field, (("gx", 0), ("gy", 1)), 1)
    return jnp.pad(padded, ((0, 0), (0, 0), (1, 1)))


def operate(field, screen, factor, level_index):
    return (6.0 * field - neighbour_sum(extend(field, level_index))) * factor + screen * field


def operate_whole(field, screen, factor):
    return (6.0 * field - neighbour_sum(jnp.pad(field, 1))) * factor + screen * field


def restrict(field):
    size_x, size_y, size_z = field.shape
    blocks = field.reshape(size_x // 2, 2, size_y // 2, 2, size_z // 2, 2)
    return blocks.sum(axis=(1, 3, 5)) * 0.125


def prolong(field):
    size_x, size_y, size_z = field.shape
    spread_out = jnp.broadcast_to(
        field[:, None, :, None, :, None], (size_x, 2, size_y, 2, size_z, 2)
    )
    return spread_out.reshape(2 * size_x, 2 * size_y, 2 * size_z)


def smooth(iterate, target, screen, inv_diag, factor, level_index):
    centre = 0.5 * (high_edge + low_edge)
    radius = 0.5 * (high_edge - low_edge)
    spread_ratio = centre / radius
    momentum = 1.0 / spread_ratio
    correction = (target - operate(iterate, screen, factor, level_index)) * inv_diag
    update = correction * (1.0 / centre)
    iterate = iterate + update
    momentum_next = 1.0 / (2.0 * spread_ratio - momentum)
    correction = (target - operate(iterate, screen, factor, level_index)) * inv_diag
    update = momentum_next * momentum * update + 2.0 * momentum_next / radius * correction
    iterate = iterate + update
    return iterate


def whole_solve(target, screen, factor):
    iterate = jnp.zeros_like(target)
    remain = target
    search = target
    norm_now = jnp.sum(remain * remain)
    for step in range(COARSE_ITERS):
        image = operate_whole(search, screen, factor)
        step_length = norm_now / jnp.sum(search * image)
        iterate = iterate + step_length * search
        if step + 1 < COARSE_ITERS:
            remain = remain - step_length * image
            norm_next = jnp.sum(remain * remain)
            search = remain + norm_next / norm_now * search
            norm_now = norm_next
    return iterate


def assemble(gathered, piece_shape):
    size_x, size_y, size_z = piece_shape
    count_x = lax.axis_size("gx")
    count_y = lax.axis_size("gy")
    blocks = gathered.reshape(count_x, count_y, size_x, size_y, size_z)
    return blocks.transpose(0, 2, 1, 3, 4).reshape(count_x * size_x, count_y * size_y, size_z)


def own_block(whole_grid, piece_shape):
    size_x, size_y, size_z = piece_shape
    start = (lax.axis_index("gx") * size_x, lax.axis_index("gy") * size_y, jnp.zeros((), jnp.int32))
    return lax.dynamic_slice(whole_grid, start, (size_x, size_y, size_z))


def per_device(point_counts, face_counts):
    fluxes = face_counts.astype(jnp.float32) * flux_scale
    edge_x = shifted(fluxes[0, -1:].astype(jnp.bfloat16), "gx", 1).astype(jnp.float32)
    edge_y = shifted(fluxes[1, :, -1:].astype(jnp.bfloat16), "gy", 1).astype(jnp.float32)
    lower_x = jnp.concatenate([edge_x, fluxes[0, :-1]], axis=0)
    lower_y = jnp.concatenate([edge_y, fluxes[1, :, :-1]], axis=1)
    lower_z = jnp.pad(fluxes[2], ((0, 0), (0, 0), (1, 0)))[:, :, :-1]
    source = lower_x - fluxes[0] + (lower_y - fluxes[1]) + (lower_z - fluxes[2])
    screens = [point_counts.astype(jnp.float32) * screen_weight]
    for level_index in range(LEVELS):
        screens.append(restrict(screens[-1]))
    factors = [0.25**level_index for level_index in range(LEVELS + 1)]
    inv_diags = [
        1.0 / (6.0 * factors[level_index] + screens[level_index]) for level_index in range(LEVELS)
    ]
    coarse_shape = screens[LEVELS].shape
    screen_whole = assemble(
        lax.all_gather(screens[LEVELS], ("gx", "gy"), axis=0, tiled=True), coarse_shape
    )

    def vcycle(iterate, target, level_index):
        iterate = smooth(
            iterate,
            target,
            screens[level_index],
            inv_diags[level_index],
            factors[level_index],
            level_index,
        )
        remain = target - operate(iterate, screens[level_index], factors[level_index], level_index)
        coarse_target = restrict(remain)
        if level_index + 1 == LEVELS:
            target_whole = assemble(
                lax.all_gather(coarse_target, ("gx", "gy"), axis=0, tiled=True), coarse_shape
            )
            coarse_error = own_block(
                whole_solve(target_whole, screen_whole, factors[LEVELS]), coarse_shape
            )
        else:
            coarse_error = vcycle(jnp.zeros_like(coarse_target), coarse_target, level_index + 1)
        iterate = iterate + prolong(coarse_error)
        return smooth(
            iterate,
            target,
            screens[level_index],
            inv_diags[level_index],
            factors[level_index],
            level_index,
        )

    solution = jnp.zeros_like(source)
    for cycle_index in range(CYCLES):
        solution = vcycle(solution, source, 0)
    residual = source - operate(solution, screens[0], factors[0], 0)
    return (solution, residual)


def solution(mesh):
    return jax.shard_map(
        per_device,
        mesh=mesh,
        in_specs=(P("gx", "gy", None), P(None, "gx", "gy", None)),
        out_specs=(P("gx", "gy", None), P("gx", "gy", None)),
        check_vma=False,
    )
```

profile of v0, /device:TPU:0, one launch (start us, length us, event | category | flops | bytes accessed | tf_op | source)
XLA Modules:
  0.0 673.9 jit_solution(741098386323297001)
XLA Ops:
  1.9 5.5 collective-permute-start.3
  10.0 4.7 collective-permute-start
  16.0 4.5 collective-permute-start.5
  24.0 4.5 collective-permute-start.7
  35.7 4.7 collective-permute-start.15
  43.1 5.4 collective-permute-start.11
  49.9 5.2 collective-permute-start.17
  56.4 4.3 collective-permute-start.13
  60.9 9.8 %reshape.102 = f32[8,2,8,2,64,2]{5,4,3,2,1,0:T(8,128)} reshape(f32[16,16,128]{2,1,0:T(8,128)S(1)} %get-tuple-element.97) | data formatting | bytes 262144 | tf_op jit(solution)/shard_map/reshape | solution.py:61
  70.7 4.0 reduce_sum.298
  75.1 9.8 %reshape.101 = f32[8,2,8,2,64,2]{5,4,3,2,1,0:T(8,128)} reshape(f32[16,16,128]{2,1,0:T(8,128)S(1)} %fusion.77) | data formatting | bytes 262144 | tf_op jit(solution)/shard_map/reshape | solution.py:61
  84.9 4.0 reduce_sum.297
  90.3 5.2 collective-permute-start.19
  102.8 5.2 collective-permute-start.27
  109.6 5.6 collective-permute-start.23
  116.5 3.5 collective-permute-start.29
  121.4 4.3 collective-permute-start.25
  129.9 5.2 collective-permute-start.31
  143.4 5.2 collective-permute-start.35
  151.2 4.4 collective-permute-start.37
  155.5 46.9 %all_gather.10 = f32[64,2,16]{2,1,0:T(2,128)S(1)} all-gather(f32[2,2,16]{2,1,0:T(2,128)S(1)} %broadcast_multiply_fusion.4), channel_id=1, replica_groups=mesh['gx'=8,'gy'=4] {'gx','gy'}, dimensions={0}, use_global_device_ids=true | all-gather | bytes 8448 | tf_op jit(solution)/shard_map/all_gather | solution.py:136
  202.9 36.8 %all_gather.9 = f32[64,2,16]{2,1,0:T(2,128)S(1)} all-gather(f32[2,2,16]{2,1,0:T(2,128)S(1)} %broadcast_multiply_fusion.5), channel_id=1, replica_groups=mesh['gx'=8,'gy'=4] {'gx','gy'}, dimensions={0}, use_global_device_ids=true | all-gather | bytes 8448 | tf_op jit(solution)/shard_map/all_gather | solution.py:152
  264.4 4.5 collective-permute-start.39
  276.8 4.8 collective-permute-start.43
  290.4 5.4 collective-permute-start.47
  298.5 4.6 collective-permute-start.49
  305.5 5.7 collective-permute-start.51
  313.8 4.7 collective-permute-start.53
  319.6 3.9 broadcast_in_dim.14
  323.5 6.9 %reshape.111 = f32[16,16,128]{2,1,0:T(8,128)S(1)} reshape(f32[8,2,8,2,64,2]{5,4,3,2,1,0:T(8,128)} %broadcast_in_dim.14) | data formatting | bytes 262144 | tf_op jit(solution)/shard_map/reshape | solution.py:70
  331.8 5.7 collective-permute-start.55
  340.1 4.8 collective-permute-start.57
  347.5 5.7 collective-permute-start.59
  355.8 4.8 collective-permute-start.61
  363.2 5.7 collective-permute-start.63
  371.6 4.8 collective-permute-start.65
  378.9 5.7 collective-permute-start.67
  387.3 4.8 collective-permute-start.69
  394.7 5.7 collective-permute-start.71
  403.0 4.8 collective-permute-start.73
  409.0 9.8 %reshape.112 = f32[8,2,8,2,64,2]{5,4,3,2,1,0:T(8,128)} reshape(f32[16,16,128]{2,1,0:T(8,128)S(1)} %fusion.37) | data formatting | bytes 262144 | tf_op jit(solution)/shard_map/reshape | solution.py:61
  418.8 4.0 reduce_sum.315
  424.2 5.7 collective-permute-start.75
  432.5 4.8 collective-permute-start.77
  439.7 5.7 collective-permute-start.79
  448.0 4.8 collective-permute-start.81
  456.4 5.7 collective-permute-start.83
  464.7 4.8 collective-permute-start.85
  471.7 5.7 collective-permute-start.87
  480.0 4.7 collective-permute-start.89
  486.0 50.8 %all_gather.11 = f32[64,2,16]{2,1,0:T(2,128)S(1)} all-gather(f32[2,2,16]{2,1,0:T(2,128)S(1)} %broadcast_multiply_fusion.3), channel_id=1, replica_groups=mesh['gx'=8,'gy'=4] {'gx','gy'}, dimensions={0}, use_global_device_ids=true | all-gather | bytes 8448 | tf_op jit(solution)/shard_map/all_gather | solution.py:152
  561.2 4.5 collective-permute-start.91
  573.7 4.8 collective-permute-start.95
  587.3 5.4 collective-permute-start.99
  601.2 5.7 collective-permute-start.103
  609.5 4.7 collective-permute-start.105
  615.3 3.9 broadcast_in_dim.17
  619.2 6.9 %reshape.119 = f32[16,16,128]{2,1,0:T(8,128)S(1)} reshape(f32[8,2,8,2,64,2]{5,4,3,2,1,0:T(8,128)} %broadcast_in_dim.17) | data formatting | bytes 262144 | tf_op jit(solution)/shard_map/reshape | solution.py:70
  627.5 5.7 collective-permute-start.107
  635.9 4.8 collective-permute-start.109
  643.2 5.7 collective-permute-start.111
  651.5 4.8 collective-permute-start.113
  658.9 5.7 collective-permute-start.115
  667.3 4.8 collective-permute-start.117
  (389 shorter events, 185.7 us)
Async XLA Ops:
  0.6 14.0 %collective-permute-start.2 = (f32[1,16,128]{2,1,0:T(8,128)S(1)}, f32[1,16,128]{2,1,0:T(8,128)S(1)}, u32[]{:S(2)}, u32[]{:S(2)}) collective-permute-start(f32[1,16,128]{2,1,0:T(8,128)S(1)} %broadcast.198), channel_id=1, source_target_pairs={{4,0},{8,4},{12,8},{16,12},{20,16},{24,20},{28,24},{5,1},{9,5},{13... | collective-permute-start | bytes 24584 | tf_op jit(solution)/shard_map/ppermute | solution.py:25
  1.9 12.7 %collective-permute-start.3 = (f32[1,16,128]{2,1,0:T(8,128)S(1)}, f32[1,16,128]{2,1,0:T(8,128)S(1)}, u32[]{:S(2)}, u32[]{:S(2)}) collective-permute-start(f32[1,16,128]{2,1,0:T(8,128)S(1)} %broadcast.198), channel_id=1, source_target_pairs={{0,4},{4,8},{8,12},{12,16},{16,20},{20,24},{24,28},{1,5},{5,9},{9,... | collective-permute-start | bytes 24584 | tf_op jit(solution)/shard_map/ppermute | solution.py:22
  8.5 12.1 %collective-permute-start.1 = (bf16[16,1,128]{2,1,0:T(2,128)(2,1)S(1)}, bf16[16,1,128]{2,1,0:T(2,128)(2,1)S(1)}, u32[]{:S(2)}, u32[]{:S(2)}) collective-permute-start(bf16[16,1,128]{2,1,0:T(2,128)(2,1)S(1)} %slice_bitcast_fusion.5), channel_id=1, source_target_pairs={{0,1},{1,2},{2,3},{4,5},{5,6},{6,7},{8,9},{9,10},{10,11},{12,13},{... | collective-permute-start | bytes 12296 | tf_op jit(solution)/shard_map/ppermute | solution.py:33
  10.0 10.6 %collective-permute-start = (bf16[1,16,128]{2,1,0:T(8,128)(2,1)S(1)}, bf16[1,16,128]{2,1,0:T(8,128)(2,1)S(1)}, u32[]{:S(2)}, u32[]{:S(2)}) collective-permute-start(bf16[1,16,128]{2,1,0:T(8,128)(2,1)S(1)} %slice_bitcast_fusion.6), channel_id=1, source_target_pairs={{0,4},{4,8},{8,12},{12,16},{16,20},{20,24},{24,28},{1,5},{5,9},{9,... | collective-permute-start | bytes 12296 | tf_op jit(solution)/shard_map/ppermute | solution.py:33
  29.9 10.5 %collective-permute-start.8 = (f32[18,1,128]{2,1,0:T(1,128)S(1)}, f32[18,1,128]{2,1,0:T(1,128)S(1)}, u32[]{:S(2)}, u32[]{:S(2)}) collective-permute-start(f32[18,1,128]{2,1,0:T(1,128)S(1)} %get-tuple-element.78), channel_id=1, source_target_pairs={{1,0},{2,1},{3,2},{5,4},{6,5},{7,6},{9,8},{10,9},{11,10},{13,12},{... | collective-permute-start | bytes 27656 | tf_op jit(solution)/shard_map/ppermute | solution.py:25
  31.2 9.2 %collective-permute-start.9 = (f32[18,1,128]{2,1,0:T(1,128)S(1)}, f32[18,1,128]{2,1,0:T(1,128)S(1)}, u32[]{:S(2)}, u32[]{:S(2)}) collective-permute-start(f32[18,1,128]{2,1,0:T(1,128)S(1)} %get-tuple-element.77), channel_id=1, source_target_pairs={{0,1},{1,2},{2,3},{4,5},{5,6},{6,7},{8,9},{9,10},{10,11},{12,13},{... | collective-permute-start | bytes 27656 | tf_op jit(solution)/shard_map/ppermute | solution.py:22
  34.4 14.2 %collective-permute-start.14 = (f32[1,8,64]{2,1,0:T(8,128)S(1)}, f32[1,8,64]{2,1,0:T(8,128)S(1)}, u32[]{:S(2)}, u32[]{:S(2)}) collective-permute-start(f32[1,8,64]{2,1,0:T(8,128)S(1)} %broadcast.204), channel_id=1, source_target_pairs={{4,0},{8,4},{12,8},{16,12},{20,16},{24,20},{28,24},{5,1},{9,5},{13... | collective-permute-start | bytes 6152 | tf_op jit(solution)/shard_map/ppermute | solution.py:25
  35.7 12.9 %collective-permute-start.15 = (f32[1,8,64]{2,1,0:T(8,128)S(1)}, f32[1,8,64]{2,1,0:T(8,128)S(1)}, u32[]{:S(2)}, u32[]{:S(2)}) collective-permute-start(f32[1,8,64]{2,1,0:T(8,128)S(1)} %broadcast.204), channel_id=1, source_target_pairs={{0,4},{4,8},{8,12},{12,16},{16,20},{20,24},{24,28},{1,5},{5,9},{9,... | collective-permute-start | bytes 6152 | tf_op jit(solution)/shard_map/ppermute | solution.py:22
  41.8 13.3 %collective-permute-start.10 = (f32[1,16,128]{2,1,0:T(8,128)S(1)}, f32[1,16,128]{2,1,0:T(8,128)S(1)}, u32[]{:S(2)}, u32[]{:S(2)}) collective-permute-start(f32[1,16,128]{2,1,0:T(8,128)S(1)} %get-tuple-element.100), channel_id=1, source_target_pairs={{4,0},{8,4},{12,8},{16,12},{20,16},{24,20},{28,24},{5,1},{9,5},{13... | collective-permute-start | bytes 24584 | tf_op jit(solution)/shard_map/ppermute | solution.py:25
  43.1 12.0 %collective-permute-start.11 = (f32[1,16,128]{2,1,0:T(8,128)S(1)}, f32[1,16,128]{2,1,0:T(8,128)S(1)}, u32[]{:S(2)}, u32[]{:S(2)}) collective-permute-start(f32[1,16,128]{2,1,0:T(8,128)S(1)} %get-tuple-element.99), channel_id=1, source_target_pairs={{0,4},{4,8},{8,12},{12,16},{16,20},{20,24},{24,28},{1,5},{5,9},{9,... | collective-permute-start | bytes 24584 | tf_op jit(solution)/shard_map/ppermute | solution.py:22
  48.6 12.1 %collective-permute-start.16 = (f32[10,1,64]{2,1,0:T(1,128)S(1)}, f32[10,1,64]{2,1,0:T(1,128)S(1)}, u32[]{:S(2)}, u32[]{:S(2)}) collective-permute-start(f32[10,1,64]{2,1,0:T(1,128)S(1)} %get-tuple-element.120), channel_id=1, source_target_pairs={{1,0},{2,1},{3,2},{5,4},{6,5},{7,6},{9,8},{10,9},{11,10},{13,12},{... | collective-permute-start | bytes 7688 | tf_op jit(solution)/shard_map/ppermute | solution.py:25
  49.9 10.8 %collective-permute-start.17 = (f32[10,1,64]{2,1,0:T(1,128)S(1)}, f32[10,1,64]{2,1,0:T(1,128)S(1)}, u32[]{:S(2)}, u32[]{:S(2)}) collective-permute-start(f32[10,1,64]{2,1,0:T(1,128)S(1)} %get-tuple-element.119), channel_id=1, source_target_pairs={{0,1},{1,2},{2,3},{4,5},{5,6},{6,7},{8,9},{9,10},{10,11},{12,13},{... | collective-permute-start | bytes 7688 | tf_op jit(solution)/shard_map/ppermute | solution.py:22
  55.1 19.5 %collective-permute-start.12 = (f32[18,1,128]{2,1,0:T(1,128)S(1)}, f32[18,1,128]{2,1,0:T(1,128)S(1)}, u32[]{:S(2)}, u32[]{:S(2)}) collective-permute-start(f32[18,1,128]{2,1,0:T(1,128)S(1)} %get-tuple-element.76), channel_id=1, source_target_pairs={{1,0},{2,1},{3,2},{5,4},{6,5},{7,6},{9,8},{10,9},{11,10},{13,12},{... | collective-permute-start | bytes 27656 | tf_op jit(solution)/shard_map/ppermute | solution.py:25
  56.4 18.2 %collective-permute-start.13 = (f32[18,1,128]{2,1,0:T(1,128)S(1)}, f32[18,1,128]{2,1,0:T(1,128)S(1)}, u32[]{:S(2)}, u32[]{:S(2)}) collective-permute-start(f32[18,1,128]{2,1,0:T(1,128)S(1)} %get-tuple-element.75), channel_id=1, source_target_pairs={{0,1},{1,2},{2,3},{4,5},{5,6},{6,7},{8,9},{9,10},{10,11},{12,13},{... | collective-permute-start | bytes 27656 | tf_op jit(solution)/shard_map/ppermute | solution.py:22
  89.0 6.5 collective-permute-start.18
  90.3 6.5 collective-permute-start.19
  96.8 11.2 %collective-permute-start.20 = (f32[10,1,64]{2,1,0:T(1,128)S(1)}, f32[10,1,64]{2,1,0:T(1,128)S(1)}, u32[]{:S(2)}, u32[]{:S(2)}) collective-permute-start(f32[10,1,64]{2,1,0:T(1,128)S(1)} %get-tuple-element.118), channel_id=1, source_target_pairs={{1,0},{2,1},{3,2},{5,4},{6,5},{7,6},{9,8},{10,9},{11,10},{13,12},{... | collective-permute-start | bytes 7688 | tf_op jit(solution)/shard_map/ppermute | solution.py:25
  98.1 9.9 %collective-permute-start.21 = (f32[10,1,64]{2,1,0:T(1,128)S(1)}, f32[10,1,64]{2,1,0:T(1,128)S(1)}, u32[]{:S(2)}, u32[]{:S(2)}) collective-permute-start(f32[10,1,64]{2,1,0:T(1,128)S(1)} %get-tuple-element.117), channel_id=1, source_target_pairs={{0,1},{1,2},{2,3},{4,5},{5,6},{6,7},{8,9},{9,10},{10,11},{12,13},{... | collective-permute-start | bytes 7688 | tf_op jit(solution)/shard_map/ppermute | solution.py:22
  101.5 13.6 %collective-permute-start.26 = (f32[1,4,32]{2,1,0:T(4,128)S(1)}, f32[1,4,32]{2,1,0:T(4,128)S(1)}, u32[]{:S(2)}, u32[]{:S(2)}) collective-permute-start(f32[1,4,32]{2,1,0:T(4,128)S(1)} %broadcast.211), channel_id=1, source_target_pairs={{4,0},{8,4},{12,8},{16,12},{20,16},{24,20},{28,24},{5,1},{9,5},{13... | collective-permute-start | bytes 1544 | tf_op jit(solution)/shard_map/ppermute | solution.py:25
  102.8 12.4 %collective-permute-start.27 = (f32[1,4,32]{2,1,0:T(4,128)S(1)}, f32[1,4,32]{2,1,0:T(4,128)S(1)}, u32[]{:S(2)}, u32[]{:S(2)}) collective-permute-start(f32[1,4,32]{2,1,0:T(4,128)S(1)} %broadcast.211), channel_id=1, source_target_pairs={{0,4},{4,8},{8,12},{12,16},{16,20},{20,24},{24,28},{1,5},{5,9},{9,... | collective-permute-start | bytes 1544 | tf_op jit(solution)/shard_map/ppermute | solution.py:22
  108.3 11.8 %collective-permute-start.22 = (f32[1,8,64]{2,1,0:T(8,128)S(1)}, f32[1,8,64]{2,1,0:T(8,128)S(1)}, u32[]{:S(2)}, u32[]{:S(2)}) collective-permute-start(f32[1,8,64]{2,1,0:T(8,128)S(1)} %get-tuple-element.135), channel_id=1, source_target_pairs={{4,0},{8,4},{12,8},{16,12},{20,16},{24,20},{28,24},{5,1},{9,5},{13... | collective-permute-start | bytes 6152 | tf_op jit(solution)/shard_map/ppermute | solution.py:25
  109.6 10.5 %collective-permute-start.23 = (f32[1,8,64]{2,1,0:T(8,128)S(1)}, f32[1,8,64]{2,1,0:T(8,128)S(1)}, u32[]{:S(2)}, u32[]{:S(2)}) collective-permute-start(f32[1,8,64]{2,1,0:T(8,128)S(1)} %get-tuple-element.134), channel_id=1, source_target_pairs={{0,4},{4,8},{8,12},{12,16},{16,20},{20,24},{24,28},{1,5},{5,9},{9,... | collective-permute-start | bytes 6152 | tf_op jit(solution)/shard_map/ppermute | solution.py:22
  115.2 10.4 %collective-permute-start.28 = (f32[6,1,32]{2,1,0:T(1,128)S(1)}, f32[6,1,32]{2,1,0:T(1,128)S(1)}, u32[]{:S(2)}, u32[]{:S(2)}) collective-permute-start(f32[6,1,32]{2,1,0:T(1,128)S(1)} %get-tuple-element.155), channel_id=1, source_target_pairs={{1,0},{2,1},{3,2},{5,4},{6,5},{7,6},{9,8},{10,9},{11,10},{13,12},{... | collective-permute-start | bytes 2312 | tf_op jit(solution)/shard_map/ppermute | solution.py:25
  116.5 9.2 %collective-permute-start.29 = (f32[6,1,32]{2,1,0:T(1,128)S(1)}, f32[6,1,32]{2,1,0:T(1,128)S(1)}, u32[]{:S(2)}, u32[]{:S(2)}) collective-permute-start(f32[6,1,32]{2,1,0:T(1,128)S(1)} %get-tuple-element.154), channel_id=1, source_target_pairs={{0,1},{1,2},{2,3},{4,5},{5,6},{6,7},{8,9},{9,10},{10,11},{12,13},{... | collective-permute-start | bytes 2312 | tf_op jit(solution)/shard_map/ppermute | solution.py:22
  120.1 6.9 %collective-permute-start.24 = (f32[10,1,64]{2,1,0:T(1,128)S(1)}, f32[10,1,64]{2,1,0:T(1,128)S(1)}, u32[]{:S(2)}, u32[]{:S(2)}) collective-permute-start(f32[10,1,64]{2,1,0:T(1,128)S(1)} %get-tuple-element.116), channel_id=1, source_target_pairs={{1,0},{2,1},{3,2},{5,4},{6,5},{7,6},{9,8},{10,9},{11,10},{13,12},{... | collective-permute-start | bytes 7688 | tf_op jit(solution)/shard_map/ppermute | solution.py:25
  128.6 6.5 collective-permute-start.30
  129.9 6.5 collective-permute-start.31
  142.1 6.5 collective-permute-start.34
  143.4 6.5 collective-permute-start.35
  149.9 52.6 %collective-permute-start.36 = (f32[6,1,32]{2,1,0:T(1,128)S(1)}, f32[6,1,32]{2,1,0:T(1,128)S(1)}, u32[]{:S(2)}, u32[]{:S(2)}) collective-permute-start(f32[6,1,32]{2,1,0:T(1,128)S(1)} %get-tuple-element.151), channel_id=1, source_target_pairs={{1,0},{2,1},{3,2},{5,4},{6,5},{7,6},{9,8},{10,9},{11,10},{13,12},{... | collective-permute-start | bytes 2312 | tf_op jit(solution)/shard_map/ppermute | solution.py:25
  151.2 51.3 %collective-permute-start.37 = (f32[6,1,32]{2,1,0:T(1,128)S(1)}, f32[6,1,32]{2,1,0:T(1,128)S(1)}, u32[]{:S(2)}, u32[]{:S(2)}) collective-permute-start(f32[6,1,32]{2,1,0:T(1,128)S(1)} %get-tuple-element.150), channel_id=1, source_target_pairs={{0,1},{1,2},{2,3},{4,5},{5,6},{6,7},{8,9},{9,10},{10,11},{12,13},{... | collective-permute-start | bytes 2312 | tf_op jit(solution)/shard_map/ppermute | solution.py:22
  289.1 6.8 %collective-permute-start.46 = (f32[1,8,64]{2,1,0:T(8,128)S(1)}, f32[1,8,64]{2,1,0:T(8,128)S(1)}, u32[]{:S(2)}, u32[]{:S(2)}) collective-permute-start(f32[1,8,64]{2,1,0:T(8,128)S(1)} %get-tuple-element.132), channel_id=1, source_target_pairs={{4,0},{8,4},{12,8},{16,12},{20,16},{24,20},{28,24},{5,1},{9,5},{13... | collective-permute-start | bytes 6152 | tf_op jit(solution)/shard_map/ppermute | solution.py:25
  290.4 6.8 %collective-permute-start.47 = (f32[1,8,64]{2,1,0:T(8,128)S(1)}, f32[1,8,64]{2,1,0:T(8,128)S(1)}, u32[]{:S(2)}, u32[]{:S(2)}) collective-permute-start(f32[1,8,64]{2,1,0:T(8,128)S(1)} %get-tuple-element.131), channel_id=1, source_target_pairs={{0,4},{4,8},{8,12},{12,16},{16,20},{20,24},{24,28},{1,5},{5,9},{9,... | collective-permute-start | bytes 6152 | tf_op jit(solution)/shard_map/ppermute | solution.py:22
  304.2 7.0 %collective-permute-start.50 = (f32[1,8,64]{2,1,0:T(8,128)S(1)}, f32[1,8,64]{2,1,0:T(8,128)S(1)}, u32[]{:S(2)}, u32[]{:S(2)}) collective-permute-start(f32[1,8,64]{2,1,0:T(8,128)S(1)} %get-tuple-element.130), channel_id=1, source_target_pairs={{4,0},{8,4},{12,8},{16,12},{20,16},{24,20},{28,24},{5,1},{9,5},{13... | collective-permute-start | bytes 6152 | tf_op jit(solution)/shard_map/ppermute | solution.py:25
  305.5 7.0 %collective-permute-start.51 = (f32[1,8,64]{2,1,0:T(8,128)S(1)}, f32[1,8,64]{2,1,0:T(8,128)S(1)}, u32[]{:S(2)}, u32[]{:S(2)}) collective-permute-start(f32[1,8,64]{2,1,0:T(8,128)S(1)} %get-tuple-element.129), channel_id=1, source_target_pairs={{0,4},{4,8},{8,12},{12,16},{16,20},{20,24},{24,28},{1,5},{5,9},{9,... | collective-permute-start | bytes 6152 | tf_op jit(solution)/shard_map/ppermute | solution.py:22
  330.5 7.0 %collective-permute-start.54 = (f32[1,16,128]{2,1,0:T(8,128)S(1)}, f32[1,16,128]{2,1,0:T(8,128)S(1)}, u32[]{:S(2)}, u32[]{:S(2)}) collective-permute-start(f32[1,16,128]{2,1,0:T(8,128)S(1)} %get-tuple-element.96), channel_id=1, source_target_pairs={{4,0},{8,4},{12,8},{16,12},{20,16},{24,20},{28,24},{5,1},{9,5},{13... | collective-permute-start | bytes 24584 | tf_op jit(solution)/shard_map/ppermute | solution.py:25
  331.8 7.1 %collective-permute-start.55 = (f32[1,16,128]{2,1,0:T(8,128)S(1)}, f32[1,16,128]{2,1,0:T(8,128)S(1)}, u32[]{:S(2)}, u32[]{:S(2)}) collective-permute-start(f32[1,16,128]{2,1,0:T(8,128)S(1)} %get-tuple-element.95), channel_id=1, source_target_pairs={{0,4},{4,8},{8,12},{12,16},{16,20},{20,24},{24,28},{1,5},{5,9},{9,... | collective-permute-start | bytes 24584 | tf_op jit(solution)/shard_map/ppermute | solution.py:22
  346.2 7.0 %collective-permute-start.58 = (f32[1,16,128]{2,1,0:T(8,128)S(1)}, f32[1,16,128]{2,1,0:T(8,128)S(1)}, u32[]{:S(2)}, u32[]{:S(2)}) collective-permute-start(f32[1,16,128]{2,1,0:T(8,128)S(1)} %get-tuple-element.94), channel_id=1, source_target_pairs={{4,0},{8,4},{12,8},{16,12},{20,16},{24,20},{28,24},{5,1},{9,5},{13... | collective-permute-start | bytes 24584 | tf_op jit(solution)/shard_map/ppermute | solution.py:25
  347.5 7.1 %collective-permute-start.59 = (f32[1,16,128]{2,1,0:T(8,128)S(1)}, f32[1,16,128]{2,1,0:T(8,128)S(1)}, u32[]{:S(2)}, u32[]{:S(2)}) collective-permute-start(f32[1,16,128]{2,1,0:T(8,128)S(1)} %get-tuple-element.93), channel_id=1, source_target_pairs={{0,4},{4,8},{8,12},{12,16},{16,20},{20,24},{24,28},{1,5},{5,9},{9,... | collective-permute-start | bytes 24584 | tf_op jit(solution)/shard_map/ppermute | solution.py:22
  361.9 7.0 %collective-permute-start.62 = (f32[1,16,128]{2,1,0:T(8,128)S(1)}, f32[1,16,128]{2,1,0:T(8,128)S(1)}, u32[]{:S(2)}, u32[]{:S(2)}) collective-permute-start(f32[1,16,128]{2,1,0:T(8,128)S(1)} %get-tuple-element.92), channel_id=1, source_target_pairs={{4,0},{8,4},{12,8},{16,12},{20,16},{24,20},{28,24},{5,1},{9,5},{13... | collective-permute-start | bytes 24584 | tf_op jit(solution)/shard_map/ppermute | solution.py:25
  363.2 7.1 %collective-permute-start.63 = (f32[1,16,128]{2,1,0:T(8,128)S(1)}, f32[1,16,128]{2,1,0:T(8,128)S(1)}, u32[]{:S(2)}, u32[]{:S(2)}) collective-permute-start(f32[1,16,128]{2,1,0:T(8,128)S(1)} %get-tuple-element.91), channel_id=1, source_target_pairs={{0,4},{4,8},{8,12},{12,16},{16,20},{20,24},{24,28},{1,5},{5,9},{9,... | collective-permute-start | bytes 24584 | tf_op jit(solution)/shard_map/ppermute | solution.py:22
  377.6 7.0 %collective-permute-start.66 = (f32[1,16,128]{2,1,0:T(8,128)S(1)}, f32[1,16,128]{2,1,0:T(8,128)S(1)}, u32[]{:S(2)}, u32[]{:S(2)}) collective-permute-start(f32[1,16,128]{2,1,0:T(8,128)S(1)} %get-tuple-element.90), channel_id=1, source_target_pairs={{4,0},{8,4},{12,8},{16,12},{20,16},{24,20},{28,24},{5,1},{9,5},{13... | collective-permute-start | bytes 24584 | tf_op jit(solution)/shard_map/ppermute | solution.py:25
  378.9 7.1 %collective-permute-start.67 = (f32[1,16,128]{2,1,0:T(8,128)S(1)}, f32[1,16,128]{2,1,0:T(8,128)S(1)}, u32[]{:S(2)}, u32[]{:S(2)}) collective-permute-start(f32[1,16,128]{2,1,0:T(8,128)S(1)} %get-tuple-element.89), channel_id=1, source_target_pairs={{0,4},{4,8},{8,12},{12,16},{16,20},{20,24},{24,28},{1,5},{5,9},{9,... | collective-permute-start | bytes 24584 | tf_op jit(solution)/shard_map/ppermute | solution.py:22
  393.4 7.0 %collective-permute-start.70 = (f32[1,16,128]{2,1,0:T(8,128)S(1)}, f32[1,16,128]{2,1,0:T(8,128)S(1)}, u32[]{:S(2)}, u32[]{:S(2)}) collective-permute-start(f32[1,16,128]{2,1,0:T(8,128)S(1)} %get-tuple-element.88), channel_id=1, source_target_pairs={{4,0},{8,4},{12,8},{16,12},{20,16},{24,20},{28,24},{5,1},{9,5},{13... | collective-permute-start | bytes 24584 | tf_op jit(solution)/shard_map/ppermute | solution.py:25
  394.7 7.1 %collective-permute-start.71 = (f32[1,16,128]{2,1,0:T(8,128)S(1)}, f32[1,16,128]{2,1,0:T(8,128)S(1)}, u32[]{:S(2)}, u32[]{:S(2)}) collective-permute-start(f32[1,16,128]{2,1,0:T(8,128)S(1)} %get-tuple-element.87), channel_id=1, source_target_pairs={{0,4},{4,8},{8,12},{12,16},{16,20},{20,24},{24,28},{1,5},{5,9},{9,... | collective-permute-start | bytes 24584 | tf_op jit(solution)/shard_map/ppermute | solution.py:22
  422.9 7.0 %collective-permute-start.74 = (f32[1,8,64]{2,1,0:T(8,128)S(1)}, f32[1,8,64]{2,1,0:T(8,128)S(1)}, u32[]{:S(2)}, u32[]{:S(2)}) collective-permute-start(f32[1,8,64]{2,1,0:T(8,128)S(1)} %get-tuple-element.128), channel_id=1, source_target_pairs={{4,0},{8,4},{12,8},{16,12},{20,16},{24,20},{28,24},{5,1},{9,5},{13... | collective-permute-start | bytes 6152 | tf_op jit(solution)/shard_map/ppermute | solution.py:25
  424.2 7.0 %collective-permute-start.75 = (f32[1,8,64]{2,1,0:T(8,128)S(1)}, f32[1,8,64]{2,1,0:T(8,128)S(1)}, u32[]{:S(2)}, u32[]{:S(2)}) collective-permute-start(f32[1,8,64]{2,1,0:T(8,128)S(1)} %get-tuple-element.127), channel_id=1, source_target_pairs={{0,4},{4,8},{8,12},{12,16},{16,20},{20,24},{24,28},{1,5},{5,9},{9,... | collective-permute-start | bytes 6152 | tf_op jit(solution)/shard_map/ppermute | solution.py:22
  438.4 7.0 %collective-permute-start.78 = (f32[1,8,64]{2,1,0:T(8,128)S(1)}, f32[1,8,64]{2,1,0:T(8,128)S(1)}, u32[]{:S(2)}, u32[]{:S(2)}) collective-permute-start(f32[1,8,64]{2,1,0:T(8,128)S(1)} %get-tuple-element.126), channel_id=1, source_target_pairs={{4,0},{8,4},{12,8},{16,12},{20,16},{24,20},{28,24},{5,1},{9,5},{13... | collective-permute-start | bytes 6152 | tf_op jit(solution)/shard_map/ppermute | solution.py:25
  439.7 7.0 %collective-permute-start.79 = (f32[1,8,64]{2,1,0:T(8,128)S(1)}, f32[1,8,64]{2,1,0:T(8,128)S(1)}, u32[]{:S(2)}, u32[]{:S(2)}) collective-permute-start(f32[1,8,64]{2,1,0:T(8,128)S(1)} %get-tuple-element.125), channel_id=1, source_target_pairs={{0,4},{4,8},{8,12},{12,16},{16,20},{20,24},{24,28},{1,5},{5,9},{9,... | collective-permute-start | bytes 6152 | tf_op jit(solution)/shard_map/ppermute | solution.py:22
  455.1 7.0 %collective-permute-start.82 = (f32[1,4,32]{2,1,0:T(4,128)S(1)}, f32[1,4,32]{2,1,0:T(4,128)S(1)}, u32[]{:S(2)}, u32[]{:S(2)}) collective-permute-start(f32[1,4,32]{2,1,0:T(4,128)S(1)} %get-tuple-element.163), channel_id=1, source_target_pairs={{4,0},{8,4},{12,8},{16,12},{20,16},{24,20},{28,24},{5,1},{9,5},{13... | collective-permute-start | bytes 1544 | tf_op jit(solution)/shard_map/ppermute | solution.py:25
  456.4 7.0 %collective-permute-start.83 = (f32[1,4,32]{2,1,0:T(4,128)S(1)}, f32[1,4,32]{2,1,0:T(4,128)S(1)}, u32[]{:S(2)}, u32[]{:S(2)}) collective-permute-start(f32[1,4,32]{2,1,0:T(4,128)S(1)} %get-tuple-element.162), channel_id=1, source_target_pairs={{0,4},{4,8},{8,12},{12,16},{16,20},{20,24},{24,28},{1,5},{5,9},{9,... | collective-permute-start | bytes 1544 | tf_op jit(solution)/shard_map/ppermute | solution.py:22
  470.4 7.0 %collective-permute-start.86 = (f32[1,4,32]{2,1,0:T(4,128)S(1)}, f32[1,4,32]{2,1,0:T(4,128)S(1)}, u32[]{:S(2)}, u32[]{:S(2)}) collective-permute-start(f32[1,4,32]{2,1,0:T(4,128)S(1)} %get-tuple-element.161), channel_id=1, source_target_pairs={{4,0},{8,4},{12,8},{16,12},{20,16},{24,20},{28,24},{5,1},{9,5},{13... | collective-permute-start | bytes 1544 | tf_op jit(solution)/shard_map/ppermute | solution.py:25
  471.7 7.0 %collective-permute-start.87 = (f32[1,4,32]{2,1,0:T(4,128)S(1)}, f32[1,4,32]{2,1,0:T(4,128)S(1)}, u32[]{:S(2)}, u32[]{:S(2)}) collective-permute-start(f32[1,4,32]{2,1,0:T(4,128)S(1)} %get-tuple-element.160), channel_id=1, source_target_pairs={{0,4},{4,8},{8,12},{12,16},{16,20},{20,24},{24,28},{1,5},{5,9},{9,... | collective-permute-start | bytes 1544 | tf_op jit(solution)/shard_map/ppermute | solution.py:22
  572.4 6.1 collective-permute-start.94
  586.0 6.8 %collective-permute-start.98 = (f32[1,8,64]{2,1,0:T(8,128)S(1)}, f32[1,8,64]{2,1,0:T(8,128)S(1)}, u32[]{:S(2)}, u32[]{:S(2)}) collective-permute-start(f32[1,8,64]{2,1,0:T(8,128)S(1)} %get-tuple-element.124), channel_id=1, source_target_pairs={{4,0},{8,4},{12,8},{16,12},{20,16},{24,20},{28,24},{5,1},{9,5},{13... | collective-permute-start | bytes 6152 | tf_op jit(solution)/shard_map/ppermute | solution.py:25
  587.3 6.8 %collective-permute-start.99 = (f32[1,8,64]{2,1,0:T(8,128)S(1)}, f32[1,8,64]{2,1,0:T(8,128)S(1)}, u32[]{:S(2)}, u32[]{:S(2)}) collective-permute-start(f32[1,8,64]{2,1,0:T(8,128)S(1)} %get-tuple-element.123), channel_id=1, source_target_pairs={{0,4},{4,8},{8,12},{12,16},{16,20},{20,24},{24,28},{1,5},{5,9},{9,... | collective-permute-start | bytes 6152 | tf_op jit(solution)/shard_map/ppermute | solution.py:22
  599.9 7.0 %collective-permute-start.102 = (f32[1,8,64]{2,1,0:T(8,128)S(1)}, f32[1,8,64]{2,1,0:T(8,128)S(1)}, u32[]{:S(2)}, u32[]{:S(2)}) collective-permute-start(f32[1,8,64]{2,1,0:T(8,128)S(1)} %get-tuple-element.122), channel_id=1, source_target_pairs={{4,0},{8,4},{12,8},{16,12},{20,16},{24,20},{28,24},{5,1},{9,5},{13... | collective-permute-start | bytes 6152 | tf_op jit(solution)/shard_map/ppermute | solution.py:25
  601.2 7.0 %collective-permute-start.103 = (f32[1,8,64]{2,1,0:T(8,128)S(1)}, f32[1,8,64]{2,1,0:T(8,128)S(1)}, u32[]{:S(2)}, u32[]{:S(2)}) collective-permute-start(f32[1,8,64]{2,1,0:T(8,128)S(1)} %get-tuple-element.121), channel_id=1, source_target_pairs={{0,4},{4,8},{8,12},{12,16},{16,20},{20,24},{24,28},{1,5},{5,9},{9,... | collective-permute-start | bytes 6152 | tf_op jit(solution)/shard_map/ppermute | solution.py:22
  626.2 7.0 %collective-permute-start.106 = (f32[1,16,128]{2,1,0:T(8,128)S(1)}, f32[1,16,128]{2,1,0:T(8,128)S(1)}, u32[]{:S(2)}, u32[]{:S(2)}) collective-permute-start(f32[1,16,128]{2,1,0:T(8,128)S(1)} %get-tuple-element.86), channel_id=1, source_target_pairs={{4,0},{8,4},{12,8},{16,12},{20,16},{24,20},{28,24},{5,1},{9,5},{13... | collective-permute-start | bytes 24584 | tf_op jit(solution)/shard_map/ppermute | solution.py:25
  627.5 7.1 %collective-permute-start.107 = (f32[1,16,128]{2,1,0:T(8,128)S(1)}, f32[1,16,128]{2,1,0:T(8,128)S(1)}, u32[]{:S(2)}, u32[]{:S(2)}) collective-permute-start(f32[1,16,128]{2,1,0:T(8,128)S(1)} %get-tuple-element.85), channel_id=1, source_target_pairs={{0,4},{4,8},{8,12},{12,16},{16,20},{20,24},{24,28},{1,5},{5,9},{9,... | collective-permute-start | bytes 24584 | tf_op jit(solution)/shard_map/ppermute | solution.py:22
  641.9 7.0 %collective-permute-start.110 = (f32[1,16,128]{2,1,0:T(8,128)S(1)}, f32[1,16,128]{2,1,0:T(8,128)S(1)}, u32[]{:S(2)}, u32[]{:S(2)}) collective-permute-start(f32[1,16,128]{2,1,0:T(8,128)S(1)} %get-tuple-element.84), channel_id=1, source_target_pairs={{4,0},{8,4},{12,8},{16,12},{20,16},{24,20},{28,24},{5,1},{9,5},{13... | collective-permute-start | bytes 24584 | tf_op jit(solution)/shard_map/ppermute | solution.py:25
  643.2 7.1 %collective-permute-start.111 = (f32[1,16,128]{2,1,0:T(8,128)S(1)}, f32[1,16,128]{2,1,0:T(8,128)S(1)}, u32[]{:S(2)}, u32[]{:S(2)}) collective-permute-start(f32[1,16,128]{2,1,0:T(8,128)S(1)} %get-tuple-element.83), channel_id=1, source_target_pairs={{0,4},{4,8},{8,12},{12,16},{16,20},{20,24},{24,28},{1,5},{5,9},{9,... | collective-permute-start | bytes 24584 | tf_op jit(solution)/shard_map/ppermute | solution.py:22
  657.6 7.0 %collective-permute-start.114 = (f32[1,16,128]{2,1,0:T(8,128)S(1)}, f32[1,16,128]{2,1,0:T(8,128)S(1)}, u32[]{:S(2)}, u32[]{:S(2)}) collective-permute-start(f32[1,16,128]{2,1,0:T(8,128)S(1)} %get-tuple-element.82), channel_id=1, source_target_pairs={{4,0},{8,4},{12,8},{16,12},{20,16},{24,20},{28,24},{5,1},{9,5},{13... | collective-permute-start | bytes 24584 | tf_op jit(solution)/shard_map/ppermute | solution.py:25
  658.9 7.1 %collective-permute-start.115 = (f32[1,16,128]{2,1,0:T(8,128)S(1)}, f32[1,16,128]{2,1,0:T(8,128)S(1)}, u32[]{:S(2)}, u32[]{:S(2)}) collective-permute-start(f32[1,16,128]{2,1,0:T(8,128)S(1)} %get-tuple-element.81), channel_id=1, source_target_pairs={{0,4},{4,8},{8,12},{12,16},{16,20},{20,24},{24,28},{1,5},{5,9},{9,... | collective-permute-start | bytes 24584 | tf_op jit(solution)/shard_map/ppermute | solution.py:22
  (56 other events, 326.6 us)
where the time goes:
time: 686 us; the launch traced here: 674 us
  starting transfers between devices  360 us (52%)
  blocking collectives  134 us (20%)
  local copies, waits for them, and re-layouts  56.9 us (8%)
  waiting for transfers between devices  48.8 us (7%)
  other arithmetic  40.9 us (6%)
  between operations  32.5 us (5%)
    ppermute x58, starting transfers between devices, padded_2(): lax.ppermute(lax.slice_in_dim(block, block.shape[dim] - width, None, axis...  279 us
    all_gather x2, blocking collectives, vcycle(): lax.all_gather(coarse_target, ('gx', 'gy'), axis=0, tiled=True)  87.6 us
    ppermute x58, starting transfers between devices, padded_2(): lax.ppermute(lax.slice_in_dim(block, 0, width, axis=dim), axis, backward)  75.1 us
    ppermute x58, waiting for transfers between devices, padded_2(): lax.ppermute(lax.slice_in_dim(block, block.shape[dim] - width, None, axis...  48.7 us
    all_gather x1, blocking collectives, per_device(): lax.all_gather(screens[LEVELS], ('gx', 'gy'), axis=0, tiled=True)  46.9 us
    reshape x7, local copies, waits for them, and re-layouts, restrict(): blocks = field.reshape(size_x // 2, 2, size_y // 2, 2, size_z // 2, 2)  31.7 us
    reshape x6, local copies, waits for them, and re-layouts, prolong(): return spread_out.reshape(2 * size_x, 2 * size_y, 2 * size_z)  15.3 us
  transfers between devices with their start and end apart: 118, of which 46 were waited for; matrix products, arithmetic and copies ran while one was open for 3% of the time, Pallas kernels for 0%

commit v1 on v0

v1 whole, which is shorter than its diff:
```python
import numpy as np
import jax
import jax.numpy as jnp
from jax import lax
from jax.experimental import pallas as pl
from jax.experimental.pallas import tpu as pltpu
from jax.sharding import Mesh, PartitionSpec as P

F32 = jnp.float32
BF16 = jnp.bfloat16
LANES = 128
HALO = 8
COARSE_ITERS = 6

screen_weight = 0.25
flux_scale = 0.125
low_edge = 0.3
high_edge = 2.0
centre = 0.5 * (high_edge + low_edge)
radius = 0.5 * (high_edge - low_edge)
ratio = centre / radius
mom_first = 1.0 / ratio
mom_second = 1.0 / (2.0 * ratio - mom_first)
keep = mom_second * mom_first
gain = 2.0 * mom_second / radius

VMEM = pl.BlockSpec(memory_space=pltpu.VMEM)
SMEM = pl.BlockSpec(memory_space=pltpu.SMEM)


def transfer_matrix(level):
    pack, size_z = 1 << level, LANES >> level
    planes = 2 if level == 0 else 4
    out = np.zeros((planes * LANES, LANES), np.float32)
    for j in range(planes):
        for q in range(pack):
            coarse = j if level == 0 else (j * pack + q) // 2
            for z in range(size_z):
                out[j * LANES + q * size_z + z, coarse * (size_z // 2) + z // 2] = 1.0
    return jnp.asarray(out, BF16)


def two_parts(value):
    high = value.astype(BF16)
    return high, (value - high.astype(F32)).astype(BF16)


def gather_lanes(value, matrix):
    high, low = two_parts(value)
    return jnp.dot(high, matrix, preferred_element_type=F32) + jnp.dot(low, matrix, preferred_element_type=F32)


def spread_lanes(value, matrix):
    dims = (((1,), (1,)), ((), ()))
    high, low = two_parts(value)
    return lax.dot_general(high, matrix, dims, preferred_element_type=F32) + lax.dot_general(
        low, matrix, dims, preferred_element_type=F32
    )


def lane_index(rows):
    return lax.broadcasted_iota(jnp.int32, (rows, LANES), 1)


def z_sum(value, size_z):
    lane = lane_index(value.shape[0]) & (size_z - 1)
    return jnp.where(lane != 0, pltpu.roll(value, 1, 1), 0.0) + jnp.where(
        lane != size_z - 1, pltpu.roll(value, LANES - 1, 1), 0.0
    )


def x_sum(before, here, after, size_z):
    if size_z == LANES:
        return before + after
    lane = lane_index(here.shape[0])
    if 2 * size_z == LANES:
        return pltpu.roll(here + jnp.where(lane < size_z, after, before), size_z, 1)
    up = pltpu.roll(jnp.where(lane < size_z, after, here), LANES - size_z, 1)
    down = pltpu.roll(jnp.where(lane >= LANES - size_z, before, here), size_z, 1)
    return up + down


def neighbours(ref, base, rows, stride, size_z):
    here = ref[pl.ds(base, rows), :]
    total = x_sum(ref[pl.ds(base - stride, rows), :], here, ref[pl.ds(base + stride, rows), :], size_z)
    total = total + (ref[pl.ds(base - 1, rows), :] + ref[pl.ds(base + 1, rows), :])
    return here, total + z_sum(here, size_z)


def for_planes(count, body, limit=64):
    if count <= limit:
        for i in range(count):
            body(i)
    else:
        step = 8

        def block(k, carry):
            for j in range(step):
                body(k * step + j)
            return carry

        lax.fori_loop(0, count // step, block, 0)


def pair_rows(ref, start, rows):
    return ref[pl.ds(start, rows // 2, stride=2), :] + ref[pl.ds(start + 1, rows // 2, stride=2), :]


def cells_kernel(place, faces, points, first, second, part, count, edge):
    size_x, size_y = points.shape[:2]
    lane = lane_index(size_y)
    row = lax.broadcasted_iota(jnp.int32, (size_y, LANES), 0)
    last_x = None
    for i in range(size_x):
        along_x = faces[0, i]
        along_y = faces[1, i]
        along_z = faces[2, i]
        total = jnp.where(row != 0, pltpu.roll(along_y, 1, 0), 0) - along_y
        total = total + (jnp.where(lane != 0, pltpu.roll(along_z, 1, 1), 0) - along_z) - along_x
        if last_x is not None:
            total = total + last_x
        last_x = along_x
        part[i] = total.astype(F32).astype(BF16)
        count[i] = (points[i] + 1).astype(F32).astype(BF16)
    edge[0] = last_x.astype(F32).astype(BF16)
    edge[1] = faces[1, :, size_y - 1, :].astype(F32).astype(BF16)

    def write(up, down):
        for target, start in ((up, size_x - HALO), (down, 0)):
            target[0:HALO] = part[start : start + HALO]
            target[HALO : 2 * HALO] = count[start : start + HALO]
            target[2 * HALO : 2 * HALO + 2] = edge[...]

    odd = place[0] % 2

    @pl.when(odd == 0)
    def _():
        write(first, second)

    @pl.when(odd == 1)
    def _():
        write(second, first)


def wide_kernel(place, got_first, got_second, part, count, edge, first, second, part_x, count_x, edge_x):
    size_x, size_y = part.shape[:2]
    wide = size_x + 2 * HALO

    def fill(below, above):
        part_x[0:HALO] = below[0:HALO]
        part_x[HALO + size_x :] = above[0:HALO]
        count_x[0:HALO] = below[HALO : 2 * HALO]
        count_x[HALO + size_x :] = above[HALO : 2 * HALO]
        part_x[HALO : HALO + size_x] = part[...]
        count_x[HALO : HALO + size_x] = count[...]
        part_x[HALO] = (part[0].astype(F32) + below[2 * HALO].astype(F32)).astype(BF16)
        part_x[HALO + size_x] = (above[0].astype(F32) + edge[0].astype(F32)).astype(BF16)
        edge_x[0:HALO] = below[2 * HALO + 1].astype(F32)[size_x - HALO :]
        edge_x[HALO : HALO + size_x] = edge[1].astype(F32)
        edge_x[HALO + size_x :] = above[2 * HALO + 1].astype(F32)[:HALO]

    odd = place[0] % 2

    @pl.when(odd == 0)
    def _():
        fill(got_second, got_first)

    @pl.when(odd == 1)
    def _():
        fill(got_first, got_second)

    def write(up, down):
        for i in range(wide):
            cells = part_x[i].astype(F32)
            points = count_x[i].astype(F32)
            up[i] = jnp.concatenate([cells[size_y - HALO :], points[size_y - HALO :]], 0).astype(BF16)
            down[i] = jnp.concatenate([cells[:HALO], points[:HALO]], 0).astype(BF16)
        for target in (up, down):
            for j in range(wide // size_y):
                target[wide + j] = edge_x[j * size_y : (j + 1) * size_y].astype(BF16)

    odd_y = place[1] % 2

    @pl.when(odd_y == 0)
    def _():
        write(first, second)

    @pl.when(odd_y == 1)
    def _():
        write(second, first)


def finest_step_one(source, target, field, scaled, start, end, plane):
    for i in range(start, end, 2):
        base = 8 + i * plane
        rows = 2 * plane
        here, total = neighbours(source, base, rows, plane, LANES)
        fit = (field[pl.ds(base, rows), :] + total) * scaled[pl.ds(base, rows), :]
        target[pl.ds(base, rows), :] = here + (fit - here) * (1.0 / centre)


def finest_step_two(source, old, field, scaled, start, end, plane):
    for i in range(start, end, 2):
        base = 8 + i * plane
        rows = 2 * plane
        here, total = neighbours(source, base, rows, plane, LANES)
        fit = (field[pl.ds(base, rows), :] + total) * scaled[pl.ds(base, rows), :]
        before = old[pl.ds(base, rows), :]
        old[pl.ds(base, rows), :] = here + (keep * (here - before) + gain * (fit - here))


def finest_residual(iterate, field, count, size_x, size_y, write):
    plane = size_y + 2 * HALO
    for i in range(size_x):
        base = 8 + (HALO + i) * plane + HALO
        here, total = neighbours(iterate, base, size_y, plane, LANES)
        diag = 6.0 + screen_weight * (count[HALO + i].astype(F32) - 1.0)
        write(i, here, field[pl.ds(base, size_y), :] + total - diag * here)


def restrict_finest(rows_ref, size_x, size_y, matrix):
    half = pair_rows(rows_ref, 0, size_x * size_y).reshape(size_x // 4, 4, size_y // 2, LANES)
    even = (half[:, 0] + half[:, 1]).reshape(-1, LANES)
    odd = (half[:, 2] + half[:, 3]).reshape(-1, LANES)
    return even, odd


def start_kernel(
    place, got_first, got_second, part_x, count_x, edge_x, matrix, iterate, field, inverse, packet, rows_ref, low, high
):
    wide, size_y = part_x.shape[:2]
    size_x = wide - 2 * HALO
    plane = size_y + 2 * HALO
    odd_y = place[1] % 2

    @pl.when(odd_y == 0)
    def _():
        low[...] = got_second[...]
        high[...] = got_first[...]

    @pl.when(odd_y == 1)
    def _():
        low[...] = got_first[...]
        high[...] = got_second[...]

    top = lax.broadcasted_iota(jnp.int32, (HALO, LANES), 0) == 0
    zero = jnp.zeros((8, LANES), F32)
    for ref in (iterate, field, inverse):
        ref[0:8] = zero
        ref[8 + wide * plane :] = zero
    low_edge_rows = [low[wide + j].astype(F32) for j in range(wide // size_y)]
    for i in range(wide):
        below = low[i].astype(F32)
        above = high[i].astype(F32)
        own = part_x[i].astype(F32)
        under = low_edge_rows[i // size_y][i % size_y : i % size_y + 1]
        over = edge_x[i : i + 1]
        cells = jnp.concatenate(
            [
                below[:HALO],
                own[:HALO] + jnp.where(top, under, 0.0),
                own[HALO:],
                above[:HALO] + jnp.where(top, over, 0.0),
            ],
            0,
        )
        points = jnp.concatenate([below[HALO:], count_x[i].astype(F32), above[HALO:]], 0)
        given = flux_scale * cells
        inv = jnp.where(points > 0.0, 1.0 / (6.0 - screen_weight + screen_weight * points), 0.0)
        base = 8 + i * plane
        field[pl.ds(base, plane), :] = given
        inverse[pl.ds(base, plane), :] = inv
        iterate[pl.ds(base, plane), :] = (given * inv) * (1.0 / centre)

    scratch = rows_ref
    for i in range(1, wide - 1, 2):
        base = 8 + i * plane
        rows = 2 * plane
        here, total = neighbours(iterate, base, rows, plane, LANES)
        fit = (field[pl.ds(base, rows), :] + total) * inverse[pl.ds(base, rows), :]
        scratch[pl.ds(base, rows), :] = here + (keep * here + gain * (fit - here))
    for i in range(1, wide - 1, 2):
        base = 8 + i * plane
        iterate[pl.ds(base, 2 * plane), :] = scratch[pl.ds(base, 2 * plane), :]

    def write(i, here, value):
        scratch[pl.ds(i * size_y, size_y), :] = value

    finest_residual(iterate, field, count_x, size_x, size_y, write)
    even, odd = restrict_finest(scratch, size_x, size_y, matrix)
    coarse = 0.125 * gather_lanes(jnp.concatenate([even, odd], 1), matrix[...])
    for i in range(size_x):
        scratch[pl.ds(i * size_y, size_y), :] = count_x[HALO + i].astype(F32) - 1.0
    even, odd = restrict_finest(scratch, size_x, size_y, matrix)
    points = jnp.dot(jnp.concatenate([even, odd], 1).astype(BF16), matrix[...], preferred_element_type=F32)
    send_coarse(packet, coarse, points, size_y // 2)


def send_coarse(packet, coarse, points, size_y):
    copies = packet.shape[0]
    planes = coarse.shape[0] // size_y
    high = coarse.astype(BF16).astype(F32)
    low = coarse - high
    for i in range(planes):
        at = slice(i * size_y, (i + 1) * size_y)
        tile = jnp.concatenate([high[at], low[at]], 0).astype(BF16)
        for k in range(copies):
            packet[k, i] = tile
    if points is not None:
        for i in range(planes // 2):
            tile = points[2 * i * size_y : 2 * (i + 1) * size_y].astype(BF16)
            for k in range(copies):
                packet[k, planes + i] = tile


def packed_apply(value, screen, factor, size_z):
    planes, size_y, _ = value.shape
    flat = value.reshape(planes * size_y, LANES)
    empty = jnp.zeros((1, size_y, LANES), F32)
    if planes > 1:
        before = jnp.concatenate([empty, value[:-1]], 0).reshape(flat.shape)
        after = jnp.concatenate([value[1:], empty], 0).reshape(flat.shape)
    else:
        before = after = jnp.zeros_like(flat)
    row = lax.broadcasted_iota(jnp.int32, value.shape, 1)
    along_y = jnp.where(row != 0, pltpu.roll(value, 1, 1), 0.0) + jnp.where(
        row != size_y - 1, pltpu.roll(value, size_y - 1, 1), 0.0
    )
    total = x_sum(before, flat, after, size_z) + z_sum(flat, size_z)
    return (6.0 * value - (total.reshape(value.shape) + along_y)) * factor + screen * value


def total_of(value):
    return jnp.sum(jnp.sum(value, 0), keepdims=True)[None]


def conjugate_gradients(target, screen, factor, size_z):
    iterate = jnp.zeros_like(target)
    remain = target
    search = target
    norm_now = total_of(remain * remain)
    for step in range(COARSE_ITERS):
        image = packed_apply(search, screen, factor, size_z)
        length = norm_now / total_of(search * image)
        iterate = iterate + length * search
        if step + 1 < COARSE_ITERS:
            remain = remain - length * image
            norm_next = total_of(remain * remain)
            search = remain + (norm_next / norm_now) * search
            norm_now = norm_next
    return iterate


def smooth_packed(iterate, target, screen, inv, factor, size_z):
    step = (target - packed_apply(iterate, screen, factor, size_z)) * inv * (1.0 / centre)
    iterate = iterate + step
    again = (target - packed_apply(iterate, screen, factor, size_z)) * inv
    return iterate + (keep * step + gain * again)


def smooth_packed_zero(target, screen, inv, factor, size_z):
    step = target * inv * (1.0 / centre)
    again = (target - packed_apply(step, screen, factor, size_z)) * inv
    return step + (keep * step + gain * again)


def add_lanes(rows_ref, planes, size_y, matrix):
    half = pair_rows(rows_ref, 0, planes * size_y).reshape(planes // 4, 4, size_y // 2, LANES)
    wide = jnp.concatenate([half[:, j].reshape(-1, LANES) for j in range(4)], 1)
    return gather_lanes(wide, matrix[...]).reshape(planes // 4, size_y // 2, LANES)


def copy_level(value, matrix):
    planes, size_y, _ = value.shape
    wide = spread_lanes(value.reshape(-1, LANES), matrix[...]).reshape(planes, size_y, 4 * LANES)
    return jnp.stack([wide[:, :, j * LANES : (j + 1) * LANES] for j in range(4)], 1).reshape(
        4 * planes, size_y, LANES
    )


class Sizes:
    def __init__(self, mesh_x, mesh_y, size_x, size_y):
        self.mesh_x, self.mesh_y = mesh_x, mesh_y
        self.own_x, self.own_y = size_x // 4, size_y // 2
        self.planes, self.rows = mesh_x * self.own_x, mesh_y * self.own_y
        self.stride = self.rows + 8
        self.flat = (self.planes + 8) * self.stride + 8
        self.pad_x = 4


def level_one(place, gathered, sizes, mats, refs, first):
    mat_1, mat_2 = mats
    given, inverse, diag, step, iterate, rows_ref, level_two, local_a, local_b = refs
    size_z = LANES // 2
    factor = 0.25
    planes, rows, stride, pad = sizes.planes, sizes.rows, sizes.stride, sizes.pad_x
    own_x, own_y = sizes.own_x, sizes.own_y

    def clear(ref):
        ref[0 : pad * stride + 8] = jnp.zeros((pad * stride + 8, LANES), F32)
        ref[(pad + planes) * stride :] = jnp.zeros((pad * stride + 8, LANES), F32)

        def gap(i):
            ref[pl.ds((pad + i) * stride, 8), :] = jnp.zeros((8, LANES), F32)

        for_planes(planes, gap)

    for ref in (given, step, iterate) + ((inverse, diag) if first else ()):
        clear(ref)

    def block(b):
        gx = b // sizes.mesh_y
        gy = b % sizes.mesh_y
        source = gathered.at[gy % 2, gx * (sizes.mesh_y // 2) + gy // 2]
        for i in range(own_x):
            at = pl.ds((pad + gx * own_x + i) * stride + 8 + gy * own_y, own_y)
            tile = source[i].astype(F32)
            value = tile[:own_y] + tile[own_y:]
            if first:
                points = source[own_x + i // 2].astype(F32)[(i % 2) * own_y : (i % 2 + 1) * own_y]
                d = 6.0 * factor + (screen_weight * 0.125) * points
                diag[at, :] = d
                inv = 1.0 / d
                inverse[at, :] = inv
            else:
                inv = inverse[at, :]
            given[at, :] = value
            step[at, :] = value * inv * (1.0 / centre)

    for_planes(sizes.mesh_x * sizes.mesh_y, block)

    def second(i):
        base = (pad + i) * stride + 8
        at = pl.ds(base, rows)
        here, total = neighbours(step, base, rows, stride, size_z)
        fit = (given[at, :] + factor * total) * inverse[at, :]
        iterate[at, :] = here + (keep * here + gain * (fit - here))

    for_planes(planes, second)

    def residual(i):
        base = (pad + i) * stride + 8
        at = pl.ds(base, rows)
        here, total = neighbours(iterate, base, rows, stride, size_z)
        rows_ref[pl.ds(i * rows, rows), :] = given[at, :] + factor * total - diag[at, :] * here

    for_planes(planes, residual)
    target = 0.125 * add_lanes(rows_ref, planes, rows, mat_1)

    screen_two, screen_three = level_two
    if first:

        def screens(i):
            at = pl.ds((pad + i) * stride + 8, rows)
            rows_ref[pl.ds(i * rows, rows), :] = diag[at, :] - 6.0 * factor

        for_planes(planes, screens)
        screen_two[...] = 0.125 * add_lanes(rows_ref, planes, rows, mat_1)
    planes_2, rows_2 = planes // 4, rows // 2
    screen = screen_two[...]
    inv = 1.0 / (6.0 * factor**2 + screen)
    if first:
        rows_ref[0 : planes_2 * rows_2] = screen.reshape(-1, LANES)
        screen_three[...] = 0.125 * add_lanes(rows_ref, planes_2, rows_2, mat_2)
    value = smooth_packed_zero(target, screen, inv, factor**2, LANES // 4)
    remain = target - packed_apply(value, screen, factor**2, LANES // 4)
    rows_ref[0 : planes_2 * rows_2] = remain.reshape(-1, LANES)
    target_3 = 0.125 * add_lanes(rows_ref, planes_2, rows_2, mat_2)
    error = conjugate_gradients(target_3, screen_three[...], factor**3, LANES // 8)
    error = copy_level(error, mat_2).reshape(-1, LANES)
    count = planes_2 * rows_2
    rows_ref[pl.ds(0, count // 2, stride=2), :] = error
    rows_ref[pl.ds(1, count // 2, stride=2), :] = error
    value = value + rows_ref[0:count].reshape(value.shape)
    value = smooth_packed(value, target, screen, inv, factor**2, LANES // 4)

    rows_ref[0:rows_2] = jnp.zeros((rows_2, LANES), F32)
    rows_ref[(planes_2 + 1) * rows_2 : (planes_2 + 2) * rows_2] = jnp.zeros((rows_2, LANES), F32)
    rows_ref[rows_2 : (planes_2 + 1) * rows_2] = value.reshape(-1, LANES)
    near_2 = own_x // 4 + 2
    start = pl.multiple_of(place[0] * (own_x // 4) * rows_2, 8)
    near = rows_ref[pl.ds(start, near_2 * rows_2), :].reshape(near_2, rows_2, LANES)
    error = copy_level(near, mat_1)
    near_x, near_y = 4 * near_2, own_y + 16
    first_plane = place[0] * own_x
    for i in range(near_x):
        base = (first_plane + i) * stride + 8
        even, odd = pl.ds(base, rows_2, stride=2), pl.ds(base + 1, rows_2, stride=2)
        iterate[even, :] = iterate[even, :] + error[i]
        iterate[odd, :] = iterate[odd, :] + error[i]
    for i in range(near_x):
        at = pl.ds(pl.multiple_of((first_plane + i) * stride + place[1] * own_y, 8), near_y)
        local_a[pl.ds(8 + i * near_y, near_y), :] = iterate[at, :]
    for ref in (local_a, local_b):
        ref[0:8] = jnp.zeros((8, LANES), F32)
        ref[8 + near_x * near_y :] = jnp.zeros((8, LANES), F32)
    ends = pl.ds(8, near_y), pl.ds(8 + (near_x - 1) * near_y, near_y)
    for at in ends:
        local_b[at, :] = jnp.zeros((near_y, LANES), F32)

    def fit_of(ref, i):
        at = pl.ds(pl.multiple_of((first_plane + i) * stride + place[1] * own_y, 8), near_y)
        here, total = neighbours(ref, 8 + i * near_y, near_y, near_y, size_z)
        return here, (given[at, :] + factor * total) * inverse[at, :]

    for i in range(1, near_x - 1):
        here, fit = fit_of(local_a, i)
        local_b[pl.ds(8 + i * near_y, near_y), :] = here + (fit - here) * (1.0 / centre)
    for i in range(2, near_x - 2):
        here, fit = fit_of(local_b, i)
        at = pl.ds(8 + i * near_y, near_y)
        local_a[at, :] = here + (keep * (here - local_a[at, :]) + gain * (fit - here))


def add_correction(iterate, local, sizes, mat_0, plane):
    near_y = sizes.own_y + 16
    half_y = plane // 2
    planes = sizes.own_x + 4
    value = jnp.concatenate(
        [local[pl.ds(8 + (2 + i) * near_y + 4, half_y), :] for i in range(planes)], 0
    )
    wide = spread_lanes(value, mat_0[...])
    for i in range(planes):
        for j in range(4):
            error = wide[i * half_y : (i + 1) * half_y, (j // 2) * LANES : (j // 2 + 1) * LANES]
            for side in (0, 1):
                at = pl.ds(8 + (4 * i + j) * plane + side, half_y, stride=2)
                iterate[at, :] = iterate[at, :] + error


def middle_kernel(sizes, place, gathered, start, field, scaled, count_x, mat_0, mat_1, mat_2, *rest):
    iterate, packet, inverse, diag, screen_two, screen_three = rest[:6]
    given, step, coarse, rows_ref, local_a, local_b, other, fine_rows = rest[6:]
    wide, size_y = count_x.shape[:2]
    size_x = wide - 2 * HALO
    plane = size_y + 2 * HALO
    refs = (given, inverse, diag, step, coarse, rows_ref, (screen_two, screen_three), local_a, local_b)
    iterate[...] = start[...]
    level_one(place, gathered, sizes, (mat_1, mat_2), refs, True)
    add_correction(iterate, local_a, sizes, mat_0, plane)
    other[...] = jnp.zeros_like(other)
    finest_step_one(iterate, other, field, scaled, 2, wide - 2, plane)
    finest_step_two(other, iterate, field, scaled, 3, wide - 3, plane)
    finest_step_one(iterate, other, field, scaled, 4, wide - 4, plane)
    finest_step_two(other, iterate, field, scaled, 5, wide - 5, plane)

    def write(i, here, value):
        fine_rows[pl.ds(i * size_y, size_y), :] = value

    finest_residual(iterate, field, count_x, size_x, size_y, write)
    even, odd = restrict_finest(fine_rows, size_x, size_y, mat_0)
    send_coarse(packet, 0.125 * gather_lanes(jnp.concatenate([even, odd], 1), mat_0[...]), None, size_y // 2)


def last_kernel(sizes, place, gathered, start, field, scaled, count_x, inverse, diag, screen_two, screen_three, *rest):
    mat_0, mat_1, mat_2, solution_out, residual_out = rest[:5]
    given, step, coarse, rows_ref, local_a, local_b, iterate, other = rest[5:]
    wide, size_y = count_x.shape[:2]
    size_x = wide - 2 * HALO
    plane = size_y + 2 * HALO
    refs = (given, inverse, diag, step, coarse, rows_ref, (screen_two, screen_three), local_a, local_b)
    iterate[...] = start[...]
    level_one(place, gathered, sizes, (mat_1, mat_2), refs, False)
    add_correction(iterate, local_a, sizes, mat_0, plane)
    other[...] = jnp.zeros_like(other)
    finest_step_one(iterate, other, field, scaled, HALO - 2, wide - HALO + 2, plane)
    finest_step_two(other, iterate, field, scaled, HALO - 1, wide - HALO + 1, plane)

    def write(i, here, value):
        solution_out[i] = here
        residual_out[i] = value

    finest_residual(iterate, field, count_x, size_x, size_y, write)


def exchange(first, second, axis):
    count = lax.axis_size(axis)

    def pairs(start):
        found = []
        for i in range(start, count - 1, 2):
            found += [(i, i + 1), (i + 1, i)]
        return found

    return lax.ppermute(first, axis, pairs(0)), lax.ppermute(second, axis, pairs(1))


def gather(packet):
    spread = lax.all_to_all(packet, ("gx", "gy_chip"), 0, 0, tiled=True)
    return lax.all_gather(spread, "gy_core", axis=0)


def per_device(point_counts, face_counts):
    size_x, size_y, size_z = point_counts.shape
    assert size_z == LANES and size_x == 16 and size_y == 16
    mesh_x = lax.axis_size("gx")
    mesh_y = lax.axis_size("gy_chip") * lax.axis_size("gy_core")
    gx = lax.axis_index("gx")
    gy = lax.axis_index("gy_chip") * 2 + lax.axis_index("gy_core")
    place = jnp.stack([gx, gy]).astype(jnp.int32)
    wide, plane = size_x + 2 * HALO, size_y + 2 * HALO
    flat = 16 + wide * plane
    sizes = Sizes(mesh_x, mesh_y, size_x, size_y)
    copies = mesh_x * mesh_y // 2
    mats = [transfer_matrix(level) for level in range(3)]
    params = pltpu.CompilerParams(vmem_limit_bytes=(24 if sizes.flat < 4096 else 56) * 2**20)

    def call(kernel, outs, scratch, *args):
        return pl.pallas_call(
            kernel,
            out_shape=[jax.ShapeDtypeStruct(shape, dtype) for shape, dtype in outs],
            in_specs=[SMEM] + [VMEM] * (len(args) - 1),
            out_specs=[VMEM] * len(outs),
            scratch_shapes=[pltpu.VMEM(shape, dtype) for shape, dtype in scratch],
            compiler_params=params,
        )(*args)

    cells = (size_x, size_y, LANES)
    packet = (2 * HALO + 2, size_y, LANES)
    first, second, part, count, edge = call(
        cells_kernel,
        [(packet, BF16), (packet, BF16), (cells, BF16), (cells, BF16), ((2, size_y, LANES), BF16)],
        [],
        place,
        face_counts,
        point_counts,
    )
    first, second = exchange(first, second, "gx")
    packet = (wide + wide // size_y, size_y, LANES)
    strip = (wide, size_y, LANES)
    first, second, part_x, count_x, edge_x = call(
        wide_kernel,
        [(packet, BF16), (packet, BF16), (strip, BF16), (strip, BF16), ((wide, LANES), F32)],
        [],
        place,
        first,
        second,
        part,
        count,
        edge,
    )
    first, second = exchange(first, second, ("gy_chip", "gy_core"))
    own = sizes.own_x
    iterate, field, scaled, packet = call(
        start_kernel,
        [((flat, LANES), F32)] * 3 + [((copies, own + own // 2, 2 * sizes.own_y, LANES), BF16)],
        [((flat, LANES), F32), (packet, BF16), (packet, BF16)],
        place,
        first,
        second,
        part_x,
        count_x,
        edge_x,
        mats[0],
    )
    level = (sizes.flat, LANES)
    near = (16 + (own + 8) * (sizes.own_y + 16), LANES)
    scratch = [
        (level, F32),
        (level, F32),
        (level, F32),
        ((sizes.planes * sizes.rows, LANES), F32),
        (near, F32),
        (near, F32),
        ((flat, LANES), F32),
    ]
    level_two = (sizes.planes // 4, sizes.rows // 2, LANES)
    level_three = (sizes.planes // 16, sizes.rows // 4, LANES)
    iterate, packet, inverse, diag, screen_two, screen_three = call(
        lambda *refs: middle_kernel(sizes, *refs),
        [
            ((flat, LANES), F32),
            ((copies, own, 2 * sizes.own_y, LANES), BF16),
            (level, F32),
            (level, F32),
            (level_two, F32),
            (level_three, F32),
        ],
        scratch + [((size_x * size_y, LANES), F32)],
        place,
        gather(packet),
        iterate,
        field,
        scaled,
        count_x,
        *mats,
    )
    solution_own, residual_own = call(
        lambda *refs: last_kernel(sizes, *refs),
        [(cells, F32), (cells, F32)],
        scratch + [((flat, LANES), F32)],
        place,
        gather(packet),
        iterate,
        field,
        scaled,
        count_x,
        inverse,
        diag,
        screen_two,
        screen_three,
        *mats,
    )
    return solution_own, residual_own


def solution(mesh):
    mesh_x, mesh_y = mesh.shape["gx"], mesh.shape["gy"]
    split = Mesh(mesh.devices.reshape(mesh_x, mesh_y // 2, 2), ("gx", "gy_chip", "gy_core"))
    rows = ("gy_chip", "gy_core")

    def run(point_counts, face_counts):
        return jax.shard_map(
            per_device,
            mesh=split,
            in_specs=(P("gx", rows, None), P(None, "gx", rows, None)),
            out_specs=(P("gx", rows, None), P("gx", rows, None)),
            check_vma=False,
        )(point_counts, face_counts)

    return run
```

time: 686 us -> 71.1 us (0.10); the launches traced: 674 us -> 70.8 us
  starting transfers between devices: 360 us -> 4.4 us
  blocking collectives: 134 us -> 46.1 us
  local copies, waits for them, and re-layouts: 56.9 us -> 1.91 us
  waiting for transfers between devices: 48.8 us -> 2.35 us
  other arithmetic: 40.9 us -> 0.08 us
  between operations: 32.5 us -> 0.7 us
  Pallas kernels: 0 us -> 15.3 us
    ppermute x118 -> x4, starting transfers between devices: 360 us -> 4.4 us  [the longest x2 3.08 us: exchange(): lax.ppermute(first, axis, pairs(0))]
    all_gather x3 -> x2, blocking collectives: 134 us -> 4.66 us  [gather(): return lax.all_gather(spread, 'gy_core', axis=0)]
    reshape x13 -> x0, local copies, waits for them, and re-layouts: 47 us -> none  [the longest x7 31.7 us: restrict(): blocks = field.reshape(size_x // 2, 2, size_y // 2, 2, size_z // 2, 2)]
    ppermute x118 -> x4, waiting for transfers between devices: 48.8 us -> 2.35 us  [the longest x2 2.34 us: exchange(): lax.ppermute(first, axis, pairs(0))]
    all_to_all x0 -> x2, blocking collectives: none -> 41.5 us  [gather(): spread = lax.all_to_all(packet, ('gx', 'gy_chip'), 0, 0, tiled=True)]
    reduce_sum x33 -> x0, other arithmetic: 28.8 us -> none  [the longest x9 12.8 us: restrict(): return blocks.sum(axis=(1, 3, 5)) * 0.125]
    pallas_call x0 -> x5, Pallas kernels: none -> 15.3 us  [call(): pl.pallas_call(kernel, out_shape=[jax.ShapeDtypeStruct(shape, dtype) for...]
    broadcast_in_dim x6 -> x0, local copies, waits for them, and re-layouts: 8.4 us -> none  [prolong(): jnp.broadcast_to(field[:, None, :, None, :, None], (size_x, 2, size_y, 2,...]
  transfers between devices with their start and end apart: 118 -> 4, of which waited for: 46 -> 2; matrix products, arithmetic and copies ran while one was open for 3% -> 0% of each run, Pallas kernels for 0% -> 0%
where the time goes in v1:
time: 71.1 us; the launch traced here: 70.8 us
  blocking collectives  46.1 us (65%)
  Pallas kernels  15.3 us (22%)
  starting transfers between devices  4.4 us (6%)
  waiting for transfers between devices  2.35 us (3%)
  local copies, waits for them, and re-layouts  1.91 us (3%)
    all_to_all x2, blocking collectives, gather(): spread = lax.all_to_all(packet, ('gx', 'gy_chip'), 0, 0, tiled=True)  41.5 us
    pallas_call x5, Pallas kernels, call(): pl.pallas_call(kernel, out_shape=[jax.ShapeDtypeStruct(shape, dtype) for...  15.3 us
    all_gather x2, blocking collectives, gather(): return lax.all_gather(spread, 'gy_core', axis=0)  4.66 us
    ppermute x2, starting transfers between devices, exchange(): lax.ppermute(first, axis, pairs(0))  3.08 us
    ppermute x2, waiting for transfers between devices, exchange(): lax.ppermute(first, axis, pairs(0))  2.34 us
    unnamed x10, local copies, waits for them, and re-layouts  1.91 us
  transfers between devices with their start and end apart: 4, of which 2 were waited for; matrix products, arithmetic and copies ran while one was open for 0% of the time, Pallas kernels for 0%

profile of v1, /device:TPU:0, one launch (start us, length us, event | category | flops | bytes accessed | tf_op | source)
XLA Modules:
  0.0 70.8 jit_solution(16699381663011212858)
XLA Ops:
  0.6 0.1 pad_add_fusion.place.refs_0_
  0.7 0.0 copy-start.3
  0.7 1.0 %copy-done.3 = s32[3,16,16,128]{3,2,1,0:T(8,128)S(1)} copy-done((s32[3,16,16,128]{3,2,1,0:T(8,128)S(1)}, s32[3,16,16,128]{3,2,1,0:T(8,128)}, u32[]{:S(2)}) %copy-start.3) | copy-done | bytes 393240
  1.7 0.0 copy-start.4
  1.7 0.9 %copy-done.4 = s32[16,16,128]{2,1,0:T(8,128)S(1)} copy-done((s32[16,16,128]{2,1,0:T(8,128)S(1)}, s32[16,16,128]{2,1,0:T(8,128)}, u32[]{:S(2)}) %copy-start.4) | copy-done | bytes 131096
  2.6 0.7 shard_map.68
  3.3 3.0 %collective-permute-start = (bf16[18,16,128]{2,1,0:T(8,128)(2,1)S(1)}, bf16[18,16,128]{2,1,0:T(8,128)(2,1)S(1)}, u32[]{:S(2)}, u32[]{:S(2)}) collective-permute-start(bf16[18,16,128]{2,1,0:T(8,128)(2,1)S(1)} %get-tuple-element.22), channel_id=1, source_target_pairs={{0,4},{4,0},{8,12},{12,8},{16,20},{20,16},{24,28},{28,24},{1,5},{5... | collective-permute-start | bytes 221192 | tf_op jit(solution)/shard_map/ppermute | solution.py:585
  6.3 0.7 collective-permute-start.1
  6.9 1.7 %collective-permute-done.got_first = bf16[18,16,128]{2,1,0:T(8,128)(2,1)S(1)} collective-permute-done((bf16[18,16,128]{2,1,0:T(8,128)(2,1)S(1)}, bf16[18,16,128]{2,1,0:T(8,128)(2,1)S(1)}, u32[]{:S(2)}, u32[]{:S(2)}) %collective-permute-start) | collective-permute-done | bytes 73760 | tf_op jit(solution)/shard_map/ppermute | solution.py:585
  8.6 0.0 collective-permute-done.1.got_second
  8.6 0.0 copy-start
  8.6 0.6 shard_map.69
  9.3 0.1 collective-permute-start.2
  9.3 0.7 collective-permute-start.3
  10.0 0.7 collective-permute-done.2.got_first
  10.7 0.0 collective-permute-done.3.got_second
  10.7 0.0 copy-done
  10.7 1.2 %shard_map.70 = (f32[1040,128]{1,0:T(8,128)S(1)}, f32[1040,128]{1,0:T(8,128)S(1)}, f32[1040,128]{1,0:T(8,128)S(1)}, bf16[16,6,16,128]{3,2,1,0:T(8,128)(2,1)S(1)}) custom-call(s32[2]{0:T(128)S(1)} %pad_add_fusion.place.refs_0_, bf16[34,16,128]{2,1,0:T(8,128)(2,1)S(1)} %collective-permute-done.2.got_first, ...), custom_call_target="tpu_custom_call" | custom-call | tf_op jit(solution)/shard_map/pallas_call | solution.py:609
  11.9 27.9 %all_to_all.10 = bf16[16,6,16,128]{3,2,1,0:T(8,128)(2,1)S(1)} all-to-all(bf16[16,6,16,128]{3,2,1,0:T(8,128)(2,1)S(1)} %get-tuple-element.32), channel_id=1, replica_groups=mesh['gx'=8,'gy_chip'=2,'gy_core'=2] {'gx','gy_chip'}, dimensions={0} | all-to-all | bytes 786432 | tf_op jit(solution)/shard_map/all_to_all | solution.py:589
  39.8 0.0 copy-start.1
  39.8 0.0 copy-start.2
  39.8 2.5 %all-gather = bf16[32,6,16,128]{3,2,1,0:T(8,128)(2,1)S(1)} all-gather(bf16[16,6,16,128]{3,2,1,0:T(8,128)(2,1)S(1)} %all_to_all.10), channel_id=2, replica_groups=mesh['gx'=8,'gy_chip'=2,'gy_core'=2] {'gy_core'}, dimensions={0}, use_global_device_ids=true | all-gather | bytes 1179648 | tf_op jit(solution)/shard_map/all_gather | solution.py:590
  42.3 0.0 copy-done.1
  42.3 0.0 copy-done.2
  42.3 6.5 %shard_map.71 = (f32[1040,128]{1,0:T(8,128)S(1)}, bf16[16,4,16,128]{3,2,1,0:T(8,128)(2,1)S(1)}, f32[1608,128]{1,0:T(8,128)S(1)}, f32[1608,128]{1,0:T(8,128)S(1)}...) custom-call(s32[2]{0:T(128)S(1)} %pad_add_fusion.place.refs_0_, bf16[2,16,6,16,128]{4,3,2,1,0:T(8,128)(2,1)S(1)} %bitcast.4, ...), custom_call_target="tpu_custom_call" | custom-call | tf_op jit(solution)/shard_map/pallas_call | solution.py:609
  48.8 13.6 %all_to_all.11 = bf16[16,4,16,128]{3,2,1,0:T(8,128)(2,1)S(1)} all-to-all(bf16[16,4,16,128]{3,2,1,0:T(8,128)(2,1)S(1)} %get-tuple-element.36), channel_id=1, replica_groups=mesh['gx'=8,'gy_chip'=2,'gy_core'=2] {'gx','gy_chip'}, dimensions={0} | all-to-all | bytes 524288 | tf_op jit(solution)/shard_map/all_to_all | solution.py:589
  62.4 2.2 %all-gather.1 = bf16[32,4,16,128]{3,2,1,0:T(8,128)(2,1)S(1)} all-gather(bf16[16,4,16,128]{3,2,1,0:T(8,128)(2,1)S(1)} %all_to_all.11), channel_id=3, replica_groups=mesh['gx'=8,'gy_chip'=2,'gy_core'=2] {'gy_core'}, dimensions={0}, use_global_device_ids=true | all-gather | bytes 786432 | tf_op jit(solution)/shard_map/all_gather | solution.py:590
  64.5 6.3 %shard_map.72 = (f32[16,16,128]{2,1,0:T(8,128)}, f32[16,16,128]{2,1,0:T(8,128)}) custom-call(s32[2]{0:T(128)S(1)} %pad_add_fusion.place.refs_0_, bf16[2,16,4,16,128]{4,3,2,1,0:T(8,128)(2,1)S(1)} %bitcast.5, f32[1040,128]{1,0:T(8,128)S(1)} %get-tuple-element.37.refs_2_, f32[1040,128]{1,0:T(8,128)S(1)} %get-tuple-element.34.refs_3_, ...), custom_call_target="tpu_custom_call" | custom-call | tf_op jit(solution)/shard_map/pallas_call | solution.py:609
Async XLA Ops:
  0.7 1.0 %copy-start.3 = (s32[3,16,16,128]{3,2,1,0:T(8,128)S(1)}, s32[3,16,16,128]{3,2,1,0:T(8,128)}, u32[]{:S(2)}) copy-start(s32[3,16,16,128]{3,2,1,0:T(8,128)} %faces.1) | copy-start | bytes 1179652
  1.7 0.9 %copy-start.4 = (s32[16,16,128]{2,1,0:T(8,128)S(1)}, s32[16,16,128]{2,1,0:T(8,128)}, u32[]{:S(2)}) copy-start(s32[16,16,128]{2,1,0:T(8,128)} %points.1) | copy-start | bytes 393220
  3.3 5.3 %collective-permute-start = (bf16[18,16,128]{2,1,0:T(8,128)(2,1)S(1)}, bf16[18,16,128]{2,1,0:T(8,128)(2,1)S(1)}, u32[]{:S(2)}, u32[]{:S(2)}) collective-permute-start(bf16[18,16,128]{2,1,0:T(8,128)(2,1)S(1)} %get-tuple-element.22), channel_id=1, source_target_pairs={{0,4},{4,0},{8,12},{12,8},{16,20},{20,16},{24,28},{28,24},{1,5},{5... | collective-permute-start | bytes 221192 | tf_op jit(solution)/shard_map/ppermute | solution.py:585
  6.3 2.3 %collective-permute-start.1 = (bf16[18,16,128]{2,1,0:T(8,128)(2,1)S(1)}, bf16[18,16,128]{2,1,0:T(8,128)(2,1)S(1)}, u32[]{:S(2)}, u32[]{:S(2)}) collective-permute-start(bf16[18,16,128]{2,1,0:T(8,128)(2,1)S(1)} %get-tuple-element.23), channel_id=1, source_target_pairs={{4,8},{8,4},{12,16},{16,12},{20,24},{24,20},{5,9},{9,5},{13,17},{1... | collective-permute-start | bytes 221192 | tf_op jit(solution)/shard_map/ppermute | solution.py:585
  8.6 2.1 %copy-start = (bf16[256,128]{1,0:T(8,128)(2,1)S(1)}, bf16[256,128]{1,0:T(8,128)(2,1)}, u32[]{:S(2)}) copy-start(bf16[256,128]{1,0:T(8,128)(2,1)} %constant.20.clone.matrix.refs_6_.refs_10_) | copy-start | bytes 196612
  9.3 1.4 %collective-permute-start.2 = (bf16[34,16,128]{2,1,0:T(8,128)(2,1)S(1)}, bf16[34,16,128]{2,1,0:T(8,128)(2,1)S(1)}, u32[]{:S(2)}, u32[]{:S(2)}) collective-permute-start(bf16[34,16,128]{2,1,0:T(8,128)(2,1)S(1)} %get-tuple-element.27), channel_id=1, source_target_pairs={{0,1},{1,0},{2,3},{3,2},{4,5},{5,4},{6,7},{7,6},{8,9},{9,8},{10,11... | collective-permute-start | bytes 417800 | tf_op jit(solution)/shard_map/ppermute | solution.py:585
  9.3 1.3 %collective-permute-start.3 = (bf16[34,16,128]{2,1,0:T(8,128)(2,1)S(1)}, bf16[34,16,128]{2,1,0:T(8,128)(2,1)S(1)}, u32[]{:S(2)}, u32[]{:S(2)}) collective-permute-start(bf16[34,16,128]{2,1,0:T(8,128)(2,1)S(1)} %get-tuple-element.28), channel_id=1, source_target_pairs={{1,2},{2,1},{5,6},{6,5},{9,10},{10,9},{13,14},{14,13},{17,18},{18,... | collective-permute-start | bytes 417800 | tf_op jit(solution)/shard_map/ppermute | solution.py:585
  39.8 2.5 %copy-start.1 = (bf16[512,128]{1,0:T(8,128)(2,1)S(1)}, bf16[512,128]{1,0:T(8,128)(2,1)}, u32[]{:S(2)}) copy-start(bf16[512,128]{1,0:T(8,128)(2,1)} %constant.22.clone.refs_8_.refs_12_) | copy-start | bytes 393220
  39.8 2.5 %copy-start.2 = (bf16[512,128]{1,0:T(8,128)(2,1)S(1)}, bf16[512,128]{1,0:T(8,128)(2,1)}, u32[]{:S(2)}) copy-start(bf16[512,128]{1,0:T(8,128)(2,1)} %constant.21.clone.refs_7_.refs_11_) | copy-start | bytes 393220

commit v2 on v1

--- a/solution.py
+++ b/solution.py
@@ -26,6 +26,7 @@
 
 VMEM = pl.BlockSpec(memory_space=pltpu.VMEM)
 SMEM = pl.BlockSpec(memory_space=pltpu.SMEM)
+FAR = pl.BlockSpec(memory_space=pltpu.HBM)
 
 
 def transfer_matrix(level):
@@ -42,37 +43,35 @@
 
 def two_parts(value):
     high = value.astype(BF16)
-    return high, (value - high.astype(F32)).astype(BF16)
+    return jnp.concatenate([high, (value - high.astype(F32)).astype(BF16)], 0)
 
 
 def gather_lanes(value, matrix):
-    high, low = two_parts(value)
-    return jnp.dot(high, matrix, preferred_element_type=F32) + jnp.dot(low, matrix, preferred_element_type=F32)
+    both = jnp.dot(two_parts(value), matrix, preferred_element_type=F32)
+    return both[: value.shape[0]] + both[value.shape[0] :]
 
 
 def spread_lanes(value, matrix):
     dims = (((1,), (1,)), ((), ()))
-    high, low = two_parts(value)
-    return lax.dot_general(high, matrix, dims, preferred_element_type=F32) + lax.dot_general(
-        low, matrix, dims, preferred_element_type=F32
-    )
-
-
-def lane_index(rows):
-    return lax.broadcasted_iota(jnp.int32, (rows, LANES), 1)
+    both = lax.dot_general(two_parts(value), matrix, dims, preferred_element_type=F32)
+    return both[: value.shape[0]] + both[value.shape[0] :]
+
+
+def lane_index():
+    return lax.broadcasted_iota(jnp.int32, (1, LANES), 1)
 
 
 def z_sum(value, size_z):
-    lane = lane_index(value.shape[0]) & (size_z - 1)
-    return jnp.where(lane != 0, pltpu.roll(value, 1, 1), 0.0) + jnp.where(
-        lane != size_z - 1, pltpu.roll(value, LANES - 1, 1), 0.0
-    )
+    lane = lane_index() & (size_z - 1)
+    inner_low = (lane != 0).astype(F32)
+    inner_high = (lane != size_z - 1).astype(F32)
+    return pltpu.roll(value, 1, 1) * inner_low + pltpu.roll(value, LANES - 1, 1) * inner_high
 
 
 def x_sum(before, here, after, size_z):
     if size_z == LANES:
         return before + after
-    lane = lane_index(here.shape[0])
+    lane = lax.broadcasted_iota(jnp.int32, here.shape, 1)
     if 2 * size_z == LANES:
         return pltpu.roll(here + jnp.where(lane < size_z, after, before), size_z, 1)
     up = pltpu.roll(jnp.where(lane < size_z, after, here), LANES - size_z, 1)
@@ -108,7 +107,7 @@
 
 def cells_kernel(place, faces, points, first, second, part, count, edge):
     size_x, size_y = points.shape[:2]
-    lane = lane_index(size_y)
+    lane = lax.broadcasted_iota(jnp.int32, (size_y, LANES), 1)
     row = lax.broadcasted_iota(jnp.int32, (size_y, LANES), 0)
     last_x = None
     for i in range(size_x):
@@ -330,25 +329,30 @@
     return (6.0 * value - (total.reshape(value.shape) + along_y)) * factor + screen * value
 
 
-def total_of(value):
-    return jnp.sum(jnp.sum(value, 0), keepdims=True)[None]
+def totals_of(*values):
+    rows = jnp.concatenate([jnp.sum(value, 0) for value in values], 0)
+    sums = jnp.sum(rows, 1, keepdims=True).reshape(len(values), -1, 1)
+    sums = jnp.sum(sums, 1, keepdims=True)
+    return [sums[i : i + 1] for i in range(len(values))]
 
 
 def conjugate_gradients(target, screen, factor, size_z):
     iterate = jnp.zeros_like(target)
     remain = target
     search = target
-    norm_now = total_of(remain * remain)
     for step in range(COARSE_ITERS):
         image = packed_apply(search, screen, factor, size_z)
-        length = norm_now / total_of(search * image)
+        if step + 1 == COARSE_ITERS:
+            norm_now, bent = totals_of(remain * remain, search * image)
+            return iterate + (norm_now / bent) * search
+        norm_now, bent, mixed, norm_image = totals_of(
+            remain * remain, search * image, remain * image, image * image
+        )
+        length = norm_now / bent
         iterate = iterate + length * search
-        if step + 1 < COARSE_ITERS:
-            remain = remain - length * image
-            norm_next = total_of(remain * remain)
-            search = remain + (norm_next / norm_now) * search
-            norm_now = norm_next
-    return iterate
+        remain = remain - length * image
+        norm_next = norm_now - 2.0 * length * mixed + length * length * norm_image
+        search = remain + (norm_next / norm_now) * search
 
 
 def smooth_packed(iterate, target, screen, inv, factor, size_z):
@@ -512,7 +516,10 @@
         local_a[at, :] = here + (keep * (here - local_a[at, :]) + gain * (fit - here))
 
 
-def add_correction(iterate, local, sizes, mat_0, plane):
+def add_correction(start, iterate, local, sizes, mat_0, plane):
+    ends = pl.ds(0, 8), pl.ds(start.shape[0] - 8, 8)
+    for at in ends:
+        iterate[at, :] = start[at, :]
     near_y = sizes.own_y + 16
     half_y = plane // 2
     planes = sizes.own_x + 4
@@ -525,7 +532,7 @@
             error = wide[i * half_y : (i + 1) * half_y, (j // 2) * LANES : (j // 2 + 1) * LANES]
             for side in (0, 1):
                 at = pl.ds(8 + (4 * i + j) * plane + side, half_y, stride=2)
-                iterate[at, :] = iterate[at, :] + error
+                iterate[at, :] = start[at, :] + error
 
 
 def middle_kernel(sizes, place, gathered, start, field, scaled, count_x, mat_0, mat_1, mat_2, *rest):
@@ -535,10 +542,8 @@
     size_x = wide - 2 * HALO
     plane = size_y + 2 * HALO
     refs = (given, inverse, diag, step, coarse, rows_ref, (screen_two, screen_three), local_a, local_b)
-    iterate[...] = start[...]
     level_one(place, gathered, sizes, (mat_1, mat_2), refs, True)
-    add_correction(iterate, local_a, sizes, mat_0, plane)
-    other[...] = jnp.zeros_like(other)
+    add_correction(start, iterate, local_a, sizes, mat_0, plane)
     finest_step_one(iterate, other, field, scaled, 2, wide - 2, plane)
     finest_step_two(other, iterate, field, scaled, 3, wide - 3, plane)
     finest_step_one(iterate, other, field, scaled, 4, wide - 4, plane)
@@ -553,24 +558,35 @@
 
 
 def last_kernel(sizes, place, gathered, start, field, scaled, count_x, inverse, diag, screen_two, screen_three, *rest):
-    mat_0, mat_1, mat_2, solution_out, residual_out = rest[:5]
-    given, step, coarse, rows_ref, local_a, local_b, iterate, other = rest[5:]
+    mat_0, mat_1, mat_2, solution_far, residual_far = rest[:5]
+    given, step, coarse, rows_ref, local_a, local_b, iterate, other, solution_out, residual_out, left = rest[5:]
     wide, size_y = count_x.shape[:2]
     size_x = wide - 2 * HALO
     plane = size_y + 2 * HALO
     refs = (given, inverse, diag, step, coarse, rows_ref, (screen_two, screen_three), local_a, local_b)
-    iterate[...] = start[...]
     level_one(place, gathered, sizes, (mat_1, mat_2), refs, False)
-    add_correction(iterate, local_a, sizes, mat_0, plane)
-    other[...] = jnp.zeros_like(other)
+    add_correction(start, iterate, local_a, sizes, mat_0, plane)
     finest_step_one(iterate, other, field, scaled, HALO - 2, wide - HALO + 2, plane)
     finest_step_two(other, iterate, field, scaled, HALO - 1, wide - HALO + 1, plane)
 
+    def send(source, target, which):
+        copy = pltpu.make_async_copy(source, target, left.at[which])
+        copy.start()
+        return copy
+
+    for i in range(size_x):
+        solution_out[i] = iterate[pl.ds(8 + (HALO + i) * plane + HALO, size_y), :]
+    copies = [send(solution_out, solution_far, 0)]
+
     def write(i, here, value):
-        solution_out[i] = here
         residual_out[i] = value
+        if (2 * i + 2) % size_x == 0:
+            half = pl.ds(i + 1 - size_x // 2, size_x // 2)
+            copies.append(send(residual_out.at[half], residual_far.at[half], 1 + (i + 1) * 2 // size_x))
 
     finest_residual(iterate, field, count_x, size_x, size_y, write)
+    for copy in copies:
+        copy.wait()
 
 
 def exchange(first, second, axis):
@@ -605,13 +621,14 @@
     mats = [transfer_matrix(level) for level in range(3)]
     params = pltpu.CompilerParams(vmem_limit_bytes=(24 if sizes.flat < 4096 else 56) * 2**20)
 
-    def call(kernel, outs, scratch, *args):
+    def call(kernel, outs, scratch, *args, copies=0, far_out=False):
         return pl.pallas_call(
             kernel,
             out_shape=[jax.ShapeDtypeStruct(shape, dtype) for shape, dtype in outs],
             in_specs=[SMEM] + [VMEM] * (len(args) - 1),
-            out_specs=[VMEM] * len(outs),
-            scratch_shapes=[pltpu.VMEM(shape, dtype) for shape, dtype in scratch],
+            out_specs=[FAR if far_out else VMEM] * len(outs),
+            scratch_shapes=[pltpu.VMEM(shape, dtype) for shape, dtype in scratch]
+            + ([pltpu.SemaphoreType.DMA((copies,))] if copies else []),
             compiler_params=params,
         )(*args)
 
@@ -688,7 +705,7 @@
     solution_own, residual_own = call(
         lambda *refs: last_kernel(sizes, *refs),
         [(cells, F32), (cells, F32)],
-        scratch + [((flat, LANES), F32)],
+        scratch + [((flat, LANES), F32), (cells, F32), (cells, F32)],
         place,
         gather(packet),
         iterate,
@@ -700,6 +717,8 @@
         screen_two,
         screen_three,
         *mats,
+        copies=4,
+        far_out=True,
     )
     return solution_own, residual_own
 

time: 71.1 us -> 69.5 us (0.977)
  Pallas kernels: 15.3 us -> 13.6 us
    pallas_call x5, Pallas kernels: 15.3 us -> 13.6 us  [call(): pl.pallas_call(kernel, out_shape=[jax.ShapeDtypeStruct(shape, dtype) for...]
where the time goes in v2:
time: 69.5 us; the launch traced here: 69.2 us
  blocking collectives  46.1 us (66%)
  Pallas kernels  13.6 us (20%)
  starting transfers between devices  4.4 us (6%)
  waiting for transfers between devices  2.35 us (3%)
  local copies, waits for them, and re-layouts  1.91 us (3%)
  between operations  0.7 us (1%)
    all_to_all x2, blocking collectives, gather(): spread = lax.all_to_all(packet, ('gx', 'gy_chip'), 0, 0, tiled=True)  41.5 us
    pallas_call x5, Pallas kernels, call(): pl.pallas_call(kernel, out_shape=[jax.ShapeDtypeStruct(shape, dtype) for...  13.6 us
    all_gather x2, blocking collectives, gather(): return lax.all_gather(spread, 'gy_core', axis=0)  4.66 us
    ppermute x2, starting transfers between devices, exchange(): lax.ppermute(first, axis, pairs(0))  3.08 us
    ppermute x2, waiting for transfers between devices, exchange(): lax.ppermute(first, axis, pairs(0))  2.34 us
    unnamed x10, local copies, waits for them, and re-layouts  1.91 us
  transfers between devices with their start and end apart: 4, of which 2 were waited for; matrix products, arithmetic and copies ran while one was open for 0% of the time, Pallas kernels for 0%

profile of v2, /device:TPU:0, one launch (start us, length us, event | category | flops | bytes accessed | tf_op | source)
XLA Modules:
  0.0 69.2 jit_solution(2705130751901807123)
XLA Ops:
  0.6 0.1 pad_add_fusion.place.refs_0_
  0.7 0.0 copy-start.3
  0.7 1.0 %copy-done.3 = s32[3,16,16,128]{3,2,1,0:T(8,128)S(1)} copy-done((s32[3,16,16,128]{3,2,1,0:T(8,128)S(1)}, s32[3,16,16,128]{3,2,1,0:T(8,128)}, u32[]{:S(2)}) %copy-start.3) | copy-done | bytes 393240
  1.7 0.0 copy-start.4
  1.7 0.9 %copy-done.4 = s32[16,16,128]{2,1,0:T(8,128)S(1)} copy-done((s32[16,16,128]{2,1,0:T(8,128)S(1)}, s32[16,16,128]{2,1,0:T(8,128)}, u32[]{:S(2)}) %copy-start.4) | copy-done | bytes 131096
  2.6 0.7 shard_map.68
  3.3 3.0 %collective-permute-start = (bf16[18,16,128]{2,1,0:T(8,128)(2,1)S(1)}, bf16[18,16,128]{2,1,0:T(8,128)(2,1)S(1)}, u32[]{:S(2)}, u32[]{:S(2)}) collective-permute-start(bf16[18,16,128]{2,1,0:T(8,128)(2,1)S(1)} %get-tuple-element.22), channel_id=1, source_target_pairs={{0,4},{4,0},{8,12},{12,8},{16,20},{20,16},{24,28},{28,24},{1,5},{5... | collective-permute-start | bytes 221192 | tf_op jit(solution)/shard_map/ppermute | solution.py:601
  6.3 0.7 collective-permute-start.1
  6.9 1.7 %collective-permute-done.got_first = bf16[18,16,128]{2,1,0:T(8,128)(2,1)S(1)} collective-permute-done((bf16[18,16,128]{2,1,0:T(8,128)(2,1)S(1)}, bf16[18,16,128]{2,1,0:T(8,128)(2,1)S(1)}, u32[]{:S(2)}, u32[]{:S(2)}) %collective-permute-start) | collective-permute-done | bytes 73760 | tf_op jit(solution)/shard_map/ppermute | solution.py:601
  8.6 0.0 collective-permute-done.1.got_second
  8.6 0.0 copy-start
  8.6 0.6 shard_map.69
  9.3 0.1 collective-permute-start.2
  9.3 0.7 collective-permute-start.3
  10.0 0.7 collective-permute-done.2.got_first
  10.7 0.0 collective-permute-done.3.got_second
  10.7 0.0 copy-done
  10.7 1.2 %shard_map.70 = (f32[1040,128]{1,0:T(8,128)S(1)}, f32[1040,128]{1,0:T(8,128)S(1)}, f32[1040,128]{1,0:T(8,128)S(1)}, bf16[16,6,16,128]{3,2,1,0:T(8,128)(2,1)S(1)}) custom-call(s32[2]{0:T(128)S(1)} %pad_add_fusion.place.refs_0_, bf16[34,16,128]{2,1,0:T(8,128)(2,1)S(1)} %collective-permute-done.2.got_first, ...), custom_call_target="tpu_custom_call" | custom-call | tf_op jit(solution)/shard_map/pallas_call | solution.py:625
  11.9 27.9 %all_to_all.10 = bf16[16,6,16,128]{3,2,1,0:T(8,128)(2,1)S(1)} all-to-all(bf16[16,6,16,128]{3,2,1,0:T(8,128)(2,1)S(1)} %get-tuple-element.32), channel_id=1, replica_groups=mesh['gx'=8,'gy_chip'=2,'gy_core'=2] {'gx','gy_chip'}, dimensions={0} | all-to-all | bytes 786432 | tf_op jit(solution)/shard_map/all_to_all | solution.py:605
  39.8 0.0 copy-start.1
  39.8 0.0 copy-start.2
  39.8 2.5 %all-gather = bf16[32,6,16,128]{3,2,1,0:T(8,128)(2,1)S(1)} all-gather(bf16[16,6,16,128]{3,2,1,0:T(8,128)(2,1)S(1)} %all_to_all.10), channel_id=2, replica_groups=mesh['gx'=8,'gy_chip'=2,'gy_core'=2] {'gy_core'}, dimensions={0}, use_global_device_ids=true | all-gather | bytes 1179648 | tf_op jit(solution)/shard_map/all_gather | solution.py:606
  42.3 0.0 copy-done.1
  42.3 0.0 copy-done.2
  42.3 5.7 %shard_map.71 = (f32[1040,128]{1,0:T(8,128)S(1)}, bf16[16,4,16,128]{3,2,1,0:T(8,128)(2,1)S(1)}, f32[1608,128]{1,0:T(8,128)S(1)}, f32[1608,128]{1,0:T(8,128)S(1)}...) custom-call(s32[2]{0:T(128)S(1)} %pad_add_fusion.place.refs_0_, bf16[2,16,6,16,128]{4,3,2,1,0:T(8,128)(2,1)S(1)} %bitcast.4, ...), custom_call_target="tpu_custom_call" | custom-call | tf_op jit(solution)/shard_map/pallas_call | solution.py:625
  48.0 13.6 %all_to_all.11 = bf16[16,4,16,128]{3,2,1,0:T(8,128)(2,1)S(1)} all-to-all(bf16[16,4,16,128]{3,2,1,0:T(8,128)(2,1)S(1)} %get-tuple-element.36), channel_id=1, replica_groups=mesh['gx'=8,'gy_chip'=2,'gy_core'=2] {'gx','gy_chip'}, dimensions={0} | all-to-all | bytes 524288 | tf_op jit(solution)/shard_map/all_to_all | solution.py:605
  61.6 2.2 %all-gather.1 = bf16[32,4,16,128]{3,2,1,0:T(8,128)(2,1)S(1)} all-gather(bf16[16,4,16,128]{3,2,1,0:T(8,128)(2,1)S(1)} %all_to_all.11), channel_id=3, replica_groups=mesh['gx'=8,'gy_chip'=2,'gy_core'=2] {'gy_core'}, dimensions={0}, use_global_device_ids=true | all-gather | bytes 786432 | tf_op jit(solution)/shard_map/all_gather | solution.py:606
  63.7 5.4 %shard_map.72 = (f32[16,16,128]{2,1,0:T(8,128)}, f32[16,16,128]{2,1,0:T(8,128)}) custom-call(s32[2]{0:T(128)S(1)} %pad_add_fusion.place.refs_0_, bf16[2,16,4,16,128]{4,3,2,1,0:T(8,128)(2,1)S(1)} %bitcast.5, f32[1040,128]{1,0:T(8,128)S(1)} %get-tuple-element.37.refs_2_, f32[1040,128]{1,0:T(8,128)S(1)} %get-tuple-element.34.refs_3_, ...), custom_call_target="tpu_custom_call" | custom-call | tf_op jit(solution)/shard_map/pallas_call | solution.py:625
Async XLA Ops:
  0.7 1.0 %copy-start.3 = (s32[3,16,16,128]{3,2,1,0:T(8,128)S(1)}, s32[3,16,16,128]{3,2,1,0:T(8,128)}, u32[]{:S(2)}) copy-start(s32[3,16,16,128]{3,2,1,0:T(8,128)} %faces.1) | copy-start | bytes 1179652
  1.7 0.9 %copy-start.4 = (s32[16,16,128]{2,1,0:T(8,128)S(1)}, s32[16,16,128]{2,1,0:T(8,128)}, u32[]{:S(2)}) copy-start(s32[16,16,128]{2,1,0:T(8,128)} %points.1) | copy-start | bytes 393220
  3.3 5.3 %collective-permute-start = (bf16[18,16,128]{2,1,0:T(8,128)(2,1)S(1)}, bf16[18,16,128]{2,1,0:T(8,128)(2,1)S(1)}, u32[]{:S(2)}, u32[]{:S(2)}) collective-permute-start(bf16[18,16,128]{2,1,0:T(8,128)(2,1)S(1)} %get-tuple-element.22), channel_id=1, source_target_pairs={{0,4},{4,0},{8,12},{12,8},{16,20},{20,16},{24,28},{28,24},{1,5},{5... | collective-permute-start | bytes 221192 | tf_op jit(solution)/shard_map/ppermute | solution.py:601
  6.3 2.3 %collective-permute-start.1 = (bf16[18,16,128]{2,1,0:T(8,128)(2,1)S(1)}, bf16[18,16,128]{2,1,0:T(8,128)(2,1)S(1)}, u32[]{:S(2)}, u32[]{:S(2)}) collective-permute-start(bf16[18,16,128]{2,1,0:T(8,128)(2,1)S(1)} %get-tuple-element.23), channel_id=1, source_target_pairs={{4,8},{8,4},{12,16},{16,12},{20,24},{24,20},{5,9},{9,5},{13,17},{1... | collective-permute-start | bytes 221192 | tf_op jit(solution)/shard_map/ppermute | solution.py:601
  8.6 2.1 %copy-start = (bf16[256,128]{1,0:T(8,128)(2,1)S(1)}, bf16[256,128]{1,0:T(8,128)(2,1)}, u32[]{:S(2)}) copy-start(bf16[256,128]{1,0:T(8,128)(2,1)} %constant.20.clone.matrix.refs_6_.refs_10_) | copy-start | bytes 196612
  9.3 1.4 %collective-permute-start.2 = (bf16[34,16,128]{2,1,0:T(8,128)(2,1)S(1)}, bf16[34,16,128]{2,1,0:T(8,128)(2,1)S(1)}, u32[]{:S(2)}, u32[]{:S(2)}) collective-permute-start(bf16[34,16,128]{2,1,0:T(8,128)(2,1)S(1)} %get-tuple-element.27), channel_id=1, source_target_pairs={{0,1},{1,0},{2,3},{3,2},{4,5},{5,4},{6,7},{7,6},{8,9},{9,8},{10,11... | collective-permute-start | bytes 417800 | tf_op jit(solution)/shard_map/ppermute | solution.py:601
  9.3 1.3 %collective-permute-start.3 = (bf16[34,16,128]{2,1,0:T(8,128)(2,1)S(1)}, bf16[34,16,128]{2,1,0:T(8,128)(2,1)S(1)}, u32[]{:S(2)}, u32[]{:S(2)}) collective-permute-start(bf16[34,16,128]{2,1,0:T(8,128)(2,1)S(1)} %get-tuple-element.28), channel_id=1, source_target_pairs={{1,2},{2,1},{5,6},{6,5},{9,10},{10,9},{13,14},{14,13},{17,18},{18,... | collective-permute-start | bytes 417800 | tf_op jit(solution)/shard_map/ppermute | solution.py:601
  39.8 2.5 %copy-start.1 = (bf16[512,128]{1,0:T(8,128)(2,1)S(1)}, bf16[512,128]{1,0:T(8,128)(2,1)}, u32[]{:S(2)}) copy-start(bf16[512,128]{1,0:T(8,128)(2,1)} %constant.22.clone.refs_8_.refs_12_) | copy-start | bytes 393220
  39.8 2.5 %copy-start.2 = (bf16[512,128]{1,0:T(8,128)(2,1)S(1)}, bf16[512,128]{1,0:T(8,128)(2,1)}, u32[]{:S(2)}) copy-start(bf16[512,128]{1,0:T(8,128)(2,1)} %constant.21.clone.refs_7_.refs_11_) | copy-start | bytes 393220

commit v3 on v2

--- a/solution.py
+++ b/solution.py
@@ -105,24 +105,30 @@
     return ref[pl.ds(start, rows // 2, stride=2), :] + ref[pl.ds(start + 1, rows // 2, stride=2), :]
 
 
-def cells_kernel(place, faces, points, first, second, part, count, edge):
-    size_x, size_y = points.shape[:2]
+def pack_cell(faces, points):
+    word = points << 18
+    for c in range(3):
+        word = word + ((faces[c] + 32) << (6 * c))
+    return word
+
+
+def cells_kernel(place, words, first, second, part, count, edge):
+    size_x, size_y = words.shape[:2]
     lane = lax.broadcasted_iota(jnp.int32, (size_y, LANES), 1)
     row = lax.broadcasted_iota(jnp.int32, (size_y, LANES), 0)
     last_x = None
     for i in range(size_x):
-        along_x = faces[0, i]
-        along_y = faces[1, i]
-        along_z = faces[2, i]
+        word = words[i]
+        along_x, along_y, along_z = [((word >> (6 * c)) & 63) - 32 for c in range(3)]
         total = jnp.where(row != 0, pltpu.roll(along_y, 1, 0), 0) - along_y
         total = total + (jnp.where(lane != 0, pltpu.roll(along_z, 1, 1), 0) - along_z) - along_x
         if last_x is not None:
             total = total + last_x
         last_x = along_x
         part[i] = total.astype(F32).astype(BF16)
-        count[i] = (points[i] + 1).astype(F32).astype(BF16)
+        count[i] = ((word >> 18) + 1).astype(F32).astype(BF16)
     edge[0] = last_x.astype(F32).astype(BF16)
-    edge[1] = faces[1, :, size_y - 1, :].astype(F32).astype(BF16)
+    edge[1] = (((words[:, size_y - 1, :] >> 6) & 63) - 32).astype(F32).astype(BF16)
 
     def write(up, down):
         for target, start in ((up, size_x - HALO), (down, 0)):
@@ -189,23 +195,35 @@
         write(second, first)
 
 
-def finest_step_one(source, target, field, scaled, start, end, plane):
-    for i in range(start, end, 2):
-        base = 8 + i * plane
-        rows = 2 * plane
+def finest_parts(margin, wide, plane):
+    planes = range(HALO - margin, wide - HALO + margin)
+    if margin > 4:
+        return [(8 + i * plane, 2 * plane) for i in planes[::2]]
+    return [(8 + i * plane + HALO - 4, plane - 2 * HALO + 8) for i in planes]
+
+
+def finest_step_one(source, target, field, scaled, margin, wide, plane):
+    for base, rows in finest_parts(margin, wide, plane):
+        at = pl.ds(base, rows)
         here, total = neighbours(source, base, rows, plane, LANES)
-        fit = (field[pl.ds(base, rows), :] + total) * scaled[pl.ds(base, rows), :]
-        target[pl.ds(base, rows), :] = here + (fit - here) * (1.0 / centre)
-
-
-def finest_step_two(source, old, field, scaled, start, end, plane):
-    for i in range(start, end, 2):
-        base = 8 + i * plane
-        rows = 2 * plane
+        fit = (field[at, :] + total) * scaled[at, :]
+        target[at, :] = here + (fit - here) * (1.0 / centre)
+
+
+def finest_step_two(source, old, field, scaled, margin, wide, plane):
+    for base, rows in finest_parts(margin, wide, plane):
+        at = pl.ds(base, rows)
         here, total = neighbours(source, base, rows, plane, LANES)
-        fit = (field[pl.ds(base, rows), :] + total) * scaled[pl.ds(base, rows), :]
-        before = old[pl.ds(base, rows), :]
-        old[pl.ds(base, rows), :] = here + (keep * (here - before) + gain * (fit - here))
+        fit = (field[at, :] + total) * scaled[at, :]
+        old[at, :] = here + (keep * (here - old[at, :]) + gain * (fit - here))
+
+
+def finest_step_two_from_zero(source, target, field, scaled, margin, wide, plane):
+    for base, rows in finest_parts(margin, wide, plane):
+        at = pl.ds(base, rows)
+        here, total = neighbours(source, base, rows, plane, LANES)
+        fit = (field[at, :] + total) * scaled[at, :]
+        target[at, :] = here + (keep * here + gain * (fit - here))
 
 
 def finest_residual(iterate, field, count, size_x, size_y, write):
@@ -224,35 +242,17 @@
     return even, odd
 
 
-def start_kernel(
-    place, got_first, got_second, part_x, count_x, edge_x, matrix, iterate, field, inverse, packet, rows_ref, low, high
-):
+def first_step(place, got, part_x, count_x, edge_x, iterate, field, inverse, margin):
     wide, size_y = part_x.shape[:2]
-    size_x = wide - 2 * HALO
     plane = size_y + 2 * HALO
-    odd_y = place[1] % 2
-
-    @pl.when(odd_y == 0)
-    def _():
-        low[...] = got_second[...]
-        high[...] = got_first[...]
-
-    @pl.when(odd_y == 1)
-    def _():
-        low[...] = got_first[...]
-        high[...] = got_second[...]
-
+    even = place[1] % 2 == 0
     top = lax.broadcasted_iota(jnp.int32, (HALO, LANES), 0) == 0
-    zero = jnp.zeros((8, LANES), F32)
-    for ref in (iterate, field, inverse):
-        ref[0:8] = zero
-        ref[8 + wide * plane :] = zero
-    low_edge_rows = [low[wide + j].astype(F32) for j in range(wide // size_y)]
-    for i in range(wide):
-        below = low[i].astype(F32)
-        above = high[i].astype(F32)
+    under_rows = [jnp.where(even, got[1][wide + j], got[0][wide + j]).astype(F32) for j in range(wide // size_y)]
+    for i in range(HALO - margin, wide - HALO + margin):
+        below = jnp.where(even, got[1][i], got[0][i]).astype(F32)
+        above = jnp.where(even, got[0][i], got[1][i]).astype(F32)
         own = part_x[i].astype(F32)
-        under = low_edge_rows[i // size_y][i % size_y : i % size_y + 1]
+        under = under_rows[i // size_y][i % size_y : i % size_y + 1]
         over = edge_x[i : i + 1]
         cells = jnp.concatenate(
             [
@@ -266,33 +266,47 @@
         points = jnp.concatenate([below[HALO:], count_x[i].astype(F32), above[HALO:]], 0)
         given = flux_scale * cells
         inv = jnp.where(points > 0.0, 1.0 / (6.0 - screen_weight + screen_weight * points), 0.0)
-        base = 8 + i * plane
-        field[pl.ds(base, plane), :] = given
-        inverse[pl.ds(base, plane), :] = inv
-        iterate[pl.ds(base, plane), :] = (given * inv) * (1.0 / centre)
-
-    scratch = rows_ref
-    for i in range(1, wide - 1, 2):
-        base = 8 + i * plane
-        rows = 2 * plane
-        here, total = neighbours(iterate, base, rows, plane, LANES)
-        fit = (field[pl.ds(base, rows), :] + total) * inverse[pl.ds(base, rows), :]
-        scratch[pl.ds(base, rows), :] = here + (keep * here + gain * (fit - here))
-    for i in range(1, wide - 1, 2):
-        base = 8 + i * plane
-        iterate[pl.ds(base, 2 * plane), :] = scratch[pl.ds(base, 2 * plane), :]
+        at = pl.ds(8 + i * plane, plane)
+        field[at, :] = given
+        inverse[at, :] = inv
+        iterate[at, :] = (given * inv) * (1.0 / centre)
+
+
+def start_kernel(
+    place, got_first, got_second, part_x, count_x, edge_x, matrix, packet, first, second, field, inverse, rows_ref
+):
+    wide, size_y = part_x.shape[:2]
+    size_x = wide - 2 * HALO
+    plane = size_y + 2 * HALO
+    first_step(place, (got_first, got_second), part_x, count_x, edge_x, first, field, inverse, 2)
+    finest_step_two_from_zero(first, second, field, inverse, 1, wide, plane)
 
     def write(i, here, value):
-        scratch[pl.ds(i * size_y, size_y), :] = value
-
-    finest_residual(iterate, field, count_x, size_x, size_y, write)
-    even, odd = restrict_finest(scratch, size_x, size_y, matrix)
+        rows_ref[pl.ds(i * size_y, size_y), :] = value
+
+    finest_residual(second, field, count_x, size_x, size_y, write)
+    even, odd = restrict_finest(rows_ref, size_x, size_y, matrix)
     coarse = 0.125 * gather_lanes(jnp.concatenate([even, odd], 1), matrix[...])
     for i in range(size_x):
-        scratch[pl.ds(i * size_y, size_y), :] = count_x[HALO + i].astype(F32) - 1.0
-    even, odd = restrict_finest(scratch, size_x, size_y, matrix)
+        rows_ref[pl.ds(i * size_y, size_y), :] = count_x[HALO + i].astype(F32) - 1.0
+    even, odd = restrict_finest(rows_ref, size_x, size_y, matrix)
     points = jnp.dot(jnp.concatenate([even, odd], 1).astype(BF16), matrix[...], preferred_element_type=F32)
     send_coarse(packet, coarse, points, size_y // 2)
+
+
+def surroundings_kernel(
+    place, after, got_first, got_second, part_x, count_x, edge_x, iterate, field, inverse, first
+):
+    wide, size_y = part_x.shape[:2]
+    plane = size_y + 2 * HALO
+    zero = jnp.zeros((8, LANES), F32)
+    for ref in (iterate, field, inverse, first):
+        ref[0:8] = zero
+        ref[8 + wide * plane :] = zero
+    first_step(place, (got_first, got_second), part_x, count_x, edge_x, first, field, inverse, HALO)
+    for base, rows in ((8, plane), (8 + (wide - 1) * plane, plane)):
+        iterate[pl.ds(base, rows), :] = first[pl.ds(base, rows), :]
+    finest_step_two_from_zero(first, iterate, field, inverse, HALO - 1, wide, plane)
 
 
 def send_coarse(packet, coarse, points, size_y):
@@ -412,12 +426,17 @@
     for ref in (given, step, iterate) + ((inverse, diag) if first else ()):
         clear(ref)
 
+    core = place[1] % 2
+    per_core = sizes.mesh_x * sizes.mesh_y // 2
+
     def block(b):
-        gx = b // sizes.mesh_y
-        gy = b % sizes.mesh_y
-        source = gathered.at[gy % 2, gx * (sizes.mesh_y // 2) + gy // 2]
+        source, side = (gathered[0], core) if b < per_core else (gathered[1], 1 - core)
+        gx = b % per_core // (sizes.mesh_y // 2)
+        gy = 2 * (b % (sizes.mesh_y // 2)) + side
+        source = source.at[b % per_core]
         for i in range(own_x):
-            at = pl.ds((pad + gx * own_x + i) * stride + 8 + gy * own_y, own_y)
+            start = (pad + gx * own_x + i) * stride + 8 + gy * own_y
+            at = pl.ds(pl.multiple_of(start, 8), own_y)
             tile = source[i].astype(F32)
             value = tile[:own_y] + tile[own_y:]
             if first:
@@ -431,7 +450,8 @@
             given[at, :] = value
             step[at, :] = value * inv * (1.0 / centre)
 
-    for_planes(sizes.mesh_x * sizes.mesh_y, block)
+    for b in range(sizes.mesh_x * sizes.mesh_y):
+        block(b)
 
     def second(i):
         base = (pad + i) * stride + 8
@@ -535,19 +555,19 @@
                 iterate[at, :] = start[at, :] + error
 
 
-def middle_kernel(sizes, place, gathered, start, field, scaled, count_x, mat_0, mat_1, mat_2, *rest):
+def middle_kernel(sizes, place, near, far, start, field, scaled, count_x, mat_0, mat_1, mat_2, *rest):
     iterate, packet, inverse, diag, screen_two, screen_three = rest[:6]
     given, step, coarse, rows_ref, local_a, local_b, other, fine_rows = rest[6:]
     wide, size_y = count_x.shape[:2]
     size_x = wide - 2 * HALO
     plane = size_y + 2 * HALO
     refs = (given, inverse, diag, step, coarse, rows_ref, (screen_two, screen_three), local_a, local_b)
-    level_one(place, gathered, sizes, (mat_1, mat_2), refs, True)
+    level_one(place, (near, far), sizes, (mat_1, mat_2), refs, True)
     add_correction(start, iterate, local_a, sizes, mat_0, plane)
-    finest_step_one(iterate, other, field, scaled, 2, wide - 2, plane)
-    finest_step_two(other, iterate, field, scaled, 3, wide - 3, plane)
-    finest_step_one(iterate, other, field, scaled, 4, wide - 4, plane)
-    finest_step_two(other, iterate, field, scaled, 5, wide - 5, plane)
+    finest_step_one(iterate, other, field, scaled, 6, wide, plane)
+    finest_step_two(other, iterate, field, scaled, 5, wide, plane)
+    finest_step_one(iterate, other, field, scaled, 4, wide, plane)
+    finest_step_two(other, iterate, field, scaled, 3, wide, plane)
 
     def write(i, here, value):
         fine_rows[pl.ds(i * size_y, size_y), :] = value
@@ -557,17 +577,17 @@
     send_coarse(packet, 0.125 * gather_lanes(jnp.concatenate([even, odd], 1), mat_0[...]), None, size_y // 2)
 
 
-def last_kernel(sizes, place, gathered, start, field, scaled, count_x, inverse, diag, screen_two, screen_three, *rest):
+def last_kernel(sizes, place, near, far, start, field, scaled, count_x, inverse, diag, screen_two, screen_three, *rest):
     mat_0, mat_1, mat_2, solution_far, residual_far = rest[:5]
     given, step, coarse, rows_ref, local_a, local_b, iterate, other, solution_out, residual_out, left = rest[5:]
     wide, size_y = count_x.shape[:2]
     size_x = wide - 2 * HALO
     plane = size_y + 2 * HALO
     refs = (given, inverse, diag, step, coarse, rows_ref, (screen_two, screen_three), local_a, local_b)
-    level_one(place, gathered, sizes, (mat_1, mat_2), refs, False)
+    level_one(place, (near, far), sizes, (mat_1, mat_2), refs, False)
     add_correction(start, iterate, local_a, sizes, mat_0, plane)
-    finest_step_one(iterate, other, field, scaled, HALO - 2, wide - HALO + 2, plane)
-    finest_step_two(other, iterate, field, scaled, HALO - 1, wide - HALO + 1, plane)
+    finest_step_one(iterate, other, field, scaled, 2, wide, plane)
+    finest_step_two(other, iterate, field, scaled, 1, wide, plane)
 
     def send(source, target, which):
         copy = pltpu.make_async_copy(source, target, left.at[which])
@@ -602,8 +622,8 @@
 
 
 def gather(packet):
-    spread = lax.all_to_all(packet, ("gx", "gy_chip"), 0, 0, tiled=True)
-    return lax.all_gather(spread, "gy_core", axis=0)
+    near = lax.all_to_all(packet, ("gx", "gy_chip"), 0, 0, tiled=True)
+    return near, lax.ppermute(near, "gy_core", [(0, 1), (1, 0)])
 
 
 def per_device(point_counts, face_counts):
@@ -621,7 +641,7 @@
     mats = [transfer_matrix(level) for level in range(3)]
     params = pltpu.CompilerParams(vmem_limit_bytes=(24 if sizes.flat < 4096 else 56) * 2**20)
 
-    def call(kernel, outs, scratch, *args, copies=0, far_out=False):
+    def call(kernel, outs, scratch, *args, copies=0, far_out=False, cost=None):
         return pl.pallas_call(
             kernel,
             out_shape=[jax.ShapeDtypeStruct(shape, dtype) for shape, dtype in outs],
@@ -630,6 +650,7 @@
             scratch_shapes=[pltpu.VMEM(shape, dtype) for shape, dtype in scratch]
             + ([pltpu.SemaphoreType.DMA((copies,))] if copies else []),
             compiler_params=params,
+            cost_estimate=cost,
         )(*args)
 
     cells = (size_x, size_y, LANES)
@@ -639,8 +660,7 @@
         [(packet, BF16), (packet, BF16), (cells, BF16), (cells, BF16), ((2, size_y, LANES), BF16)],
         [],
         place,
-        face_counts,
-        point_counts,
+        pack_cell(face_counts, point_counts),
     )
     first, second = exchange(first, second, "gx")
     packet = (wide + wide // size_y, size_y, LANES)
@@ -658,27 +678,35 @@
     )
     first, second = exchange(first, second, ("gy_chip", "gy_core"))
     own = sizes.own_x
-    iterate, field, scaled, packet = call(
+    received = (first, second, part_x, count_x, edge_x)
+    flat_f32 = ((flat, LANES), F32)
+    (packet,) = call(
         start_kernel,
-        [((flat, LANES), F32)] * 3 + [((copies, own + own // 2, 2 * sizes.own_y, LANES), BF16)],
-        [((flat, LANES), F32), (packet, BF16), (packet, BF16)],
+        [((copies, own + own // 2, 2 * sizes.own_y, LANES), BF16)],
+        [flat_f32] * 4 + [((size_x * size_y, LANES), F32)],
         place,
-        first,
-        second,
-        part_x,
-        count_x,
-        edge_x,
+        *received,
         mats[0],
     )
+    near, far = gather(packet)
+    iterate, field, scaled = call(
+        surroundings_kernel,
+        [flat_f32] * 3,
+        [flat_f32],
+        place,
+        near,
+        *received,
+        cost=pl.CostEstimate(flops=1 << 22, bytes_accessed=4 << 20, transcendentals=0),
+    )
     level = (sizes.flat, LANES)
-    near = (16 + (own + 8) * (sizes.own_y + 16), LANES)
+    around = (16 + (own + 8) * (sizes.own_y + 16), LANES)
     scratch = [
         (level, F32),
         (level, F32),
         (level, F32),
         ((sizes.planes * sizes.rows, LANES), F32),
-        (near, F32),
-        (near, F32),
+        (around, F32),
+        (around, F32),
         ((flat, LANES), F32),
     ]
     level_two = (sizes.planes // 4, sizes.rows // 2, LANES)
@@ -695,7 +723,8 @@
         ],
         scratch + [((size_x * size_y, LANES), F32)],
         place,
-        gather(packet),
+        near,
+        far,
         iterate,
         field,
         scaled,
@@ -707,7 +736,7 @@
         [(cells, F32), (cells, F32)],
         scratch + [((flat, LANES), F32), (cells, F32), (cells, F32)],
         place,
-        gather(packet),
+        *gather(packet),
         iterate,
         field,
         scaled,

time: 69.5 us -> 67.2 us (0.967)
  blocking collectives: 46.1 us -> 41.5 us
  waiting for transfers between devices: 2.35 us -> 4.55 us
  local copies, waits for them, and re-layouts: 1.91 us -> 0.01 us
  other arithmetic: 0.08 us -> 1.21 us
  Pallas kernels: 13.6 us -> 14.6 us
    all_gather x2 -> x0, blocking collectives: 4.66 us -> none  [gather(): return lax.all_gather(spread, 'gy_core', axis=0)]
    ppermute x0 -> x2, waiting for transfers between devices: none -> 2.21 us  [gather(): return (near, lax.ppermute(near, 'gy_core', [(0, 1), (1, 0)]))]
    unnamed x10 -> x6, local copies, waits for them, and re-layouts: 1.91 us -> 0.01 us
    add x0 -> x1, other arithmetic: none -> 1.14 us  [pack_cell(): word = word + (faces[c] + 32 << 6 * c)]
    pallas_call x5 -> x6, Pallas kernels: 13.6 us -> 14.6 us  [call(): pl.pallas_call(kernel, out_shape=[jax.ShapeDtypeStruct(shape, dtype) for...]
  transfers between devices with their start and end apart: 4 -> 6, of which waited for: 2 -> 4; matrix products, arithmetic and copies ran while one was open for 0% -> 0% of each run, Pallas kernels for 0% -> 2%
where the time goes in v3:
time: 67.2 us; the launch traced here: 67 us
  blocking collectives  41.5 us (62%)
  Pallas kernels  14.6 us (22%)
  waiting for transfers between devices  4.55 us (7%)
  starting transfers between devices  4.41 us (7%)
  other arithmetic  1.21 us (2%)
  between operations  0.7 us (1%)
    all_to_all x2, blocking collectives, gather(): near = lax.all_to_all(packet, ('gx', 'gy_chip'), 0, 0, tiled=True)  41.5 us
    pallas_call x6, Pallas kernels, call(): pl.pallas_call(kernel, out_shape=[jax.ShapeDtypeStruct(shape, dtype) for...  14.6 us
    ppermute x2, starting transfers between devices, exchange(): lax.ppermute(first, axis, pairs(0))  3.08 us
    ppermute x2, waiting for transfers between devices, exchange(): lax.ppermute(first, axis, pairs(0))  2.34 us
    ppermute x2, waiting for transfers between devices, gather(): return (near, lax.ppermute(near, 'gy_core', [(0, 1), (1, 0)]))  2.21 us
  transfers between devices with their start and end apart: 6, of which 4 were waited for; matrix products, arithmetic and copies ran while one was open for 0% of the time, Pallas kernels for 2%

profile of v3, /device:TPU:0, one launch (start us, length us, event | category | flops | bytes accessed | tf_op | source)
XLA Modules:
  0.0 67.0 jit_solution(10298744506452363022)
XLA Ops:
  0.6 0.1 pad_add_fusion.place.refs_0_
  0.7 1.1 %bitcast_add_fusion.words = s32[16,16,128]{2,1,0:T(8,128)S(1)} fusion(s32[3,16,16,128]{3,2,1,0:T(8,128)} %param.6, s32[16,16,128]{2,1,0:T(8,128)} %param.5), kind=kLoop, calls=%fused_computation | loop fusion | flops 327680 | bytes 655360 | tf_op jit(solution)/shard_map/add | solution.py:111
  1.9 0.7 %shard_map.68 = (bf16[18,16,128]{2,1,0:T(8,128)(2,1)S(1)}, bf16[18,16,128]{2,1,0:T(8,128)(2,1)S(1)}, bf16[16,16,128]{2,1,0:T(8,128)(2,1)S(1)}, bf16[16,16,128]{2,1,0:T(8,128)(2,1)S(1)}, bf16[2,16,128]{2,1,0:T(8,128)(2,1)S(1)}) custom-call(s32[2]{0:T(128)S(1)} %pad_add_fusion.place.refs_0_, s32[16,16,128]{2,1,0:T(8,128)S(1)} %bitcast_add_fusion.words), custom_call_target="tpu_custom_call" | custom-call | tf_op jit(solution)/shard_map/pallas_call | solution.py:645
  2.5 3.0 %collective-permute-start = (bf16[18,16,128]{2,1,0:T(8,128)(2,1)S(1)}, bf16[18,16,128]{2,1,0:T(8,128)(2,1)S(1)}, u32[]{:S(2)}, u32[]{:S(2)}) collective-permute-start(bf16[18,16,128]{2,1,0:T(8,128)(2,1)S(1)} %get-tuple-element.21), channel_id=1, source_target_pairs={{0,4},{4,0},{8,12},{12,8},{16,20},{20,16},{24,28},{28,24},{1,5},{5... | collective-permute-start | bytes 221192 | tf_op jit(solution)/shard_map/ppermute | solution.py:621
  5.5 0.7 collective-permute-start.1
  6.2 1.7 %collective-permute-done.got_first = bf16[18,16,128]{2,1,0:T(8,128)(2,1)S(1)} collective-permute-done((bf16[18,16,128]{2,1,0:T(8,128)(2,1)S(1)}, bf16[18,16,128]{2,1,0:T(8,128)(2,1)S(1)}, u32[]{:S(2)}, u32[]{:S(2)}) %collective-permute-start) | collective-permute-done | bytes 73760 | tf_op jit(solution)/shard_map/ppermute | solution.py:621
  7.9 0.0 collective-permute-done.1.got_second
  7.9 0.0 copy-start
  7.9 0.6 shard_map.69
  8.5 0.1 collective-permute-start.2
  8.6 0.7 collective-permute-start.3
  9.3 0.7 collective-permute-done.2.got_first
  9.9 0.0 collective-permute-done.3.got_second
  9.9 0.0 copy-done
  9.9 1.1 %shard_map.70 = bf16[16,6,16,128]{3,2,1,0:T(8,128)(2,1)S(1)} custom-call(s32[2]{0:T(128)S(1)} %pad_add_fusion.place.refs_0_, bf16[34,16,128]{2,1,0:T(8,128)(2,1)S(1)} %collective-permute-done.2.got_first, bf16[34,16,128]{2,1,0:T(8,128)(2,1)S(1)} %collective-permute-done.3.got_second, bf16[32,16,128]{2,1,0:T(8,128)(2,1)S(1)} %get-tuple-element.28.part_x, ...), custom_call_target="tpu_custom_call" | custom-call | tf_op jit(solution)/shard_map/pallas_call | solution.py:645
  11.1 27.9 %all_to_all.10.after.refs_1_ = bf16[16,6,16,128]{3,2,1,0:T(8,128)(2,1)S(1)} all-to-all(bf16[16,6,16,128]{3,2,1,0:T(8,128)(2,1)S(1)} %shard_map.70), channel_id=1, replica_groups=mesh['gx'=8,'gy_chip'=2,'gy_core'=2] {'gx','gy_chip'}, dimensions={0} | all-to-all | bytes 786432 | tf_op jit(solution)/shard_map/all_to_all | solution.py:625
  38.9 0.0 copy-start.1
  38.9 0.0 copy-start.2
  38.9 0.0 collective-permute-start.4
  38.9 1.0 %shard_map.71 = (f32[1040,128]{1,0:T(8,128)S(1)}, f32[1040,128]{1,0:T(8,128)S(1)}, f32[1040,128]{1,0:T(8,128)S(1)}) custom-call(s32[2]{0:T(128)S(1)} %pad_add_fusion.place.refs_0_, bf16[16,6,16,128]{3,2,1,0:T(8,128)(2,1)S(1)} %all_to_all.10.after.refs_1_, bf16[34,16,128]{2,1,0:T(8,128)(2,1)S(1)} %collective-permute-done.2.got_first, ...), custom_call_target="tpu_custom_call" | custom-call | flops 4194304 | bytes 4194304 | tf_op jit(solution)/shard_map/pallas_call | solution.py:645
  40.0 0.7 %collective-permute-done.4.refs_2_ = bf16[16,6,16,128]{3,2,1,0:T(8,128)(2,1)S(1)} collective-permute-done((bf16[16,6,16,128]{3,2,1,0:T(8,128)(2,1)S(1)}, bf16[16,6,16,128]{3,2,1,0:T(8,128)(2,1)S(1)}, u32[]{:S(2)}, u32[]{:S(2)}) %collective-permute-start.4) | collective-permute-done | bytes 393248 | tf_op jit(solution)/shard_map/ppermute | solution.py:626
  40.7 0.0 copy-done.1
  40.7 0.0 copy-done.2
  40.7 5.7 %shard_map.72 = (f32[1040,128]{1,0:T(8,128)S(1)}, bf16[16,4,16,128]{3,2,1,0:T(8,128)(2,1)S(1)}, f32[1608,128]{1,0:T(8,128)S(1)}, f32[1608,128]{1,0:T(8,128)S(1)}...) custom-call(s32[2]{0:T(128)S(1)} %pad_add_fusion.place.refs_0_, ...), custom_call_target="tpu_custom_call" | custom-call | tf_op jit(solution)/shard_map/pallas_call | solution.py:645
  46.4 13.6 %all_to_all.11.refs_1_ = bf16[16,4,16,128]{3,2,1,0:T(8,128)(2,1)S(1)} all-to-all(bf16[16,4,16,128]{3,2,1,0:T(8,128)(2,1)S(1)} %get-tuple-element.34), channel_id=1, replica_groups=mesh['gx'=8,'gy_chip'=2,'gy_core'=2] {'gx','gy_chip'}, dimensions={0} | all-to-all | bytes 524288 | tf_op jit(solution)/shard_map/all_to_all | solution.py:625
  60.0 0.0 collective-permute-start.5
  60.0 1.5 %collective-permute-done.5.refs_2_ = bf16[16,4,16,128]{3,2,1,0:T(8,128)(2,1)S(1)} collective-permute-done((bf16[16,4,16,128]{3,2,1,0:T(8,128)(2,1)S(1)}, bf16[16,4,16,128]{3,2,1,0:T(8,128)(2,1)S(1)}, u32[]{:S(2)}, u32[]{:S(2)}) %collective-permute-start.5) | collective-permute-done | bytes 262176 | tf_op jit(solution)/shard_map/ppermute | solution.py:626
  61.5 5.5 %shard_map.73 = (f32[16,16,128]{2,1,0:T(8,128)}, f32[16,16,128]{2,1,0:T(8,128)}) custom-call(s32[2]{0:T(128)S(1)} %pad_add_fusion.place.refs_0_, bf16[16,4,16,128]{3,2,1,0:T(8,128)(2,1)S(1)} %all_to_all.11.refs_1_, bf16[16,4,16,128]{3,2,1,0:T(8,128)(2,1)S(1)} %collective-permute-done.5.refs_2_, f32[1040,128]{1,0:T(8,128)S(1)} %get-tuple-element.35.refs_3_, ...), custom_call_target="tpu_custom_call" | custom-call | tf_op jit(solution)/shard_map/pallas_call | solution.py:645
Async XLA Ops:
  2.5 5.3 %collective-permute-start = (bf16[18,16,128]{2,1,0:T(8,128)(2,1)S(1)}, bf16[18,16,128]{2,1,0:T(8,128)(2,1)S(1)}, u32[]{:S(2)}, u32[]{:S(2)}) collective-permute-start(bf16[18,16,128]{2,1,0:T(8,128)(2,1)S(1)} %get-tuple-element.21), channel_id=1, source_target_pairs={{0,4},{4,0},{8,12},{12,8},{16,20},{20,16},{24,28},{28,24},{1,5},{5... | collective-permute-start | bytes 221192 | tf_op jit(solution)/shard_map/ppermute | solution.py:621
  5.5 2.3 %collective-permute-start.1 = (bf16[18,16,128]{2,1,0:T(8,128)(2,1)S(1)}, bf16[18,16,128]{2,1,0:T(8,128)(2,1)S(1)}, u32[]{:S(2)}, u32[]{:S(2)}) collective-permute-start(bf16[18,16,128]{2,1,0:T(8,128)(2,1)S(1)} %get-tuple-element.22), channel_id=1, source_target_pairs={{4,8},{8,4},{12,16},{16,12},{20,24},{24,20},{5,9},{9,5},{13,17},{1... | collective-permute-start | bytes 221192 | tf_op jit(solution)/shard_map/ppermute | solution.py:621
  7.9 2.1 %copy-start = (bf16[256,128]{1,0:T(8,128)(2,1)S(1)}, bf16[256,128]{1,0:T(8,128)(2,1)}, u32[]{:S(2)}) copy-start(bf16[256,128]{1,0:T(8,128)(2,1)} %constant.30.clone.matrix.refs_7_.refs_11_) | copy-start | bytes 196612
  8.5 1.4 %collective-permute-start.2 = (bf16[34,16,128]{2,1,0:T(8,128)(2,1)S(1)}, bf16[34,16,128]{2,1,0:T(8,128)(2,1)S(1)}, u32[]{:S(2)}, u32[]{:S(2)}) collective-permute-start(bf16[34,16,128]{2,1,0:T(8,128)(2,1)S(1)} %get-tuple-element.26), channel_id=1, source_target_pairs={{0,1},{1,0},{2,3},{3,2},{4,5},{5,4},{6,7},{7,6},{8,9},{9,8},{10,11... | collective-permute-start | bytes 417800 | tf_op jit(solution)/shard_map/ppermute | solution.py:621
  8.6 1.3 %collective-permute-start.3 = (bf16[34,16,128]{2,1,0:T(8,128)(2,1)S(1)}, bf16[34,16,128]{2,1,0:T(8,128)(2,1)S(1)}, u32[]{:S(2)}, u32[]{:S(2)}) collective-permute-start(bf16[34,16,128]{2,1,0:T(8,128)(2,1)S(1)} %get-tuple-element.27), channel_id=1, source_target_pairs={{1,2},{2,1},{5,6},{6,5},{9,10},{10,9},{13,14},{14,13},{17,18},{18,... | collective-permute-start | bytes 417800 | tf_op jit(solution)/shard_map/ppermute | solution.py:621
  38.9 1.7 %copy-start.1 = (bf16[512,128]{1,0:T(8,128)(2,1)S(1)}, bf16[512,128]{1,0:T(8,128)(2,1)}, u32[]{:S(2)}) copy-start(bf16[512,128]{1,0:T(8,128)(2,1)} %constant.32.clone.refs_9_.refs_13_) | copy-start | bytes 393220
  38.9 1.7 %copy-start.2 = (bf16[512,128]{1,0:T(8,128)(2,1)S(1)}, bf16[512,128]{1,0:T(8,128)(2,1)}, u32[]{:S(2)}) copy-start(bf16[512,128]{1,0:T(8,128)(2,1)} %constant.31.clone.refs_8_.refs_12_) | copy-start | bytes 393220
  38.9 1.7 %collective-permute-start.4 = (bf16[16,6,16,128]{3,2,1,0:T(8,128)(2,1)S(1)}, bf16[16,6,16,128]{3,2,1,0:T(8,128)(2,1)S(1)}, u32[]{:S(2)}, u32[]{:S(2)}) collective-permute-start(bf16[16,6,16,128]{3,2,1,0:T(8,128)(2,1)S(1)} %all_to_all.10.after.refs_1_), channel_id=1, source_target_pairs={{0,1},{1,0},{2,3},{3,2},{4,5},{5,4},{6,7},{7,6},{8,9},{9,8},{10,11... | collective-permute-start | bytes 1179656 | tf_op jit(solution)/shard_map/ppermute | solution.py:626
  60.0 1.5 %collective-permute-start.5 = (bf16[16,4,16,128]{3,2,1,0:T(8,128)(2,1)S(1)}, bf16[16,4,16,128]{3,2,1,0:T(8,128)(2,1)S(1)}, u32[]{:S(2)}, u32[]{:S(2)}) collective-permute-start(bf16[16,4,16,128]{3,2,1,0:T(8,128)(2,1)S(1)} %all_to_all.11.refs_1_), channel_id=1, source_target_pairs={{0,1},{1,0},{2,3},{3,2},{4,5},{5,4},{6,7},{7,6},{8,9},{9,8},{10,11... | collective-permute-start | bytes 786440 | tf_op jit(solution)/shard_map/ppermute | solution.py:626

commit v4 on v3

--- a/solution.py
+++ b/solution.py
@@ -309,21 +309,27 @@
     finest_step_two_from_zero(first, iterate, field, inverse, HALO - 1, wide, plane)
 
 
+def scale_of(code):
+    return jnp.exp2(code * (1.0 / 128.0))
+
+
 def send_coarse(packet, coarse, points, size_y):
     copies = packet.shape[0]
-    planes = coarse.shape[0] // size_y
-    high = coarse.astype(BF16).astype(F32)
-    low = coarse - high
-    for i in range(planes):
-        at = slice(i * size_y, (i + 1) * size_y)
-        tile = jnp.concatenate([high[at], low[at]], 0).astype(BF16)
+    tiles = [coarse[i : i + size_y] for i in range(0, coarse.shape[0], size_y)]
+    largest = jnp.abs(tiles[0])
+    for tile in tiles[1:]:
+        largest = jnp.maximum(largest, jnp.abs(tile))
+    largest = jnp.maximum(jnp.max(largest, 1, keepdims=True), 1e-30)
+    code = jnp.ceil(128.0 * jnp.log2(largest * (1.0 / 32766.0)))
+    scale = scale_of(-code)
+    rows = [jnp.round(tile * scale) for tile in tiles]
+    rows += [jnp.broadcast_to(code, (size_y, LANES)), jnp.zeros((size_y, LANES), F32)]
+    if points is not None:
+        rows += [points[i : i + size_y] for i in range(0, points.shape[0], size_y)]
+    for i in range(0, len(rows), 2):
+        tile = jnp.concatenate(rows[i : i + 2], 0).astype(jnp.int32).astype(jnp.int16)
         for k in range(copies):
-            packet[k, i] = tile
-    if points is not None:
-        for i in range(planes // 2):
-            tile = points[2 * i * size_y : 2 * (i + 1) * size_y].astype(BF16)
-            for k in range(copies):
-                packet[k, planes + i] = tile
+            packet[k, i // 2] = tile
 
 
 def packed_apply(value, screen, factor, size_z):
@@ -433,15 +439,17 @@
         source, side = (gathered[0], core) if b < per_core else (gathered[1], 1 - core)
         gx = b % per_core // (sizes.mesh_y // 2)
         gy = 2 * (b % (sizes.mesh_y // 2)) + side
-        source = source.at[b % per_core]
+        tiles = []
+        for i in range(source.shape[1]):
+            tile = source[b % per_core, i].astype(jnp.int32).astype(F32)
+            tiles += [tile[:own_y], tile[own_y:]]
+        scale = scale_of(tiles[own_x])
         for i in range(own_x):
             start = (pad + gx * own_x + i) * stride + 8 + gy * own_y
             at = pl.ds(pl.multiple_of(start, 8), own_y)
-            tile = source[i].astype(F32)
-            value = tile[:own_y] + tile[own_y:]
+            value = tiles[i] * scale
             if first:
-                points = source[own_x + i // 2].astype(F32)[(i % 2) * own_y : (i % 2 + 1) * own_y]
-                d = 6.0 * factor + (screen_weight * 0.125) * points
+                d = 6.0 * factor + (screen_weight * 0.125) * tiles[own_x + 2 + i]
                 diag[at, :] = d
                 inv = 1.0 / d
                 inverse[at, :] = inv
@@ -682,7 +690,7 @@
     flat_f32 = ((flat, LANES), F32)
     (packet,) = call(
         start_kernel,
-        [((copies, own + own // 2, 2 * sizes.own_y, LANES), BF16)],
+        [((copies, own + 1, 2 * sizes.own_y, LANES), jnp.int16)],
         [flat_f32] * 4 + [((size_x * size_y, LANES), F32)],
         place,
         *received,
@@ -715,7 +723,7 @@
         lambda *refs: middle_kernel(sizes, *refs),
         [
             ((flat, LANES), F32),
-            ((copies, own, 2 * sizes.own_y, LANES), BF16),
+            ((copies, own // 2 + 1, 2 * sizes.own_y, LANES), jnp.int16),
             (level, F32),
             (level, F32),
             (level_two, F32),

time: 67.2 us -> 64.6 us (0.961)
  blocking collectives: 41.5 us -> 38.8 us
    all_to_all x2, blocking collectives: 41.5 us -> 38.8 us  [gather(): near = lax.all_to_all(packet, ('gx', 'gy_chip'), 0, 0, tiled=True)]
where the time goes in v4:
time: 64.6 us; the launch traced here: 64.3 us
  blocking collectives  38.8 us (60%)
  Pallas kernels  14.8 us (23%)
  starting transfers between devices  4.41 us (7%)
  waiting for transfers between devices  4.36 us (7%)
  other arithmetic  1.21 us (2%)
  between operations  0.7 us (1%)
    all_to_all x2, blocking collectives, gather(): near = lax.all_to_all(packet, ('gx', 'gy_chip'), 0, 0, tiled=True)  38.8 us
    pallas_call x6, Pallas kernels, call(): pl.pallas_call(kernel, out_shape=[jax.ShapeDtypeStruct(shape, dtype) for...  14.8 us
    ppermute x2, starting transfers between devices, exchange(): lax.ppermute(first, axis, pairs(0))  3.08 us
    ppermute x2, waiting for transfers between devices, exchange(): lax.ppermute(first, axis, pairs(0))  2.34 us
    ppermute x2, waiting for transfers between devices, gather(): return (near, lax.ppermute(near, 'gy_core', [(0, 1), (1, 0)]))  2.02 us
    ppermute x2, starting transfers between devices, exchange(): lax.ppermute(second, axis, pairs(1))  1.32 us
  transfers between devices with their start and end apart: 6, of which 4 were waited for; matrix products, arithmetic and copies ran while one was open for 0% of the time, Pallas kernels for 2%

profile of v4, /device:TPU:0, one launch (start us, length us, event | category | flops | bytes accessed | tf_op | source)
XLA Modules:
  0.0 64.3 jit_solution(5042041738341705889)
XLA Ops:
  0.6 0.1 pad_add_fusion.place.refs_0_
  0.7 1.1 %bitcast_add_fusion.words = s32[16,16,128]{2,1,0:T(8,128)S(1)} fusion(s32[3,16,16,128]{3,2,1,0:T(8,128)} %param.6, s32[16,16,128]{2,1,0:T(8,128)} %param.5), kind=kLoop, calls=%fused_computation | loop fusion | flops 327680 | bytes 655360 | tf_op jit(solution)/shard_map/add | solution.py:111
  1.9 0.7 %shard_map.68 = (bf16[18,16,128]{2,1,0:T(8,128)(2,1)S(1)}, bf16[18,16,128]{2,1,0:T(8,128)(2,1)S(1)}, bf16[16,16,128]{2,1,0:T(8,128)(2,1)S(1)}, bf16[16,16,128]{2,1,0:T(8,128)(2,1)S(1)}, bf16[2,16,128]{2,1,0:T(8,128)(2,1)S(1)}) custom-call(s32[2]{0:T(128)S(1)} %pad_add_fusion.place.refs_0_, s32[16,16,128]{2,1,0:T(8,128)S(1)} %bitcast_add_fusion.words), custom_call_target="tpu_custom_call" | custom-call | tf_op jit(solution)/shard_map/pallas_call | solution.py:653
  2.5 3.0 %collective-permute-start = (bf16[18,16,128]{2,1,0:T(8,128)(2,1)S(1)}, bf16[18,16,128]{2,1,0:T(8,128)(2,1)S(1)}, u32[]{:S(2)}, u32[]{:S(2)}) collective-permute-start(bf16[18,16,128]{2,1,0:T(8,128)(2,1)S(1)} %get-tuple-element.21), channel_id=1, source_target_pairs={{0,4},{4,0},{8,12},{12,8},{16,20},{20,16},{24,28},{28,24},{1,5},{5... | collective-permute-start | bytes 221192 | tf_op jit(solution)/shard_map/ppermute | solution.py:629
  5.5 0.7 %collective-permute-start.1 = (bf16[18,16,128]{2,1,0:T(8,128)(2,1)S(1)}, bf16[18,16,128]{2,1,0:T(8,128)(2,1)S(1)}, u32[]{:S(2)}, u32[]{:S(2)}) collective-permute-start(bf16[18,16,128]{2,1,0:T(8,128)(2,1)S(1)} %get-tuple-element.22), channel_id=1, source_target_pairs={{4,8},{8,4},{12,16},{16,12},{20,24},{24,20},{5,9},{9,5},{13,17},{1... | collective-permute-start | bytes 221192 | tf_op jit(solution)/shard_map/ppermute | solution.py:629
  6.2 1.7 %collective-permute-done.got_first = bf16[18,16,128]{2,1,0:T(8,128)(2,1)S(1)} collective-permute-done((bf16[18,16,128]{2,1,0:T(8,128)(2,1)S(1)}, bf16[18,16,128]{2,1,0:T(8,128)(2,1)S(1)}, u32[]{:S(2)}, u32[]{:S(2)}) %collective-permute-start) | collective-permute-done | bytes 73760 | tf_op jit(solution)/shard_map/ppermute | solution.py:629
  7.9 0.0 collective-permute-done.1.got_second
  7.9 0.0 copy-start
  7.9 0.6 shard_map.69
  8.5 0.1 collective-permute-start.2
  8.6 0.7 %collective-permute-start.3 = (bf16[34,16,128]{2,1,0:T(8,128)(2,1)S(1)}, bf16[34,16,128]{2,1,0:T(8,128)(2,1)S(1)}, u32[]{:S(2)}, u32[]{:S(2)}) collective-permute-start(bf16[34,16,128]{2,1,0:T(8,128)(2,1)S(1)} %get-tuple-element.27), channel_id=1, source_target_pairs={{1,2},{2,1},{5,6},{6,5},{9,10},{10,9},{13,14},{14,13},{17,18},{18,... | collective-permute-start | bytes 417800 | tf_op jit(solution)/shard_map/ppermute | solution.py:629
  9.3 0.7 %collective-permute-done.2.got_first = bf16[34,16,128]{2,1,0:T(8,128)(2,1)S(1)} collective-permute-done((bf16[34,16,128]{2,1,0:T(8,128)(2,1)S(1)}, bf16[34,16,128]{2,1,0:T(8,128)(2,1)S(1)}, u32[]{:S(2)}, u32[]{:S(2)}) %collective-permute-start.2) | collective-permute-done | bytes 139296 | tf_op jit(solution)/shard_map/ppermute | solution.py:629
  9.9 0.0 collective-permute-done.3.got_second
  9.9 0.0 copy-done
  9.9 1.2 %shard_map.70 = s16[16,5,16,128]{3,2,1,0:T(8,128)(2,1)S(1)} custom-call(s32[2]{0:T(128)S(1)} %pad_add_fusion.place.refs_0_, bf16[34,16,128]{2,1,0:T(8,128)(2,1)S(1)} %collective-permute-done.2.got_first, bf16[34,16,128]{2,1,0:T(8,128)(2,1)S(1)} %collective-permute-done.3.got_second, bf16[32,16,128]{2,1,0:T(8,128)(2,1)S(1)} %get-tuple-element.28.part_x, ...), custom_call_target="tpu_custom_call" | custom-call | tf_op jit(solution)/shard_map/pallas_call | solution.py:653
  11.1 26.6 %all_to_all.10.after.refs_1_ = s16[16,5,16,128]{3,2,1,0:T(8,128)(2,1)S(1)} all-to-all(s16[16,5,16,128]{3,2,1,0:T(8,128)(2,1)S(1)} %shard_map.70), channel_id=1, replica_groups=mesh['gx'=8,'gy_chip'=2,'gy_core'=2] {'gx','gy_chip'}, dimensions={0} | all-to-all | bytes 655360 | tf_op jit(solution)/shard_map/all_to_all | solution.py:633
  37.7 0.0 copy-start.1
  37.7 0.0 copy-start.2
  37.7 0.0 collective-permute-start.4
  37.7 1.0 %shard_map.71 = (f32[1040,128]{1,0:T(8,128)S(1)}, f32[1040,128]{1,0:T(8,128)S(1)}, f32[1040,128]{1,0:T(8,128)S(1)}) custom-call(s32[2]{0:T(128)S(1)} %pad_add_fusion.place.refs_0_, s16[16,5,16,128]{3,2,1,0:T(8,128)(2,1)S(1)} %all_to_all.10.after.refs_1_, bf16[34,16,128]{2,1,0:T(8,128)(2,1)S(1)} %collective-permute-done.2.got_first, ...), custom_call_target="tpu_custom_call" | custom-call | flops 4194304 | bytes 4194304 | tf_op jit(solution)/shard_map/pallas_call | solution.py:653
  38.8 0.6 collective-permute-done.4.refs_2_
  39.4 0.0 copy-done.1
  39.4 0.0 copy-done.2
  39.4 5.8 %shard_map.72 = (f32[1040,128]{1,0:T(8,128)S(1)}, s16[16,3,16,128]{3,2,1,0:T(8,128)(2,1)S(1)}, f32[1608,128]{1,0:T(8,128)S(1)}, f32[1608,128]{1,0:T(8,128)S(1)},...) custom-call(s32[2]{0:T(128)S(1)} %pad_add_fusion.place.refs_0_, ...), custom_call_target="tpu_custom_call" | custom-call | tf_op jit(solution)/shard_map/pallas_call | solution.py:653
  45.2 12.2 %all_to_all.11.refs_1_ = s16[16,3,16,128]{3,2,1,0:T(8,128)(2,1)S(1)} all-to-all(s16[16,3,16,128]{3,2,1,0:T(8,128)(2,1)S(1)} %get-tuple-element.34), channel_id=1, replica_groups=mesh['gx'=8,'gy_chip'=2,'gy_core'=2] {'gx','gy_chip'}, dimensions={0} | all-to-all | bytes 393216 | tf_op jit(solution)/shard_map/all_to_all | solution.py:633
  57.5 0.0 collective-permute-start.5
  57.5 1.4 %collective-permute-done.5.refs_2_ = s16[16,3,16,128]{3,2,1,0:T(8,128)(2,1)S(1)} collective-permute-done((s16[16,3,16,128]{3,2,1,0:T(8,128)(2,1)S(1)}, s16[16,3,16,128]{3,2,1,0:T(8,128)(2,1)S(1)}, u32[]{:S(2)}, u32[]{:S(2)}) %collective-permute-start.5) | collective-permute-done | bytes 196640 | tf_op jit(solution)/shard_map/ppermute | solution.py:634
  58.9 5.5 %shard_map.73 = (f32[16,16,128]{2,1,0:T(8,128)}, f32[16,16,128]{2,1,0:T(8,128)}) custom-call(s32[2]{0:T(128)S(1)} %pad_add_fusion.place.refs_0_, s16[16,3,16,128]{3,2,1,0:T(8,128)(2,1)S(1)} %all_to_all.11.refs_1_, s16[16,3,16,128]{3,2,1,0:T(8,128)(2,1)S(1)} %collective-permute-done.5.refs_2_, f32[1040,128]{1,0:T(8,128)S(1)} %get-tuple-element.35.refs_3_, ...), custom_call_target="tpu_custom_call" | custom-call | tf_op jit(solution)/shard_map/pallas_call | solution.py:653
Async XLA Ops:
  2.5 5.3 %collective-permute-start = (bf16[18,16,128]{2,1,0:T(8,128)(2,1)S(1)}, bf16[18,16,128]{2,1,0:T(8,128)(2,1)S(1)}, u32[]{:S(2)}, u32[]{:S(2)}) collective-permute-start(bf16[18,16,128]{2,1,0:T(8,128)(2,1)S(1)} %get-tuple-element.21), channel_id=1, source_target_pairs={{0,4},{4,0},{8,12},{12,8},{16,20},{20,16},{24,28},{28,24},{1,5},{5... | collective-permute-start | bytes 221192 | tf_op jit(solution)/shard_map/ppermute | solution.py:629
  5.5 2.3 %collective-permute-start.1 = (bf16[18,16,128]{2,1,0:T(8,128)(2,1)S(1)}, bf16[18,16,128]{2,1,0:T(8,128)(2,1)S(1)}, u32[]{:S(2)}, u32[]{:S(2)}) collective-permute-start(bf16[18,16,128]{2,1,0:T(8,128)(2,1)S(1)} %get-tuple-element.22), channel_id=1, source_target_pairs={{4,8},{8,4},{12,16},{16,12},{20,24},{24,20},{5,9},{9,5},{13,17},{1... | collective-permute-start | bytes 221192 | tf_op jit(solution)/shard_map/ppermute | solution.py:629
  7.9 2.1 %copy-start = (bf16[256,128]{1,0:T(8,128)(2,1)S(1)}, bf16[256,128]{1,0:T(8,128)(2,1)}, u32[]{:S(2)}) copy-start(bf16[256,128]{1,0:T(8,128)(2,1)} %constant.30.clone.matrix.refs_7_.refs_11_) | copy-start | bytes 196612
  8.5 1.4 %collective-permute-start.2 = (bf16[34,16,128]{2,1,0:T(8,128)(2,1)S(1)}, bf16[34,16,128]{2,1,0:T(8,128)(2,1)S(1)}, u32[]{:S(2)}, u32[]{:S(2)}) collective-permute-start(bf16[34,16,128]{2,1,0:T(8,128)(2,1)S(1)} %get-tuple-element.26), channel_id=1, source_target_pairs={{0,1},{1,0},{2,3},{3,2},{4,5},{5,4},{6,7},{7,6},{8,9},{9,8},{10,11... | collective-permute-start | bytes 417800 | tf_op jit(solution)/shard_map/ppermute | solution.py:629
  8.6 1.3 %collective-permute-start.3 = (bf16[34,16,128]{2,1,0:T(8,128)(2,1)S(1)}, bf16[34,16,128]{2,1,0:T(8,128)(2,1)S(1)}, u32[]{:S(2)}, u32[]{:S(2)}) collective-permute-start(bf16[34,16,128]{2,1,0:T(8,128)(2,1)S(1)} %get-tuple-element.27), channel_id=1, source_target_pairs={{1,2},{2,1},{5,6},{6,5},{9,10},{10,9},{13,14},{14,13},{17,18},{18,... | collective-permute-start | bytes 417800 | tf_op jit(solution)/shard_map/ppermute | solution.py:629
  37.7 1.6 %copy-start.1 = (bf16[512,128]{1,0:T(8,128)(2,1)S(1)}, bf16[512,128]{1,0:T(8,128)(2,1)}, u32[]{:S(2)}) copy-start(bf16[512,128]{1,0:T(8,128)(2,1)} %constant.32.clone.refs_9_.refs_13_) | copy-start | bytes 393220
  37.7 1.6 %copy-start.2 = (bf16[512,128]{1,0:T(8,128)(2,1)S(1)}, bf16[512,128]{1,0:T(8,128)(2,1)}, u32[]{:S(2)}) copy-start(bf16[512,128]{1,0:T(8,128)(2,1)} %constant.31.clone.refs_8_.refs_12_) | copy-start | bytes 393220
  37.7 1.6 %collective-permute-start.4 = (s16[16,5,16,128]{3,2,1,0:T(8,128)(2,1)S(1)}, s16[16,5,16,128]{3,2,1,0:T(8,128)(2,1)S(1)}, u32[]{:S(2)}, u32[]{:S(2)}) collective-permute-start(s16[16,5,16,128]{3,2,1,0:T(8,128)(2,1)S(1)} %all_to_all.10.after.refs_1_), channel_id=1, source_target_pairs={{0,1},{1,0},{2,3},{3,2},{4,5},{5,4},{6,7},{7,6},{8,9},{9,8},{10,11... | collective-permute-start | bytes 983048 | tf_op jit(solution)/shard_map/ppermute | solution.py:634
  57.5 1.4 %collective-permute-start.5 = (s16[16,3,16,128]{3,2,1,0:T(8,128)(2,1)S(1)}, s16[16,3,16,128]{3,2,1,0:T(8,128)(2,1)S(1)}, u32[]{:S(2)}, u32[]{:S(2)}) collective-permute-start(s16[16,3,16,128]{3,2,1,0:T(8,128)(2,1)S(1)} %all_to_all.11.refs_1_), channel_id=1, source_target_pairs={{0,1},{1,0},{2,3},{3,2},{4,5},{5,4},{6,7},{7,6},{8,9},{9,8},{10,11... | collective-permute-start | bytes 589832 | tf_op jit(solution)/shard_map/ppermute | solution.py:634

commit v5 on v4

--- a/solution.py
+++ b/solution.py
@@ -41,20 +41,24 @@
     return jnp.asarray(out, BF16)
 
 
-def two_parts(value):
+def in_parts(value):
     high = value.astype(BF16)
-    return jnp.concatenate([high, (value - high.astype(F32)).astype(BF16)], 0)
+    rest = value - high.astype(F32)
+    middle = rest.astype(BF16)
+    return jnp.concatenate([high, middle, (rest - middle.astype(F32)).astype(BF16)], 0)
+
+
+def add_parts(value, rows):
+    return value[:rows] + (value[rows : 2 * rows] + value[2 * rows :])
 
 
 def gather_lanes(value, matrix):
-    both = jnp.dot(two_parts(value), matrix, preferred_element_type=F32)
-    return both[: value.shape[0]] + both[value.shape[0] :]
+    return add_parts(jnp.dot(in_parts(value), matrix, preferred_element_type=F32), value.shape[0])
 
 
 def spread_lanes(value, matrix):
     dims = (((1,), (1,)), ((), ()))
-    both = lax.dot_general(two_parts(value), matrix, dims, preferred_element_type=F32)
-    return both[: value.shape[0]] + both[value.shape[0] :]
+    return add_parts(lax.dot_general(in_parts(value), matrix, dims, preferred_element_type=F32), value.shape[0])
 
 
 def lane_index():
@@ -357,35 +361,33 @@
 
 
 def conjugate_gradients(target, screen, factor, size_z):
-    iterate = jnp.zeros_like(target)
+    planes, size_y, _ = target.shape
+    least = sum(2.0 - 2.0 * np.cos(np.pi / (n + 1)) for n in (planes * (LANES // size_z), size_y, size_z))
+    longest = 1.001 / (factor * least)
     remain = target
-    search = target
+    image = packed_apply(remain, screen, factor, size_z)
     for step in range(COARSE_ITERS):
-        image = packed_apply(search, screen, factor, size_z)
-        if step + 1 == COARSE_ITERS:
-            norm_now, bent = totals_of(remain * remain, search * image)
-            return iterate + (norm_now / bent) * search
-        norm_now, bent, mixed, norm_image = totals_of(
-            remain * remain, search * image, remain * image, image * image
-        )
-        length = norm_now / bent
-        iterate = iterate + length * search
-        remain = remain - length * image
-        norm_next = norm_now - 2.0 * length * mixed + length * length * norm_image
-        search = remain + (norm_next / norm_now) * search
-
-
-def smooth_packed(iterate, target, screen, inv, factor, size_z):
-    step = (target - packed_apply(iterate, screen, factor, size_z)) * inv * (1.0 / centre)
-    iterate = iterate + step
-    again = (target - packed_apply(iterate, screen, factor, size_z)) * inv
-    return iterate + (keep * step + gain * again)
-
-
-def smooth_packed_zero(target, screen, inv, factor, size_z):
-    step = target * inv * (1.0 / centre)
-    again = (target - packed_apply(step, screen, factor, size_z)) * inv
-    return step + (keep * step + gain * again)
+        more = step + 1 < COARSE_ITERS
+        norm, bent = totals_of(remain * remain, remain * image)
+        if more:
+            ahead = packed_apply(image, screen, factor, size_z)
+        if step == 0:
+            length = norm / bent
+            search, search_image, search_ahead = remain, image, ahead
+            iterate = length * search
+        else:
+            ratio = norm / norm_before
+            length = jnp.clip(norm / (bent - ratio * norm / length), 0.0, longest)
+            search = remain + ratio * search
+            iterate = iterate + length * search
+            if more:
+                search_image = image + ratio * search_image
+                search_ahead = ahead + ratio * search_ahead
+        if more:
+            remain = remain - length * search_image
+            image = image - length * search_ahead
+        norm_before = norm
+    return iterate
 
 
 def add_lanes(rows_ref, planes, size_y, matrix):
@@ -414,7 +416,7 @@
 
 def level_one(place, gathered, sizes, mats, refs, first):
     mat_1, mat_2 = mats
-    given, inverse, diag, step, iterate, rows_ref, level_two, local_a, local_b = refs
+    given, inverse, diag, step, iterate, rows_ref, level_two, local_a, local_b, two_a, two_b = refs
     size_z = LANES // 2
     factor = 0.25
     planes, rows, stride, pad = sizes.planes, sizes.rows, sizes.stride, sizes.pad_x
@@ -490,25 +492,52 @@
         screen_two[...] = 0.125 * add_lanes(rows_ref, planes, rows, mat_1)
     planes_2, rows_2 = planes // 4, rows // 2
     screen = screen_two[...]
-    inv = 1.0 / (6.0 * factor**2 + screen)
+    level = 6.0 * factor**2 + screen
+    inv = 1.0 / level
     if first:
         rows_ref[0 : planes_2 * rows_2] = screen.reshape(-1, LANES)
         screen_three[...] = 0.125 * add_lanes(rows_ref, planes_2, rows_2, mat_2)
-    value = smooth_packed_zero(target, screen, inv, factor**2, LANES // 4)
-    remain = target - packed_apply(value, screen, factor**2, LANES // 4)
-    rows_ref[0 : planes_2 * rows_2] = remain.reshape(-1, LANES)
+    stride_2 = rows_2 + 8
+
+    def at_2(i):
+        return (1 + i) * stride_2 + 8
+
+    for ref in (two_a, two_b):
+        for start, count in ((0, stride_2 + 8), ((planes_2 + 1) * stride_2, stride_2 + 8)):
+            ref[start : start + count] = jnp.zeros((count, LANES), F32)
+        for i in range(planes_2):
+            ref[at_2(i) - 8 : at_2(i)] = jnp.zeros((8, LANES), F32)
+
+    def fit_two(ref, i):
+        here, total = neighbours(ref, at_2(i), rows_2, stride_2, LANES // 4)
+        return here, (target[i] + factor**2 * total) * inv[i]
+
+    for i in range(planes_2):
+        two_a[pl.ds(at_2(i), rows_2), :] = target[i] * inv[i] * (1.0 / centre)
+    for i in range(planes_2):
+        here, fit = fit_two(two_a, i)
+        two_b[pl.ds(at_2(i), rows_2), :] = here + (keep * here + gain * (fit - here))
+    for i in range(planes_2):
+        here, total = neighbours(two_b, at_2(i), rows_2, stride_2, LANES // 4)
+        rows_ref[i * rows_2 : (i + 1) * rows_2] = target[i] + factor**2 * total - level[i] * here
     target_3 = 0.125 * add_lanes(rows_ref, planes_2, rows_2, mat_2)
     error = conjugate_gradients(target_3, screen_three[...], factor**3, LANES // 8)
     error = copy_level(error, mat_2).reshape(-1, LANES)
     count = planes_2 * rows_2
     rows_ref[pl.ds(0, count // 2, stride=2), :] = error
     rows_ref[pl.ds(1, count // 2, stride=2), :] = error
-    value = value + rows_ref[0:count].reshape(value.shape)
-    value = smooth_packed(value, target, screen, inv, factor**2, LANES // 4)
+    for i in range(planes_2):
+        two_a[pl.ds(at_2(i), rows_2), :] = two_b[pl.ds(at_2(i), rows_2), :] + rows_ref[i * rows_2 : (i + 1) * rows_2]
+    for i in range(planes_2):
+        here, fit = fit_two(two_a, i)
+        two_b[pl.ds(at_2(i), rows_2), :] = here + (fit - here) * (1.0 / centre)
 
     rows_ref[0:rows_2] = jnp.zeros((rows_2, LANES), F32)
     rows_ref[(planes_2 + 1) * rows_2 : (planes_2 + 2) * rows_2] = jnp.zeros((rows_2, LANES), F32)
-    rows_ref[rows_2 : (planes_2 + 1) * rows_2] = value.reshape(-1, LANES)
+    for i in range(planes_2):
+        here, fit = fit_two(two_b, i)
+        before = two_a[pl.ds(at_2(i), rows_2), :]
+        rows_ref[(i + 1) * rows_2 : (i + 2) * rows_2] = here + (keep * (here - before) + gain * (fit - here))
     near_2 = own_x // 4 + 2
     start = pl.multiple_of(place[0] * (own_x // 4) * rows_2, 8)
     near = rows_ref[pl.ds(start, near_2 * rows_2), :].reshape(near_2, rows_2, LANES)
@@ -565,11 +594,11 @@
 
 def middle_kernel(sizes, place, near, far, start, field, scaled, count_x, mat_0, mat_1, mat_2, *rest):
     iterate, packet, inverse, diag, screen_two, screen_three = rest[:6]
-    given, step, coarse, rows_ref, local_a, local_b, other, fine_rows = rest[6:]
+    given, step, coarse, rows_ref, local_a, local_b, two_a, two_b, other, fine_rows = rest[6:]
     wide, size_y = count_x.shape[:2]
     size_x = wide - 2 * HALO
     plane = size_y + 2 * HALO
-    refs = (given, inverse, diag, step, coarse, rows_ref, (screen_two, screen_three), local_a, local_b)
+    refs = (given, inverse, diag, step, coarse, rows_ref, (screen_two, screen_three), local_a, local_b, two_a, two_b)
     level_one(place, (near, far), sizes, (mat_1, mat_2), refs, True)
     add_correction(start, iterate, local_a, sizes, mat_0, plane)
     finest_step_one(iterate, other, field, scaled, 6, wide, plane)
@@ -587,11 +616,12 @@
 
 def last_kernel(sizes, place, near, far, start, field, scaled, count_x, inverse, diag, screen_two, screen_three, *rest):
     mat_0, mat_1, mat_2, solution_far, residual_far = rest[:5]
-    given, step, coarse, rows_ref, local_a, local_b, iterate, other, solution_out, residual_out, left = rest[5:]
+    given, step, coarse, rows_ref, local_a, local_b, two_a, two_b, iterate, other = rest[5:15]
+    solution_out, residual_out, left = rest[15:]
     wide, size_y = count_x.shape[:2]
     size_x = wide - 2 * HALO
     plane = size_y + 2 * HALO
-    refs = (given, inverse, diag, step, coarse, rows_ref, (screen_two, screen_three), local_a, local_b)
+    refs = (given, inverse, diag, step, coarse, rows_ref, (screen_two, screen_three), local_a, local_b, two_a, two_b)
     level_one(place, (near, far), sizes, (mat_1, mat_2), refs, False)
     add_correction(start, iterate, local_a, sizes, mat_0, plane)
     finest_step_one(iterate, other, field, scaled, 2, wide, plane)
@@ -707,6 +737,7 @@
         cost=pl.CostEstimate(flops=1 << 22, bytes_accessed=4 << 20, transcendentals=0),
     )
     level = (sizes.flat, LANES)
+    flat_two = ((sizes.planes // 4 + 2) * (sizes.rows // 2 + 8) + 8, LANES)
     around = (16 + (own + 8) * (sizes.own_y + 16), LANES)
     scratch = [
         (level, F32),
@@ -715,6 +746,8 @@
         ((sizes.planes * sizes.rows, LANES), F32),
         (around, F32),
         (around, F32),
+        (flat_two, F32),
+        (flat_two, F32),
         ((flat, LANES), F32),
     ]
     level_two = (sizes.planes // 4, sizes.rows // 2, LANES)

time: 64.6 us -> 64 us (level)
  no operation moved by 1% of the time
where the time goes in v5:
time: 64 us; the launch traced here: 63.8 us
  blocking collectives  38.8 us (61%)
  Pallas kernels  14.3 us (22%)
  starting transfers between devices  4.41 us (7%)
  waiting for transfers between devices  4.36 us (7%)
  other arithmetic  1.21 us (2%)
  between operations  0.7 us (1%)
    all_to_all x2, blocking collectives, gather(): near = lax.all_to_all(packet, ('gx', 'gy_chip'), 0, 0, tiled=True)  38.8 us
    pallas_call x6, Pallas kernels, call(): pl.pallas_call(kernel, out_shape=[jax.ShapeDtypeStruct(shape, dtype) for...  14.3 us
    ppermute x2, starting transfers between devices, exchange(): lax.ppermute(first, axis, pairs(0))  3.08 us
    ppermute x2, waiting for transfers between devices, exchange(): lax.ppermute(first, axis, pairs(0))  2.34 us
    ppermute x2, waiting for transfers between devices, gather(): return (near, lax.ppermute(near, 'gy_core', [(0, 1), (1, 0)]))  2.02 us
    ppermute x2, starting transfers between devices, exchange(): lax.ppermute(second, axis, pairs(1))  1.32 us
  transfers between devices with their start and end apart: 6, of which 4 were waited for; matrix products, arithmetic and copies ran while one was open for 0% of the time, Pallas kernels for 2%

profile of v5, /device:TPU:0, one launch (start us, length us, event | category | flops | bytes accessed | tf_op | source)
XLA Modules:
  0.0 63.8 jit_solution(10890780181452082133)
XLA Ops:
  0.6 0.1 pad_add_fusion.place.refs_0_
  0.7 1.1 %bitcast_add_fusion.words = s32[16,16,128]{2,1,0:T(8,128)S(1)} fusion(s32[3,16,16,128]{3,2,1,0:T(8,128)} %param.6, s32[16,16,128]{2,1,0:T(8,128)} %param.5), kind=kLoop, calls=%fused_computation | loop fusion | flops 327680 | bytes 655360 | tf_op jit(solution)/shard_map/add | solution.py:115
  1.9 0.7 %shard_map.68 = (bf16[18,16,128]{2,1,0:T(8,128)(2,1)S(1)}, bf16[18,16,128]{2,1,0:T(8,128)(2,1)S(1)}, bf16[16,16,128]{2,1,0:T(8,128)(2,1)S(1)}, bf16[16,16,128]{2,1,0:T(8,128)(2,1)S(1)}, bf16[2,16,128]{2,1,0:T(8,128)(2,1)S(1)}) custom-call(s32[2]{0:T(128)S(1)} %pad_add_fusion.place.refs_0_, s32[16,16,128]{2,1,0:T(8,128)S(1)} %bitcast_add_fusion.words), custom_call_target="tpu_custom_call" | custom-call | tf_op jit(solution)/shard_map/pallas_call | solution.py:683
  2.5 3.0 %collective-permute-start = (bf16[18,16,128]{2,1,0:T(8,128)(2,1)S(1)}, bf16[18,16,128]{2,1,0:T(8,128)(2,1)S(1)}, u32[]{:S(2)}, u32[]{:S(2)}) collective-permute-start(bf16[18,16,128]{2,1,0:T(8,128)(2,1)S(1)} %get-tuple-element.21), channel_id=1, source_target_pairs={{0,4},{4,0},{8,12},{12,8},{16,20},{20,16},{24,28},{28,24},{1,5},{5... | collective-permute-start | bytes 221192 | tf_op jit(solution)/shard_map/ppermute | solution.py:659
  5.5 0.7 %collective-permute-start.1 = (bf16[18,16,128]{2,1,0:T(8,128)(2,1)S(1)}, bf16[18,16,128]{2,1,0:T(8,128)(2,1)S(1)}, u32[]{:S(2)}, u32[]{:S(2)}) collective-permute-start(bf16[18,16,128]{2,1,0:T(8,128)(2,1)S(1)} %get-tuple-element.22), channel_id=1, source_target_pairs={{4,8},{8,4},{12,16},{16,12},{20,24},{24,20},{5,9},{9,5},{13,17},{1... | collective-permute-start | bytes 221192 | tf_op jit(solution)/shard_map/ppermute | solution.py:659
  6.2 1.7 %collective-permute-done.got_first = bf16[18,16,128]{2,1,0:T(8,128)(2,1)S(1)} collective-permute-done((bf16[18,16,128]{2,1,0:T(8,128)(2,1)S(1)}, bf16[18,16,128]{2,1,0:T(8,128)(2,1)S(1)}, u32[]{:S(2)}, u32[]{:S(2)}) %collective-permute-start) | collective-permute-done | bytes 73760 | tf_op jit(solution)/shard_map/ppermute | solution.py:659
  7.9 0.0 collective-permute-done.1.got_second
  7.9 0.0 copy-start
  7.9 0.6 shard_map.69
  8.5 0.1 collective-permute-start.2
  8.6 0.7 %collective-permute-start.3 = (bf16[34,16,128]{2,1,0:T(8,128)(2,1)S(1)}, bf16[34,16,128]{2,1,0:T(8,128)(2,1)S(1)}, u32[]{:S(2)}, u32[]{:S(2)}) collective-permute-start(bf16[34,16,128]{2,1,0:T(8,128)(2,1)S(1)} %get-tuple-element.27), channel_id=1, source_target_pairs={{1,2},{2,1},{5,6},{6,5},{9,10},{10,9},{13,14},{14,13},{17,18},{18,... | collective-permute-start | bytes 417800 | tf_op jit(solution)/shard_map/ppermute | solution.py:659
  9.3 0.7 %collective-permute-done.2.got_first = bf16[34,16,128]{2,1,0:T(8,128)(2,1)S(1)} collective-permute-done((bf16[34,16,128]{2,1,0:T(8,128)(2,1)S(1)}, bf16[34,16,128]{2,1,0:T(8,128)(2,1)S(1)}, u32[]{:S(2)}, u32[]{:S(2)}) %collective-permute-start.2) | collective-permute-done | bytes 139296 | tf_op jit(solution)/shard_map/ppermute | solution.py:659
  9.9 0.0 collective-permute-done.3.got_second
  9.9 0.0 copy-done
  9.9 1.2 %shard_map.70 = s16[16,5,16,128]{3,2,1,0:T(8,128)(2,1)S(1)} custom-call(s32[2]{0:T(128)S(1)} %pad_add_fusion.place.refs_0_, bf16[34,16,128]{2,1,0:T(8,128)(2,1)S(1)} %collective-permute-done.2.got_first, bf16[34,16,128]{2,1,0:T(8,128)(2,1)S(1)} %collective-permute-done.3.got_second, bf16[32,16,128]{2,1,0:T(8,128)(2,1)S(1)} %get-tuple-element.28.part_x, ...), custom_call_target="tpu_custom_call" | custom-call | tf_op jit(solution)/shard_map/pallas_call | solution.py:683
  11.2 26.6 %all_to_all.10.after.refs_1_ = s16[16,5,16,128]{3,2,1,0:T(8,128)(2,1)S(1)} all-to-all(s16[16,5,16,128]{3,2,1,0:T(8,128)(2,1)S(1)} %shard_map.70), channel_id=1, replica_groups=mesh['gx'=8,'gy_chip'=2,'gy_core'=2] {'gx','gy_chip'}, dimensions={0} | all-to-all | bytes 655360 | tf_op jit(solution)/shard_map/all_to_all | solution.py:663
  37.7 0.0 copy-start.1
  37.7 0.0 copy-start.2
  37.7 0.0 collective-permute-start.4
  37.7 1.0 %shard_map.71 = (f32[1040,128]{1,0:T(8,128)S(1)}, f32[1040,128]{1,0:T(8,128)S(1)}, f32[1040,128]{1,0:T(8,128)S(1)}) custom-call(s32[2]{0:T(128)S(1)} %pad_add_fusion.place.refs_0_, s16[16,5,16,128]{3,2,1,0:T(8,128)(2,1)S(1)} %all_to_all.10.after.refs_1_, bf16[34,16,128]{2,1,0:T(8,128)(2,1)S(1)} %collective-permute-done.2.got_first, ...), custom_call_target="tpu_custom_call" | custom-call | flops 4194304 | bytes 4194304 | tf_op jit(solution)/shard_map/pallas_call | solution.py:683
  38.8 0.6 collective-permute-done.4.refs_2_
  39.4 0.0 copy-done.1
  39.4 0.0 copy-done.2
  39.4 5.6 %shard_map.72 = (f32[1040,128]{1,0:T(8,128)S(1)}, s16[16,3,16,128]{3,2,1,0:T(8,128)(2,1)S(1)}, f32[1608,128]{1,0:T(8,128)S(1)}, f32[1608,128]{1,0:T(8,128)S(1)},...) custom-call(s32[2]{0:T(128)S(1)} %pad_add_fusion.place.refs_0_, ...), custom_call_target="tpu_custom_call" | custom-call | tf_op jit(solution)/shard_map/pallas_call | solution.py:683
  44.9 12.3 %all_to_all.11.refs_1_ = s16[16,3,16,128]{3,2,1,0:T(8,128)(2,1)S(1)} all-to-all(s16[16,3,16,128]{3,2,1,0:T(8,128)(2,1)S(1)} %get-tuple-element.34), channel_id=1, replica_groups=mesh['gx'=8,'gy_chip'=2,'gy_core'=2] {'gx','gy_chip'}, dimensions={0} | all-to-all | bytes 393216 | tf_op jit(solution)/shard_map/all_to_all | solution.py:663
  57.2 0.0 collective-permute-start.5
  57.2 1.4 %collective-permute-done.5.refs_2_ = s16[16,3,16,128]{3,2,1,0:T(8,128)(2,1)S(1)} collective-permute-done((s16[16,3,16,128]{3,2,1,0:T(8,128)(2,1)S(1)}, s16[16,3,16,128]{3,2,1,0:T(8,128)(2,1)S(1)}, u32[]{:S(2)}, u32[]{:S(2)}) %collective-permute-start.5) | collective-permute-done | bytes 196640 | tf_op jit(solution)/shard_map/ppermute | solution.py:664
  58.6 5.2 %shard_map.73 = (f32[16,16,128]{2,1,0:T(8,128)}, f32[16,16,128]{2,1,0:T(8,128)}) custom-call(s32[2]{0:T(128)S(1)} %pad_add_fusion.place.refs_0_, s16[16,3,16,128]{3,2,1,0:T(8,128)(2,1)S(1)} %all_to_all.11.refs_1_, s16[16,3,16,128]{3,2,1,0:T(8,128)(2,1)S(1)} %collective-permute-done.5.refs_2_, f32[1040,128]{1,0:T(8,128)S(1)} %get-tuple-element.35.refs_3_, ...), custom_call_target="tpu_custom_call" | custom-call | tf_op jit(solution)/shard_map/pallas_call | solution.py:683
Async XLA Ops:
  2.5 5.3 %collective-permute-start = (bf16[18,16,128]{2,1,0:T(8,128)(2,1)S(1)}, bf16[18,16,128]{2,1,0:T(8,128)(2,1)S(1)}, u32[]{:S(2)}, u32[]{:S(2)}) collective-permute-start(bf16[18,16,128]{2,1,0:T(8,128)(2,1)S(1)} %get-tuple-element.21), channel_id=1, source_target_pairs={{0,4},{4,0},{8,12},{12,8},{16,20},{20,16},{24,28},{28,24},{1,5},{5... | collective-permute-start | bytes 221192 | tf_op jit(solution)/shard_map/ppermute | solution.py:659
  5.5 2.3 %collective-permute-start.1 = (bf16[18,16,128]{2,1,0:T(8,128)(2,1)S(1)}, bf16[18,16,128]{2,1,0:T(8,128)(2,1)S(1)}, u32[]{:S(2)}, u32[]{:S(2)}) collective-permute-start(bf16[18,16,128]{2,1,0:T(8,128)(2,1)S(1)} %get-tuple-element.22), channel_id=1, source_target_pairs={{4,8},{8,4},{12,16},{16,12},{20,24},{24,20},{5,9},{9,5},{13,17},{1... | collective-permute-start | bytes 221192 | tf_op jit(solution)/shard_map/ppermute | solution.py:659
  7.9 2.1 %copy-start = (bf16[256,128]{1,0:T(8,128)(2,1)S(1)}, bf16[256,128]{1,0:T(8,128)(2,1)}, u32[]{:S(2)}) copy-start(bf16[256,128]{1,0:T(8,128)(2,1)} %constant.30.clone.matrix.refs_7_.refs_11_) | copy-start | bytes 196612
  8.5 1.4 %collective-permute-start.2 = (bf16[34,16,128]{2,1,0:T(8,128)(2,1)S(1)}, bf16[34,16,128]{2,1,0:T(8,128)(2,1)S(1)}, u32[]{:S(2)}, u32[]{:S(2)}) collective-permute-start(bf16[34,16,128]{2,1,0:T(8,128)(2,1)S(1)} %get-tuple-element.26), channel_id=1, source_target_pairs={{0,1},{1,0},{2,3},{3,2},{4,5},{5,4},{6,7},{7,6},{8,9},{9,8},{10,11... | collective-permute-start | bytes 417800 | tf_op jit(solution)/shard_map/ppermute | solution.py:659
  8.6 1.3 %collective-permute-start.3 = (bf16[34,16,128]{2,1,0:T(8,128)(2,1)S(1)}, bf16[34,16,128]{2,1,0:T(8,128)(2,1)S(1)}, u32[]{:S(2)}, u32[]{:S(2)}) collective-permute-start(bf16[34,16,128]{2,1,0:T(8,128)(2,1)S(1)} %get-tuple-element.27), channel_id=1, source_target_pairs={{1,2},{2,1},{5,6},{6,5},{9,10},{10,9},{13,14},{14,13},{17,18},{18,... | collective-permute-start | bytes 417800 | tf_op jit(solution)/shard_map/ppermute | solution.py:659
  37.7 1.6 %copy-start.1 = (bf16[512,128]{1,0:T(8,128)(2,1)S(1)}, bf16[512,128]{1,0:T(8,128)(2,1)}, u32[]{:S(2)}) copy-start(bf16[512,128]{1,0:T(8,128)(2,1)} %constant.32.clone.refs_9_.refs_13_) | copy-start | bytes 393220
  37.7 1.6 %copy-start.2 = (bf16[512,128]{1,0:T(8,128)(2,1)S(1)}, bf16[512,128]{1,0:T(8,128)(2,1)}, u32[]{:S(2)}) copy-start(bf16[512,128]{1,0:T(8,128)(2,1)} %constant.31.clone.refs_8_.refs_12_) | copy-start | bytes 393220
  37.7 1.6 %collective-permute-start.4 = (s16[16,5,16,128]{3,2,1,0:T(8,128)(2,1)S(1)}, s16[16,5,16,128]{3,2,1,0:T(8,128)(2,1)S(1)}, u32[]{:S(2)}, u32[]{:S(2)}) collective-permute-start(s16[16,5,16,128]{3,2,1,0:T(8,128)(2,1)S(1)} %all_to_all.10.after.refs_1_), channel_id=1, source_target_pairs={{0,1},{1,0},{2,3},{3,2},{4,5},{5,4},{6,7},{7,6},{8,9},{9,8},{10,11... | collective-permute-start | bytes 983048 | tf_op jit(solution)/shard_map/ppermute | solution.py:664
  57.2 1.4 %collective-permute-start.5 = (s16[16,3,16,128]{3,2,1,0:T(8,128)(2,1)S(1)}, s16[16,3,16,128]{3,2,1,0:T(8,128)(2,1)S(1)}, u32[]{:S(2)}, u32[]{:S(2)}) collective-permute-start(s16[16,3,16,128]{3,2,1,0:T(8,128)(2,1)S(1)} %all_to_all.11.refs_1_), channel_id=1, source_target_pairs={{0,1},{1,0},{2,3},{3,2},{4,5},{5,4},{6,7},{7,6},{8,9},{9,8},{10,11... | collective-permute-start | bytes 589832 | tf_op jit(solution)/shard_map/ppermute | solution.py:664

commit v6 on v5

--- a/solution.py
+++ b/solution.py
@@ -140,7 +140,7 @@
             target[HALO : 2 * HALO] = count[start : start + HALO]
             target[2 * HALO : 2 * HALO + 2] = edge[...]
 
-    odd = place[0] % 2
+    odd = 1 - place[0] % 2
 
     @pl.when(odd == 0)
     def _():
@@ -168,7 +168,7 @@
         edge_x[HALO : HALO + size_x] = edge[1].astype(F32)
         edge_x[HALO + size_x :] = above[2 * HALO + 1].astype(F32)[:HALO]
 
-    odd = place[0] % 2
+    odd = 1 - place[0] % 2
 
     @pl.when(odd == 0)
     def _():
@@ -188,7 +188,7 @@
             for j in range(wide // size_y):
                 target[wide + j] = edge_x[j * size_y : (j + 1) * size_y].astype(BF16)
 
-    odd_y = place[1] % 2
+    odd_y = 1 - place[1] % 2
 
     @pl.when(odd_y == 0)
     def _():
@@ -249,7 +249,7 @@
 def first_step(place, got, part_x, count_x, edge_x, iterate, field, inverse, margin):
     wide, size_y = part_x.shape[:2]
     plane = size_y + 2 * HALO
-    even = place[1] % 2 == 0
+    even = place[1] % 2 == 1
     top = lax.broadcasted_iota(jnp.int32, (HALO, LANES), 0) == 0
     under_rows = [jnp.where(even, got[1][wide + j], got[0][wide + j]).astype(F32) for j in range(wide // size_y)]
     for i in range(HALO - margin, wide - HALO + margin):
@@ -656,7 +656,7 @@
             found += [(i, i + 1), (i + 1, i)]
         return found
 
-    return lax.ppermute(first, axis, pairs(0)), lax.ppermute(second, axis, pairs(1))
+    return lax.ppermute(first, axis, pairs(1)), lax.ppermute(second, axis, pairs(0))
 
 
 def gather(packet):

time: 64 us -> 63.1 us (0.986)
  blocking collectives: 38.8 us -> 31.2 us
  starting transfers between devices: 4.41 us -> 10.1 us
  waiting for transfers between devices: 4.36 us -> 5.38 us
    all_to_all x2, blocking collectives: 38.8 us -> 31.2 us  [gather(): near = lax.all_to_all(packet, ('gx', 'gy_chip'), 0, 0, tiled=True)]
    ppermute x4, starting transfers between devices: 4.4 us -> 10.1 us  [the longest x2 8.73 us: exchange(): lax.ppermute(second, axis, pairs(0))]
    ppermute x4, waiting for transfers between devices: 2.35 us -> 3.36 us  [the longest x2 3.36 us: exchange(): lax.ppermute(second, axis, pairs(0))]
where the time goes in v6:
time: 63.1 us; the launch traced here: 62.8 us
  blocking collectives  31.2 us (49%)
  Pallas kernels  14.3 us (23%)
  starting transfers between devices  10.1 us (16%)
  waiting for transfers between devices  5.38 us (9%)
  other arithmetic  1.21 us (2%)
  between operations  0.7 us (1%)
    all_to_all x2, blocking collectives, gather(): near = lax.all_to_all(packet, ('gx', 'gy_chip'), 0, 0, tiled=True)  31.2 us
    pallas_call x6, Pallas kernels, call(): pl.pallas_call(kernel, out_shape=[jax.ShapeDtypeStruct(shape, dtype) for...  14.3 us
    ppermute x2, starting transfers between devices, exchange(): lax.ppermute(second, axis, pairs(0))  8.73 us
    ppermute x2, waiting for transfers between devices, exchange(): lax.ppermute(second, axis, pairs(0))  3.36 us
    ppermute x2, waiting for transfers between devices, gather(): return (near, lax.ppermute(near, 'gy_core', [(0, 1), (1, 0)]))  2.02 us
    ppermute x2, starting transfers between devices, exchange(): lax.ppermute(first, axis, pairs(1))  1.33 us
  transfers between devices with their start and end apart: 6, of which 4 were waited for; matrix products, arithmetic and copies ran while one was open for 0% of the time, Pallas kernels for 2%

profile of v6, /device:TPU:0, one launch (start us, length us, event | category | flops | bytes accessed | tf_op | source)
XLA Modules:
  0.0 62.8 jit_solution(9411166312817792889)
XLA Ops:
  0.6 0.1 pad_add_fusion.place.refs_0_
  0.7 1.1 %bitcast_add_fusion.words = s32[16,16,128]{2,1,0:T(8,128)S(1)} fusion(s32[3,16,16,128]{3,2,1,0:T(8,128)} %param.6, s32[16,16,128]{2,1,0:T(8,128)} %param.5), kind=kLoop, calls=%fused_computation | loop fusion | flops 327680 | bytes 655360 | tf_op jit(solution)/shard_map/add | solution.py:115
  1.9 0.7 %shard_map.68 = (bf16[18,16,128]{2,1,0:T(8,128)(2,1)S(1)}, bf16[18,16,128]{2,1,0:T(8,128)(2,1)S(1)}, bf16[16,16,128]{2,1,0:T(8,128)(2,1)S(1)}, bf16[16,16,128]{2,1,0:T(8,128)(2,1)S(1)}, bf16[2,16,128]{2,1,0:T(8,128)(2,1)S(1)}) custom-call(s32[2]{0:T(128)S(1)} %pad_add_fusion.place.refs_0_, s32[16,16,128]{2,1,0:T(8,128)S(1)} %bitcast_add_fusion.words), custom_call_target="tpu_custom_call" | custom-call | tf_op jit(solution)/shard_map/pallas_call | solution.py:683
  2.5 0.7 %collective-permute-start = (bf16[18,16,128]{2,1,0:T(8,128)(2,1)S(1)}, bf16[18,16,128]{2,1,0:T(8,128)(2,1)S(1)}, u32[]{:S(2)}, u32[]{:S(2)}) collective-permute-start(bf16[18,16,128]{2,1,0:T(8,128)(2,1)S(1)} %get-tuple-element.21), channel_id=1, source_target_pairs={{4,8},{8,4},{12,16},{16,12},{20,24},{24,20},{5,9},{9,5},{13,17},{1... | collective-permute-start | bytes 221192 | tf_op jit(solution)/shard_map/ppermute | solution.py:659
  3.2 5.8 %collective-permute-start.1 = (bf16[18,16,128]{2,1,0:T(8,128)(2,1)S(1)}, bf16[18,16,128]{2,1,0:T(8,128)(2,1)S(1)}, u32[]{:S(2)}, u32[]{:S(2)}) collective-permute-start(bf16[18,16,128]{2,1,0:T(8,128)(2,1)S(1)} %get-tuple-element.22), channel_id=1, source_target_pairs={{0,4},{4,0},{8,12},{12,8},{16,20},{20,16},{24,28},{28,24},{1,5},{5... | collective-permute-start | bytes 221192 | tf_op jit(solution)/shard_map/ppermute | solution.py:659
  9.0 0.0 collective-permute-done.got_first
  9.0 2.4 %collective-permute-done.1.got_second = bf16[18,16,128]{2,1,0:T(8,128)(2,1)S(1)} collective-permute-done((bf16[18,16,128]{2,1,0:T(8,128)(2,1)S(1)}, bf16[18,16,128]{2,1,0:T(8,128)(2,1)S(1)}, u32[]{:S(2)}, u32[]{:S(2)}) %collective-permute-start.1) | collective-permute-done | bytes 73760 | tf_op jit(solution)/shard_map/ppermute | solution.py:659
  11.4 0.0 copy-start
  11.4 0.6 %shard_map.69 = (bf16[34,16,128]{2,1,0:T(8,128)(2,1)S(1)}, bf16[34,16,128]{2,1,0:T(8,128)(2,1)S(1)}, bf16[32,16,128]{2,1,0:T(8,128)(2,1)S(1)}, bf16[32,16,128]{2,1,0:T(8,128)(2,1)S(1)}, f32[32,128]{1,0:T(8,128)S(1)}) custom-call(s32[2]{0:T(128)S(1)} %pad_add_fusion.place.refs_0_, bf16[18,16,128]{2,1,0:T(8,128)(2,1)S(1)} %collective-permute-done.got_first, ...), custom_call_target="tpu_custom_call" | custom-call | tf_op jit(solution)/shard_map/pallas_call | solution.py:683
  12.0 0.7 %collective-permute-start.2 = (bf16[34,16,128]{2,1,0:T(8,128)(2,1)S(1)}, bf16[34,16,128]{2,1,0:T(8,128)(2,1)S(1)}, u32[]{:S(2)}, u32[]{:S(2)}) collective-permute-start(bf16[34,16,128]{2,1,0:T(8,128)(2,1)S(1)} %get-tuple-element.26), channel_id=1, source_target_pairs={{1,2},{2,1},{5,6},{6,5},{9,10},{10,9},{13,14},{14,13},{17,18},{18,... | collective-permute-start | bytes 417800 | tf_op jit(solution)/shard_map/ppermute | solution.py:659
  12.7 2.9 %collective-permute-start.3 = (bf16[34,16,128]{2,1,0:T(8,128)(2,1)S(1)}, bf16[34,16,128]{2,1,0:T(8,128)(2,1)S(1)}, u32[]{:S(2)}, u32[]{:S(2)}) collective-permute-start(bf16[34,16,128]{2,1,0:T(8,128)(2,1)S(1)} %get-tuple-element.27), channel_id=1, source_target_pairs={{0,1},{1,0},{2,3},{3,2},{4,5},{5,4},{6,7},{7,6},{8,9},{9,8},{10,11... | collective-permute-start | bytes 417800 | tf_op jit(solution)/shard_map/ppermute | solution.py:659
  15.6 0.0 collective-permute-done.2.got_first
  15.6 1.0 %collective-permute-done.3.got_second = bf16[34,16,128]{2,1,0:T(8,128)(2,1)S(1)} collective-permute-done((bf16[34,16,128]{2,1,0:T(8,128)(2,1)S(1)}, bf16[34,16,128]{2,1,0:T(8,128)(2,1)S(1)}, u32[]{:S(2)}, u32[]{:S(2)}) %collective-permute-start.3) | collective-permute-done | bytes 139296 | tf_op jit(solution)/shard_map/ppermute | solution.py:659
  16.6 0.0 copy-done
  16.6 1.2 %shard_map.70 = s16[16,5,16,128]{3,2,1,0:T(8,128)(2,1)S(1)} custom-call(s32[2]{0:T(128)S(1)} %pad_add_fusion.place.refs_0_, bf16[34,16,128]{2,1,0:T(8,128)(2,1)S(1)} %collective-permute-done.2.got_first, bf16[34,16,128]{2,1,0:T(8,128)(2,1)S(1)} %collective-permute-done.3.got_second, bf16[32,16,128]{2,1,0:T(8,128)(2,1)S(1)} %get-tuple-element.28.part_x, ...), custom_call_target="tpu_custom_call" | custom-call | tf_op jit(solution)/shard_map/pallas_call | solution.py:683
  17.8 18.9 %all_to_all.10.after.refs_1_ = s16[16,5,16,128]{3,2,1,0:T(8,128)(2,1)S(1)} all-to-all(s16[16,5,16,128]{3,2,1,0:T(8,128)(2,1)S(1)} %shard_map.70), channel_id=1, replica_groups=mesh['gx'=8,'gy_chip'=2,'gy_core'=2] {'gx','gy_chip'}, dimensions={0} | all-to-all | bytes 655360 | tf_op jit(solution)/shard_map/all_to_all | solution.py:663
  36.8 0.0 copy-start.1
  36.8 0.0 copy-start.2
  36.8 0.0 collective-permute-start.4
  36.8 1.0 %shard_map.71 = (f32[1040,128]{1,0:T(8,128)S(1)}, f32[1040,128]{1,0:T(8,128)S(1)}, f32[1040,128]{1,0:T(8,128)S(1)}) custom-call(s32[2]{0:T(128)S(1)} %pad_add_fusion.place.refs_0_, s16[16,5,16,128]{3,2,1,0:T(8,128)(2,1)S(1)} %all_to_all.10.after.refs_1_, bf16[34,16,128]{2,1,0:T(8,128)(2,1)S(1)} %collective-permute-done.2.got_first, ...), custom_call_target="tpu_custom_call" | custom-call | flops 4194304 | bytes 4194304 | tf_op jit(solution)/shard_map/pallas_call | solution.py:683
  37.8 0.6 collective-permute-done.4.refs_2_
  38.4 0.0 copy-done.1
  38.4 0.0 copy-done.2
  38.4 5.6 %shard_map.72 = (f32[1040,128]{1,0:T(8,128)S(1)}, s16[16,3,16,128]{3,2,1,0:T(8,128)(2,1)S(1)}, f32[1608,128]{1,0:T(8,128)S(1)}, f32[1608,128]{1,0:T(8,128)S(1)},...) custom-call(s32[2]{0:T(128)S(1)} %pad_add_fusion.place.refs_0_, ...), custom_call_target="tpu_custom_call" | custom-call | tf_op jit(solution)/shard_map/pallas_call | solution.py:683
  44.0 12.3 %all_to_all.11.refs_1_ = s16[16,3,16,128]{3,2,1,0:T(8,128)(2,1)S(1)} all-to-all(s16[16,3,16,128]{3,2,1,0:T(8,128)(2,1)S(1)} %get-tuple-element.34), channel_id=1, replica_groups=mesh['gx'=8,'gy_chip'=2,'gy_core'=2] {'gx','gy_chip'}, dimensions={0} | all-to-all | bytes 393216 | tf_op jit(solution)/shard_map/all_to_all | solution.py:663
  56.2 0.0 collective-permute-start.5
  56.2 1.4 %collective-permute-done.5.refs_2_ = s16[16,3,16,128]{3,2,1,0:T(8,128)(2,1)S(1)} collective-permute-done((s16[16,3,16,128]{3,2,1,0:T(8,128)(2,1)S(1)}, s16[16,3,16,128]{3,2,1,0:T(8,128)(2,1)S(1)}, u32[]{:S(2)}, u32[]{:S(2)}) %collective-permute-start.5) | collective-permute-done | bytes 196640 | tf_op jit(solution)/shard_map/ppermute | solution.py:664
  57.7 5.2 %shard_map.73 = (f32[16,16,128]{2,1,0:T(8,128)}, f32[16,16,128]{2,1,0:T(8,128)}) custom-call(s32[2]{0:T(128)S(1)} %pad_add_fusion.place.refs_0_, s16[16,3,16,128]{3,2,1,0:T(8,128)(2,1)S(1)} %all_to_all.11.refs_1_, s16[16,3,16,128]{3,2,1,0:T(8,128)(2,1)S(1)} %collective-permute-done.5.refs_2_, f32[1040,128]{1,0:T(8,128)S(1)} %get-tuple-element.35.refs_3_, ...), custom_call_target="tpu_custom_call" | custom-call | tf_op jit(solution)/shard_map/pallas_call | solution.py:683
Async XLA Ops:
  2.5 6.5 %collective-permute-start = (bf16[18,16,128]{2,1,0:T(8,128)(2,1)S(1)}, bf16[18,16,128]{2,1,0:T(8,128)(2,1)S(1)}, u32[]{:S(2)}, u32[]{:S(2)}) collective-permute-start(bf16[18,16,128]{2,1,0:T(8,128)(2,1)S(1)} %get-tuple-element.21), channel_id=1, source_target_pairs={{4,8},{8,4},{12,16},{16,12},{20,24},{24,20},{5,9},{9,5},{13,17},{1... | collective-permute-start | bytes 221192 | tf_op jit(solution)/shard_map/ppermute | solution.py:659
  3.2 8.2 %collective-permute-start.1 = (bf16[18,16,128]{2,1,0:T(8,128)(2,1)S(1)}, bf16[18,16,128]{2,1,0:T(8,128)(2,1)S(1)}, u32[]{:S(2)}, u32[]{:S(2)}) collective-permute-start(bf16[18,16,128]{2,1,0:T(8,128)(2,1)S(1)} %get-tuple-element.22), channel_id=1, source_target_pairs={{0,4},{4,0},{8,12},{12,8},{16,20},{20,16},{24,28},{28,24},{1,5},{5... | collective-permute-start | bytes 221192 | tf_op jit(solution)/shard_map/ppermute | solution.py:659
  11.4 5.3 %copy-start = (bf16[256,128]{1,0:T(8,128)(2,1)S(1)}, bf16[256,128]{1,0:T(8,128)(2,1)}, u32[]{:S(2)}) copy-start(bf16[256,128]{1,0:T(8,128)(2,1)} %constant.30.clone.matrix.refs_7_.refs_11_) | copy-start | bytes 196612
  12.0 3.6 %collective-permute-start.2 = (bf16[34,16,128]{2,1,0:T(8,128)(2,1)S(1)}, bf16[34,16,128]{2,1,0:T(8,128)(2,1)S(1)}, u32[]{:S(2)}, u32[]{:S(2)}) collective-permute-start(bf16[34,16,128]{2,1,0:T(8,128)(2,1)S(1)} %get-tuple-element.26), channel_id=1, source_target_pairs={{1,2},{2,1},{5,6},{6,5},{9,10},{10,9},{13,14},{14,13},{17,18},{18,... | collective-permute-start | bytes 417800 | tf_op jit(solution)/shard_map/ppermute | solution.py:659
  12.7 3.9 %collective-permute-start.3 = (bf16[34,16,128]{2,1,0:T(8,128)(2,1)S(1)}, bf16[34,16,128]{2,1,0:T(8,128)(2,1)S(1)}, u32[]{:S(2)}, u32[]{:S(2)}) collective-permute-start(bf16[34,16,128]{2,1,0:T(8,128)(2,1)S(1)} %get-tuple-element.27), channel_id=1, source_target_pairs={{0,1},{1,0},{2,3},{3,2},{4,5},{5,4},{6,7},{7,6},{8,9},{9,8},{10,11... | collective-permute-start | bytes 417800 | tf_op jit(solution)/shard_map/ppermute | solution.py:659
  36.8 1.6 %copy-start.1 = (bf16[512,128]{1,0:T(8,128)(2,1)S(1)}, bf16[512,128]{1,0:T(8,128)(2,1)}, u32[]{:S(2)}) copy-start(bf16[512,128]{1,0:T(8,128)(2,1)} %constant.32.clone.refs_9_.refs_13_) | copy-start | bytes 393220
  36.8 1.6 %copy-start.2 = (bf16[512,128]{1,0:T(8,128)(2,1)S(1)}, bf16[512,128]{1,0:T(8,128)(2,1)}, u32[]{:S(2)}) copy-start(bf16[512,128]{1,0:T(8,128)(2,1)} %constant.31.clone.refs_8_.refs_12_) | copy-start | bytes 393220
  36.8 1.6 %collective-permute-start.4 = (s16[16,5,16,128]{3,2,1,0:T(8,128)(2,1)S(1)}, s16[16,5,16,128]{3,2,1,0:T(8,128)(2,1)S(1)}, u32[]{:S(2)}, u32[]{:S(2)}) collective-permute-start(s16[16,5,16,128]{3,2,1,0:T(8,128)(2,1)S(1)} %all_to_all.10.after.refs_1_), channel_id=1, source_target_pairs={{0,1},{1,0},{2,3},{3,2},{4,5},{5,4},{6,7},{7,6},{8,9},{9,8},{10,11... | collective-permute-start | bytes 983048 | tf_op jit(solution)/shard_map/ppermute | solution.py:664
  56.2 1.4 %collective-permute-start.5 = (s16[16,3,16,128]{3,2,1,0:T(8,128)(2,1)S(1)}, s16[16,3,16,128]{3,2,1,0:T(8,128)(2,1)S(1)}, u32[]{:S(2)}, u32[]{:S(2)}) collective-permute-start(s16[16,3,16,128]{3,2,1,0:T(8,128)(2,1)S(1)} %all_to_all.11.refs_1_), channel_id=1, source_target_pairs={{0,1},{1,0},{2,3},{3,2},{4,5},{5,4},{6,7},{7,6},{8,9},{9,8},{10,11... | collective-permute-start | bytes 589832 | tf_op jit(solution)/shard_map/ppermute | solution.py:664

commit v7 on v6

--- a/solution.py
+++ b/solution.py
@@ -151,6 +151,16 @@
         write(second, first)
 
 
+def plane_slot(i, wide):
+    size_x = wide - 2 * HALO
+    if HALO <= i < HALO + size_x:
+        return i - HALO, None
+    distance = HALO - i if i < HALO else i - HALO - size_x + 1
+    near = min(distance, HALO + 1 - distance)
+    slot = size_x + near - 1 + (0 if i < HALO else HALO // 2)
+    return slot, (near if near != distance else None)
+
+
 def wide_kernel(place, got_first, got_second, part, count, edge, first, second, part_x, count_x, edge_x):
     size_x, size_y = part.shape[:2]
     wide = size_x + 2 * HALO
@@ -179,14 +189,27 @@
         fill(got_first, got_second)
 
     def write(up, down):
+        row = lax.broadcasted_iota(jnp.int32, (HALO, LANES), 0)
         for i in range(wide):
-            cells = part_x[i].astype(F32)
-            points = count_x[i].astype(F32)
-            up[i] = jnp.concatenate([cells[size_y - HALO :], points[size_y - HALO :]], 0).astype(BF16)
-            down[i] = jnp.concatenate([cells[:HALO], points[:HALO]], 0).astype(BF16)
+            slot, far = plane_slot(i, wide)
+            if far is not None:
+                continue
+            pairs = [(part_x[i].astype(F32), count_x[i].astype(F32))]
+            for k in range(wide):
+                other, d = plane_slot(k, wide)
+                if other == slot and d is not None:
+                    pairs.append((part_x[k].astype(F32), count_x[k].astype(F32)))
+                    break
+            tops = [[value[size_y - HALO :] for value in pair] for pair in pairs]
+            ends = [[value[:HALO] for value in pair] for pair in pairs]
+            if len(pairs) == 2:
+                tops[0] = [jnp.where(row >= d, a, pltpu.roll(b, d - 1, 0)) for a, b in zip(*tops)]
+                ends[0] = [jnp.where(row < HALO - d, a, pltpu.roll(b, HALO + 1 - d, 0)) for a, b in zip(*ends)]
+            up[slot] = jnp.concatenate(tops[0], 0).astype(BF16)
+            down[slot] = jnp.concatenate(ends[0], 0).astype(BF16)
         for target in (up, down):
             for j in range(wide // size_y):
-                target[wide + j] = edge_x[j * size_y : (j + 1) * size_y].astype(BF16)
+                target[wide - HALO + j] = edge_x[j * size_y : (j + 1) * size_y].astype(BF16)
 
     odd_y = 1 - place[1] % 2
 
@@ -251,10 +274,16 @@
     plane = size_y + 2 * HALO
     even = place[1] % 2 == 1
     top = lax.broadcasted_iota(jnp.int32, (HALO, LANES), 0) == 0
-    under_rows = [jnp.where(even, got[1][wide + j], got[0][wide + j]).astype(F32) for j in range(wide // size_y)]
+    under_rows = [
+        jnp.where(even, got[1][wide - HALO + j], got[0][wide - HALO + j]).astype(F32) for j in range(wide // size_y)
+    ]
     for i in range(HALO - margin, wide - HALO + margin):
-        below = jnp.where(even, got[1][i], got[0][i]).astype(F32)
-        above = jnp.where(even, got[0][i], got[1][i]).astype(F32)
+        slot, d = plane_slot(i, wide)
+        below = jnp.where(even, got[1][slot], got[0][slot]).astype(F32)
+        above = jnp.where(even, got[0][slot], got[1][slot]).astype(F32)
+        if d is not None:
+            below = jnp.concatenate([pltpu.roll(part, HALO + 1 - d, 0) for part in (below[:HALO], below[HALO:])], 0)
+            above = jnp.concatenate([pltpu.roll(part, d - 1, 0) for part in (above[:HALO], above[HALO:])], 0)
         own = part_x[i].astype(F32)
         under = under_rows[i // size_y][i % size_y : i % size_y + 1]
         over = edge_x[i : i + 1]
@@ -701,7 +730,7 @@
         pack_cell(face_counts, point_counts),
     )
     first, second = exchange(first, second, "gx")
-    packet = (wide + wide // size_y, size_y, LANES)
+    packet = (wide - HALO + wide // size_y, size_y, LANES)
     strip = (wide, size_y, LANES)
     first, second, part_x, count_x, edge_x = call(
         wide_kernel,

time: 63.1 us -> 62.7 us (level)
  no operation moved by 1% of the time
where the time goes in v7:
time: 62.7 us; the launch traced here: 62.5 us
  blocking collectives  30.9 us (49%)
  Pallas kernels  14.3 us (23%)
  starting transfers between devices  10.1 us (16%)
  waiting for transfers between devices  5.34 us (9%)
  other arithmetic  1.21 us (2%)
  between operations  0.69 us (1%)
    all_to_all x2, blocking collectives, gather(): near = lax.all_to_all(packet, ('gx', 'gy_chip'), 0, 0, tiled=True)  30.9 us
    pallas_call x6, Pallas kernels, call(): pl.pallas_call(kernel, out_shape=[jax.ShapeDtypeStruct(shape, dtype) for...  14.3 us
    ppermute x2, starting transfers between devices, exchange(): lax.ppermute(second, axis, pairs(0))  8.74 us
    ppermute x2, waiting for transfers between devices, exchange(): lax.ppermute(second, axis, pairs(0))  3.31 us
    ppermute x2, waiting for transfers between devices, gather(): return (near, lax.ppermute(near, 'gy_core', [(0, 1), (1, 0)]))  2.02 us
    ppermute x2, starting transfers between devices, exchange(): lax.ppermute(first, axis, pairs(1))  1.33 us
  transfers between devices with their start and end apart: 6, of which 4 were waited for; matrix products, arithmetic and copies ran while one was open for 0% of the time, Pallas kernels for 2%

profile of v7, /device:TPU:0, one launch (start us, length us, event | category | flops | bytes accessed | tf_op | source)
XLA Modules:
  0.0 62.5 jit_solution(12856571518326109946)
XLA Ops:
  0.6 0.1 pad_add_fusion.place.refs_0_
  0.7 1.1 %bitcast_add_fusion.words = s32[16,16,128]{2,1,0:T(8,128)S(1)} fusion(s32[3,16,16,128]{3,2,1,0:T(8,128)} %param.6, s32[16,16,128]{2,1,0:T(8,128)} %param.5), kind=kLoop, calls=%fused_computation | loop fusion | flops 327680 | bytes 655360 | tf_op jit(solution)/shard_map/add | solution.py:115
  1.9 0.7 %shard_map.68 = (bf16[18,16,128]{2,1,0:T(8,128)(2,1)S(1)}, bf16[18,16,128]{2,1,0:T(8,128)(2,1)S(1)}, bf16[16,16,128]{2,1,0:T(8,128)(2,1)S(1)}, bf16[16,16,128]{2,1,0:T(8,128)(2,1)S(1)}, bf16[2,16,128]{2,1,0:T(8,128)(2,1)S(1)}) custom-call(s32[2]{0:T(128)S(1)} %pad_add_fusion.place.refs_0_, s32[16,16,128]{2,1,0:T(8,128)S(1)} %bitcast_add_fusion.words), custom_call_target="tpu_custom_call" | custom-call | tf_op jit(solution)/shard_map/pallas_call | solution.py:712
  2.5 0.7 %collective-permute-start = (bf16[18,16,128]{2,1,0:T(8,128)(2,1)S(1)}, bf16[18,16,128]{2,1,0:T(8,128)(2,1)S(1)}, u32[]{:S(2)}, u32[]{:S(2)}) collective-permute-start(bf16[18,16,128]{2,1,0:T(8,128)(2,1)S(1)} %get-tuple-element.21), channel_id=1, source_target_pairs={{4,8},{8,4},{12,16},{16,12},{20,24},{24,20},{5,9},{9,5},{13,17},{1... | collective-permute-start | bytes 221192 | tf_op jit(solution)/shard_map/ppermute | solution.py:688
  3.2 5.8 %collective-permute-start.1 = (bf16[18,16,128]{2,1,0:T(8,128)(2,1)S(1)}, bf16[18,16,128]{2,1,0:T(8,128)(2,1)S(1)}, u32[]{:S(2)}, u32[]{:S(2)}) collective-permute-start(bf16[18,16,128]{2,1,0:T(8,128)(2,1)S(1)} %get-tuple-element.22), channel_id=1, source_target_pairs={{0,4},{4,0},{8,12},{12,8},{16,20},{20,16},{24,28},{28,24},{1,5},{5... | collective-permute-start | bytes 221192 | tf_op jit(solution)/shard_map/ppermute | solution.py:688
  9.0 0.0 collective-permute-done.got_first
  9.0 2.4 %collective-permute-done.1.got_second = bf16[18,16,128]{2,1,0:T(8,128)(2,1)S(1)} collective-permute-done((bf16[18,16,128]{2,1,0:T(8,128)(2,1)S(1)}, bf16[18,16,128]{2,1,0:T(8,128)(2,1)S(1)}, u32[]{:S(2)}, u32[]{:S(2)}) %collective-permute-start.1) | collective-permute-done | bytes 73760 | tf_op jit(solution)/shard_map/ppermute | solution.py:688
  11.4 0.0 copy-start
  11.4 0.6 %shard_map.69 = (bf16[26,16,128]{2,1,0:T(8,128)(2,1)S(1)}, bf16[26,16,128]{2,1,0:T(8,128)(2,1)S(1)}, bf16[32,16,128]{2,1,0:T(8,128)(2,1)S(1)}, bf16[32,16,128]{2,1,0:T(8,128)(2,1)S(1)}, f32[32,128]{1,0:T(8,128)S(1)}) custom-call(s32[2]{0:T(128)S(1)} %pad_add_fusion.place.refs_0_, bf16[18,16,128]{2,1,0:T(8,128)(2,1)S(1)} %collective-permute-done.got_first, ...), custom_call_target="tpu_custom_call" | custom-call | tf_op jit(solution)/shard_map/pallas_call | solution.py:712
  12.0 0.7 %collective-permute-start.2 = (bf16[26,16,128]{2,1,0:T(8,128)(2,1)S(1)}, bf16[26,16,128]{2,1,0:T(8,128)(2,1)S(1)}, u32[]{:S(2)}, u32[]{:S(2)}) collective-permute-start(bf16[26,16,128]{2,1,0:T(8,128)(2,1)S(1)} %get-tuple-element.26), channel_id=1, source_target_pairs={{1,2},{2,1},{5,6},{6,5},{9,10},{10,9},{13,14},{14,13},{17,18},{18,... | collective-permute-start | bytes 319496 | tf_op jit(solution)/shard_map/ppermute | solution.py:688
  12.7 2.9 %collective-permute-start.3 = (bf16[26,16,128]{2,1,0:T(8,128)(2,1)S(1)}, bf16[26,16,128]{2,1,0:T(8,128)(2,1)S(1)}, u32[]{:S(2)}, u32[]{:S(2)}) collective-permute-start(bf16[26,16,128]{2,1,0:T(8,128)(2,1)S(1)} %get-tuple-element.27), channel_id=1, source_target_pairs={{0,1},{1,0},{2,3},{3,2},{4,5},{5,4},{6,7},{7,6},{8,9},{9,8},{10,11... | collective-permute-start | bytes 319496 | tf_op jit(solution)/shard_map/ppermute | solution.py:688
  15.6 0.0 collective-permute-done.2.got_first
  15.6 1.0 %collective-permute-done.3.got_second = bf16[26,16,128]{2,1,0:T(8,128)(2,1)S(1)} collective-permute-done((bf16[26,16,128]{2,1,0:T(8,128)(2,1)S(1)}, bf16[26,16,128]{2,1,0:T(8,128)(2,1)S(1)}, u32[]{:S(2)}, u32[]{:S(2)}) %collective-permute-start.3) | collective-permute-done | bytes 106528 | tf_op jit(solution)/shard_map/ppermute | solution.py:688
  16.6 0.0 copy-done
  16.6 1.2 %shard_map.70 = s16[16,5,16,128]{3,2,1,0:T(8,128)(2,1)S(1)} custom-call(s32[2]{0:T(128)S(1)} %pad_add_fusion.place.refs_0_, bf16[26,16,128]{2,1,0:T(8,128)(2,1)S(1)} %collective-permute-done.2.got_first, bf16[26,16,128]{2,1,0:T(8,128)(2,1)S(1)} %collective-permute-done.3.got_second, bf16[32,16,128]{2,1,0:T(8,128)(2,1)S(1)} %get-tuple-element.28.part_x, ...), custom_call_target="tpu_custom_call" | custom-call | tf_op jit(solution)/shard_map/pallas_call | solution.py:712
  17.8 18.6 %all_to_all.10.after.refs_1_ = s16[16,5,16,128]{3,2,1,0:T(8,128)(2,1)S(1)} all-to-all(s16[16,5,16,128]{3,2,1,0:T(8,128)(2,1)S(1)} %shard_map.70), channel_id=1, replica_groups=mesh['gx'=8,'gy_chip'=2,'gy_core'=2] {'gx','gy_chip'}, dimensions={0} | all-to-all | bytes 655360 | tf_op jit(solution)/shard_map/all_to_all | solution.py:692
  36.4 0.0 copy-start.1
  36.4 0.0 copy-start.2
  36.4 0.0 collective-permute-start.4
  36.4 1.0 %shard_map.71 = (f32[1040,128]{1,0:T(8,128)S(1)}, f32[1040,128]{1,0:T(8,128)S(1)}, f32[1040,128]{1,0:T(8,128)S(1)}) custom-call(s32[2]{0:T(128)S(1)} %pad_add_fusion.place.refs_0_, s16[16,5,16,128]{3,2,1,0:T(8,128)(2,1)S(1)} %all_to_all.10.after.refs_1_, bf16[26,16,128]{2,1,0:T(8,128)(2,1)S(1)} %collective-permute-done.2.got_first, ...), custom_call_target="tpu_custom_call" | custom-call | flops 4194304 | bytes 4194304 | tf_op jit(solution)/shard_map/pallas_call | solution.py:712
  37.5 0.6 collective-permute-done.4.refs_2_
  38.0 0.0 copy-done.1
  38.0 0.0 copy-done.2
  38.0 5.6 %shard_map.72 = (f32[1040,128]{1,0:T(8,128)S(1)}, s16[16,3,16,128]{3,2,1,0:T(8,128)(2,1)S(1)}, f32[1608,128]{1,0:T(8,128)S(1)}, f32[1608,128]{1,0:T(8,128)S(1)},...) custom-call(s32[2]{0:T(128)S(1)} %pad_add_fusion.place.refs_0_, ...), custom_call_target="tpu_custom_call" | custom-call | tf_op jit(solution)/shard_map/pallas_call | solution.py:712
  43.6 12.3 %all_to_all.11.refs_1_ = s16[16,3,16,128]{3,2,1,0:T(8,128)(2,1)S(1)} all-to-all(s16[16,3,16,128]{3,2,1,0:T(8,128)(2,1)S(1)} %get-tuple-element.34), channel_id=1, replica_groups=mesh['gx'=8,'gy_chip'=2,'gy_core'=2] {'gx','gy_chip'}, dimensions={0} | all-to-all | bytes 393216 | tf_op jit(solution)/shard_map/all_to_all | solution.py:692
  55.9 0.0 collective-permute-start.5
  55.9 1.4 %collective-permute-done.5.refs_2_ = s16[16,3,16,128]{3,2,1,0:T(8,128)(2,1)S(1)} collective-permute-done((s16[16,3,16,128]{3,2,1,0:T(8,128)(2,1)S(1)}, s16[16,3,16,128]{3,2,1,0:T(8,128)(2,1)S(1)}, u32[]{:S(2)}, u32[]{:S(2)}) %collective-permute-start.5) | collective-permute-done | bytes 196640 | tf_op jit(solution)/shard_map/ppermute | solution.py:693
  57.3 5.2 %shard_map.73 = (f32[16,16,128]{2,1,0:T(8,128)}, f32[16,16,128]{2,1,0:T(8,128)}) custom-call(s32[2]{0:T(128)S(1)} %pad_add_fusion.place.refs_0_, s16[16,3,16,128]{3,2,1,0:T(8,128)(2,1)S(1)} %all_to_all.11.refs_1_, s16[16,3,16,128]{3,2,1,0:T(8,128)(2,1)S(1)} %collective-permute-done.5.refs_2_, f32[1040,128]{1,0:T(8,128)S(1)} %get-tuple-element.35.refs_3_, ...), custom_call_target="tpu_custom_call" | custom-call | tf_op jit(solution)/shard_map/pallas_call | solution.py:712
Async XLA Ops:
  2.5 6.5 %collective-permute-start = (bf16[18,16,128]{2,1,0:T(8,128)(2,1)S(1)}, bf16[18,16,128]{2,1,0:T(8,128)(2,1)S(1)}, u32[]{:S(2)}, u32[]{:S(2)}) collective-permute-start(bf16[18,16,128]{2,1,0:T(8,128)(2,1)S(1)} %get-tuple-element.21), channel_id=1, source_target_pairs={{4,8},{8,4},{12,16},{16,12},{20,24},{24,20},{5,9},{9,5},{13,17},{1... | collective-permute-start | bytes 221192 | tf_op jit(solution)/shard_map/ppermute | solution.py:688
  3.2 8.2 %collective-permute-start.1 = (bf16[18,16,128]{2,1,0:T(8,128)(2,1)S(1)}, bf16[18,16,128]{2,1,0:T(8,128)(2,1)S(1)}, u32[]{:S(2)}, u32[]{:S(2)}) collective-permute-start(bf16[18,16,128]{2,1,0:T(8,128)(2,1)S(1)} %get-tuple-element.22), channel_id=1, source_target_pairs={{0,4},{4,0},{8,12},{12,8},{16,20},{20,16},{24,28},{28,24},{1,5},{5... | collective-permute-start | bytes 221192 | tf_op jit(solution)/shard_map/ppermute | solution.py:688
  11.4 5.2 %copy-start = (bf16[256,128]{1,0:T(8,128)(2,1)S(1)}, bf16[256,128]{1,0:T(8,128)(2,1)}, u32[]{:S(2)}) copy-start(bf16[256,128]{1,0:T(8,128)(2,1)} %constant.30.clone.matrix.refs_7_.refs_11_) | copy-start | bytes 196612
  12.0 3.6 %collective-permute-start.2 = (bf16[26,16,128]{2,1,0:T(8,128)(2,1)S(1)}, bf16[26,16,128]{2,1,0:T(8,128)(2,1)S(1)}, u32[]{:S(2)}, u32[]{:S(2)}) collective-permute-start(bf16[26,16,128]{2,1,0:T(8,128)(2,1)S(1)} %get-tuple-element.26), channel_id=1, source_target_pairs={{1,2},{2,1},{5,6},{6,5},{9,10},{10,9},{13,14},{14,13},{17,18},{18,... | collective-permute-start | bytes 319496 | tf_op jit(solution)/shard_map/ppermute | solution.py:688
  12.7 3.9 %collective-permute-start.3 = (bf16[26,16,128]{2,1,0:T(8,128)(2,1)S(1)}, bf16[26,16,128]{2,1,0:T(8,128)(2,1)S(1)}, u32[]{:S(2)}, u32[]{:S(2)}) collective-permute-start(bf16[26,16,128]{2,1,0:T(8,128)(2,1)S(1)} %get-tuple-element.27), channel_id=1, source_target_pairs={{0,1},{1,0},{2,3},{3,2},{4,5},{5,4},{6,7},{7,6},{8,9},{9,8},{10,11... | collective-permute-start | bytes 319496 | tf_op jit(solution)/shard_map/ppermute | solution.py:688
  36.4 1.6 %copy-start.1 = (bf16[512,128]{1,0:T(8,128)(2,1)S(1)}, bf16[512,128]{1,0:T(8,128)(2,1)}, u32[]{:S(2)}) copy-start(bf16[512,128]{1,0:T(8,128)(2,1)} %constant.32.clone.refs_9_.refs_13_) | copy-start | bytes 393220
  36.4 1.6 %copy-start.2 = (bf16[512,128]{1,0:T(8,128)(2,1)S(1)}, bf16[512,128]{1,0:T(8,128)(2,1)}, u32[]{:S(2)}) copy-start(bf16[512,128]{1,0:T(8,128)(2,1)} %constant.31.clone.refs_8_.refs_12_) | copy-start | bytes 393220
  36.4 1.6 %collective-permute-start.4 = (s16[16,5,16,128]{3,2,1,0:T(8,128)(2,1)S(1)}, s16[16,5,16,128]{3,2,1,0:T(8,128)(2,1)S(1)}, u32[]{:S(2)}, u32[]{:S(2)}) collective-permute-start(s16[16,5,16,128]{3,2,1,0:T(8,128)(2,1)S(1)} %all_to_all.10.after.refs_1_), channel_id=1, source_target_pairs={{0,1},{1,0},{2,3},{3,2},{4,5},{5,4},{6,7},{7,6},{8,9},{9,8},{10,11... | collective-permute-start | bytes 983048 | tf_op jit(solution)/shard_map/ppermute | solution.py:693
  55.9 1.4 %collective-permute-start.5 = (s16[16,3,16,128]{3,2,1,0:T(8,128)(2,1)S(1)}, s16[16,3,16,128]{3,2,1,0:T(8,128)(2,1)S(1)}, u32[]{:S(2)}, u32[]{:S(2)}) collective-permute-start(s16[16,3,16,128]{3,2,1,0:T(8,128)(2,1)S(1)} %all_to_all.11.refs_1_), channel_id=1, source_target_pairs={{0,1},{1,0},{2,3},{3,2},{4,5},{5,4},{6,7},{7,6},{8,9},{9,8},{10,11... | collective-permute-start | bytes 589832 | tf_op jit(solution)/shard_map/ppermute | solution.py:693

commit v8 on v7

--- a/solution.py
+++ b/solution.py
@@ -269,7 +269,22 @@
     return even, odd
 
 
-def first_step(place, got, part_x, count_x, edge_x, iterate, field, inverse, margin):
+def inverse_diag(count):
+    return jnp.where(count > 0.0, 1.0 / (6.0 - screen_weight + screen_weight * count), 0.0)
+
+
+def columns_kernel(place, count_x, matrix, inverse_x, points, rows_ref):
+    wide, size_y = count_x.shape[:2]
+    size_x = wide - 2 * HALO
+    for i in range(wide):
+        inverse_x[i] = inverse_diag(count_x[i].astype(F32))
+    for i in range(size_x):
+        rows_ref[pl.ds(i * size_y, size_y), :] = count_x[HALO + i].astype(F32) - 1.0
+    even, odd = restrict_finest(rows_ref, size_x, size_y, matrix)
+    points[...] = jnp.dot(jnp.concatenate([even, odd], 1).astype(BF16), matrix[...], preferred_element_type=F32)
+
+
+def first_step(place, got, part_x, inverse_x, edge_x, iterate, field, inverse, margin):
     wide, size_y = part_x.shape[:2]
     plane = size_y + 2 * HALO
     even = place[1] % 2 == 1
@@ -296,9 +311,8 @@
             ],
             0,
         )
-        points = jnp.concatenate([below[HALO:], count_x[i].astype(F32), above[HALO:]], 0)
         given = flux_scale * cells
-        inv = jnp.where(points > 0.0, 1.0 / (6.0 - screen_weight + screen_weight * points), 0.0)
+        inv = jnp.concatenate([inverse_diag(below[HALO:]), inverse_x[i], inverse_diag(above[HALO:])], 0)
         at = pl.ds(8 + i * plane, plane)
         field[at, :] = given
         inverse[at, :] = inv
@@ -306,12 +320,26 @@
 
 
 def start_kernel(
-    place, got_first, got_second, part_x, count_x, edge_x, matrix, packet, first, second, field, inverse, rows_ref
+    place,
+    got_first,
+    got_second,
+    part_x,
+    inverse_x,
+    edge_x,
+    count_x,
+    points,
+    matrix,
+    packet,
+    first,
+    second,
+    field,
+    inverse,
+    rows_ref,
 ):
     wide, size_y = part_x.shape[:2]
     size_x = wide - 2 * HALO
     plane = size_y + 2 * HALO
-    first_step(place, (got_first, got_second), part_x, count_x, edge_x, first, field, inverse, 2)
+    first_step(place, (got_first, got_second), part_x, inverse_x, edge_x, first, field, inverse, 2)
     finest_step_two_from_zero(first, second, field, inverse, 1, wide, plane)
 
     def write(i, here, value):
@@ -320,15 +348,11 @@
     finest_residual(second, field, count_x, size_x, size_y, write)
     even, odd = restrict_finest(rows_ref, size_x, size_y, matrix)
     coarse = 0.125 * gather_lanes(jnp.concatenate([even, odd], 1), matrix[...])
-    for i in range(size_x):
-        rows_ref[pl.ds(i * size_y, size_y), :] = count_x[HALO + i].astype(F32) - 1.0
-    even, odd = restrict_finest(rows_ref, size_x, size_y, matrix)
-    points = jnp.dot(jnp.concatenate([even, odd], 1).astype(BF16), matrix[...], preferred_element_type=F32)
-    send_coarse(packet, coarse, points, size_y // 2)
+    send_coarse(packet, coarse, points[...], size_y // 2)
 
 
 def surroundings_kernel(
-    place, after, got_first, got_second, part_x, count_x, edge_x, iterate, field, inverse, first
+    place, after, got_first, got_second, part_x, inverse_x, edge_x, iterate, field, inverse, first
 ):
     wide, size_y = part_x.shape[:2]
     plane = size_y + 2 * HALO
@@ -336,7 +360,7 @@
     for ref in (iterate, field, inverse, first):
         ref[0:8] = zero
         ref[8 + wide * plane :] = zero
-    first_step(place, (got_first, got_second), part_x, count_x, edge_x, first, field, inverse, HALO)
+    first_step(place, (got_first, got_second), part_x, inverse_x, edge_x, first, field, inverse, HALO)
     for base, rows in ((8, plane), (8 + (wide - 1) * plane, plane)):
         iterate[pl.ds(base, rows), :] = first[pl.ds(base, rows), :]
     finest_step_two_from_zero(first, iterate, field, inverse, HALO - 1, wide, plane)
@@ -419,8 +443,8 @@
     return iterate
 
 
-def add_lanes(rows_ref, planes, size_y, matrix):
-    half = pair_rows(rows_ref, 0, planes * size_y).reshape(planes // 4, 4, size_y // 2, LANES)
+def add_lanes(rows_ref, planes, size_y, matrix, first_plane=0):
+    half = pair_rows(rows_ref, first_plane * size_y, planes * size_y).reshape(planes // 4, 4, size_y // 2, LANES)
     wide = jnp.concatenate([half[:, j].reshape(-1, LANES) for j in range(4)], 1)
     return gather_lanes(wide, matrix[...]).reshape(planes // 4, size_y // 2, LANES)
 
@@ -507,8 +531,15 @@
         here, total = neighbours(iterate, base, rows, stride, size_z)
         rows_ref[pl.ds(i * rows, rows), :] = given[at, :] + factor * total - diag[at, :] * here
 
-    for_planes(planes, residual)
-    target = 0.125 * add_lanes(rows_ref, planes, rows, mat_1)
+    groups = 4 if planes <= 64 else 1
+    if groups == 1:
+        for_planes(planes, residual)
+    targets = []
+    for k in range(groups):
+        for i in range(k * planes // groups, (k + 1) * planes // groups if groups > 1 else 0):
+            residual(i)
+        targets.append(add_lanes(rows_ref, planes // groups, rows, mat_1, k * planes // groups))
+    target = 0.125 * jnp.concatenate(targets, 0)
 
     screen_two, screen_three = level_two
     if first:
@@ -720,6 +751,7 @@
             cost_estimate=cost,
         )(*args)
 
+    beside = pl.CostEstimate(flops=1 << 22, bytes_accessed=4 << 20, transcendentals=0)
     cells = (size_x, size_y, LANES)
     packet = (2 * HALO + 2, size_y, LANES)
     first, second, part, count, edge = call(
@@ -745,14 +777,25 @@
     )
     first, second = exchange(first, second, ("gy_chip", "gy_core"))
     own = sizes.own_x
-    received = (first, second, part_x, count_x, edge_x)
     flat_f32 = ((flat, LANES), F32)
+    inverse_x, points = call(
+        columns_kernel,
+        [(strip, F32), ((own * sizes.own_y, LANES), F32)],
+        [((size_x * size_y, LANES), F32)],
+        place,
+        count_x,
+        mats[0],
+        cost=beside,
+    )
+    received = (first, second, part_x, inverse_x, edge_x)
     (packet,) = call(
         start_kernel,
         [((copies, own + 1, 2 * sizes.own_y, LANES), jnp.int16)],
         [flat_f32] * 4 + [((size_x * size_y, LANES), F32)],
         place,
         *received,
+        count_x,
+        points,
         mats[0],
     )
     near, far = gather(packet)
@@ -763,7 +806,7 @@
         place,
         near,
         *received,
-        cost=pl.CostEstimate(flops=1 << 22, bytes_accessed=4 << 20, transcendentals=0),
+        cost=beside,
     )
     level = (sizes.flat, LANES)
     flat_two = ((sizes.planes // 4 + 2) * (sizes.rows // 2 + 8) + 8, LANES)

time: 62.7 us -> 62.5 us (level)
  waiting for transfers between devices: 5.34 us -> 4.62 us
    ppermute x2, waiting for transfers between devices: 3.31 us -> 2.58 us  [exchange(): lax.ppermute(second, axis, pairs(0))]
    pallas_call x6 -> x7, Pallas kernels: 14.3 us -> 14.8 us  [call(): pl.pallas_call(kernel, out_shape=[jax.ShapeDtypeStruct(shape, dtype) for...]
  transfers between devices with their start and end apart: 6 -> 6, of which waited for: 4 -> 4; matrix products, arithmetic and copies ran while one was open for 0% -> 0% of each run, Pallas kernels for 2% -> 3%
where the time goes in v8:
time: 62.5 us; the launch traced here: 62.3 us
  blocking collectives  30.9 us (49%)
  Pallas kernels  14.8 us (24%)
  starting transfers between devices  10.1 us (16%)
  waiting for transfers between devices  4.62 us (7%)
  other arithmetic  1.21 us (2%)
  between operations  0.7 us (1%)
    all_to_all x2, blocking collectives, gather(): near = lax.all_to_all(packet, ('gx', 'gy_chip'), 0, 0, tiled=True)  30.9 us
    pallas_call x7, Pallas kernels, call(): pl.pallas_call(kernel, out_shape=[jax.ShapeDtypeStruct(shape, dtype) for...  14.8 us
    ppermute x2, starting transfers between devices, exchange(): lax.ppermute(second, axis, pairs(0))  8.74 us
    ppermute x2, waiting for transfers between devices, exchange(): lax.ppermute(second, axis, pairs(0))  2.58 us
    ppermute x2, waiting for transfers between devices, gather(): return (near, lax.ppermute(near, 'gy_core', [(0, 1), (1, 0)]))  2.03 us
    ppermute x2, starting transfers between devices, exchange(): lax.ppermute(first, axis, pairs(1))  1.33 us
  transfers between devices with their start and end apart: 6, of which 4 were waited for; matrix products, arithmetic and copies ran while one was open for 0% of the time, Pallas kernels for 3%

profile of v8, /device:TPU:0, one launch (start us, length us, event | category | flops | bytes accessed | tf_op | source)
XLA Modules:
  0.0 62.3 jit_solution(9828651681041024398)
XLA Ops:
  0.6 0.1 pad_add_fusion.place.refs_0_
  0.7 1.1 %bitcast_add_fusion.words = s32[16,16,128]{2,1,0:T(8,128)S(1)} fusion(s32[3,16,16,128]{3,2,1,0:T(8,128)} %param.6, s32[16,16,128]{2,1,0:T(8,128)} %param.5), kind=kLoop, calls=%fused_computation | loop fusion | flops 327680 | bytes 655360 | tf_op jit(solution)/shard_map/add | solution.py:115
  1.9 0.7 %shard_map.68 = (bf16[18,16,128]{2,1,0:T(8,128)(2,1)S(1)}, bf16[18,16,128]{2,1,0:T(8,128)(2,1)S(1)}, bf16[16,16,128]{2,1,0:T(8,128)(2,1)S(1)}, bf16[16,16,128]{2,1,0:T(8,128)(2,1)S(1)}, bf16[2,16,128]{2,1,0:T(8,128)(2,1)S(1)}) custom-call(s32[2]{0:T(128)S(1)} %pad_add_fusion.place.refs_0_, s32[16,16,128]{2,1,0:T(8,128)S(1)} %bitcast_add_fusion.words), custom_call_target="tpu_custom_call" | custom-call | tf_op jit(solution)/shard_map/pallas_call | solution.py:743
  2.5 0.7 %collective-permute-start = (bf16[18,16,128]{2,1,0:T(8,128)(2,1)S(1)}, bf16[18,16,128]{2,1,0:T(8,128)(2,1)S(1)}, u32[]{:S(2)}, u32[]{:S(2)}) collective-permute-start(bf16[18,16,128]{2,1,0:T(8,128)(2,1)S(1)} %get-tuple-element.23), channel_id=1, source_target_pairs={{4,8},{8,4},{12,16},{16,12},{20,24},{24,20},{5,9},{9,5},{13,17},{1... | collective-permute-start | bytes 221192 | tf_op jit(solution)/shard_map/ppermute | solution.py:719
  3.2 5.8 %collective-permute-start.1 = (bf16[18,16,128]{2,1,0:T(8,128)(2,1)S(1)}, bf16[18,16,128]{2,1,0:T(8,128)(2,1)S(1)}, u32[]{:S(2)}, u32[]{:S(2)}) collective-permute-start(bf16[18,16,128]{2,1,0:T(8,128)(2,1)S(1)} %get-tuple-element.24), channel_id=1, source_target_pairs={{0,4},{4,0},{8,12},{12,8},{16,20},{20,16},{24,28},{28,24},{1,5},{5... | collective-permute-start | bytes 221192 | tf_op jit(solution)/shard_map/ppermute | solution.py:719
  9.0 0.0 collective-permute-done.got_first
  9.0 2.4 %collective-permute-done.1.got_second = bf16[18,16,128]{2,1,0:T(8,128)(2,1)S(1)} collective-permute-done((bf16[18,16,128]{2,1,0:T(8,128)(2,1)S(1)}, bf16[18,16,128]{2,1,0:T(8,128)(2,1)S(1)}, u32[]{:S(2)}, u32[]{:S(2)}) %collective-permute-start.1) | collective-permute-done | bytes 73760 | tf_op jit(solution)/shard_map/ppermute | solution.py:719
  11.4 0.0 copy-start
  11.4 0.6 %shard_map.69 = (bf16[26,16,128]{2,1,0:T(8,128)(2,1)S(1)}, bf16[26,16,128]{2,1,0:T(8,128)(2,1)S(1)}, bf16[32,16,128]{2,1,0:T(8,128)(2,1)S(1)}, bf16[32,16,128]{2,1,0:T(8,128)(2,1)S(1)}, f32[32,128]{1,0:T(8,128)S(1)}) custom-call(s32[2]{0:T(128)S(1)} %pad_add_fusion.place.refs_0_, bf16[18,16,128]{2,1,0:T(8,128)(2,1)S(1)} %collective-permute-done.got_first, ...), custom_call_target="tpu_custom_call" | custom-call | tf_op jit(solution)/shard_map/pallas_call | solution.py:743
  12.0 0.7 %collective-permute-start.2 = (bf16[26,16,128]{2,1,0:T(8,128)(2,1)S(1)}, bf16[26,16,128]{2,1,0:T(8,128)(2,1)S(1)}, u32[]{:S(2)}, u32[]{:S(2)}) collective-permute-start(bf16[26,16,128]{2,1,0:T(8,128)(2,1)S(1)} %get-tuple-element.28), channel_id=1, source_target_pairs={{1,2},{2,1},{5,6},{6,5},{9,10},{10,9},{13,14},{14,13},{17,18},{18,... | collective-permute-start | bytes 319496 | tf_op jit(solution)/shard_map/ppermute | solution.py:719
  12.7 2.9 %collective-permute-start.3 = (bf16[26,16,128]{2,1,0:T(8,128)(2,1)S(1)}, bf16[26,16,128]{2,1,0:T(8,128)(2,1)S(1)}, u32[]{:S(2)}, u32[]{:S(2)}) collective-permute-start(bf16[26,16,128]{2,1,0:T(8,128)(2,1)S(1)} %get-tuple-element.29), channel_id=1, source_target_pairs={{0,1},{1,0},{2,3},{3,2},{4,5},{5,4},{6,7},{7,6},{8,9},{9,8},{10,11... | collective-permute-start | bytes 319496 | tf_op jit(solution)/shard_map/ppermute | solution.py:719
  15.6 0.0 copy-done
  15.6 0.7 %shard_map.70 = (f32[32,16,128]{2,1,0:T(8,128)S(1)}, f32[32,128]{1,0:T(8,128)S(1)}) custom-call(s32[2]{0:T(128)S(1)} %pad_add_fusion.place.refs_0_, bf16[32,16,128]{2,1,0:T(8,128)(2,1)S(1)} %get-tuple-element.31.count_x.refs_6_, bf16[256,128]{1,0:T(8,128)(2,1)S(1)} %copy-done), custom_call_target="tpu_custom_call" | custom-call | flops 4194304 | bytes 4194304 | tf_op jit(solution)/shard_map/pallas_call | solution.py:743
  16.3 0.0 collective-permute-done.2.got_first
  16.4 0.2 collective-permute-done.3.got_second
  16.6 1.1 %shard_map.71 = s16[16,5,16,128]{3,2,1,0:T(8,128)(2,1)S(1)} custom-call(s32[2]{0:T(128)S(1)} %pad_add_fusion.place.refs_0_, bf16[26,16,128]{2,1,0:T(8,128)(2,1)S(1)} %collective-permute-done.2.got_first, bf16[26,16,128]{2,1,0:T(8,128)(2,1)S(1)} %collective-permute-done.3.got_second, bf16[32,16,128]{2,1,0:T(8,128)(2,1)S(1)} %get-tuple-element.30.part_x, ...), custom_call_target="tpu_custom_call" | custom-call | tf_op jit(solution)/shard_map/pallas_call | solution.py:743
  17.7 18.6 %all_to_all.10.after.refs_1_ = s16[16,5,16,128]{3,2,1,0:T(8,128)(2,1)S(1)} all-to-all(s16[16,5,16,128]{3,2,1,0:T(8,128)(2,1)S(1)} %shard_map.71), channel_id=1, replica_groups=mesh['gx'=8,'gy_chip'=2,'gy_core'=2] {'gx','gy_chip'}, dimensions={0} | all-to-all | bytes 655360 | tf_op jit(solution)/shard_map/all_to_all | solution.py:723
  36.3 0.0 copy-start.1
  36.3 0.0 copy-start.2
  36.3 0.0 collective-permute-start.4
  36.3 1.0 %shard_map.72 = (f32[1040,128]{1,0:T(8,128)S(1)}, f32[1040,128]{1,0:T(8,128)S(1)}, f32[1040,128]{1,0:T(8,128)S(1)}) custom-call(s32[2]{0:T(128)S(1)} %pad_add_fusion.place.refs_0_, s16[16,5,16,128]{3,2,1,0:T(8,128)(2,1)S(1)} %all_to_all.10.after.refs_1_, bf16[26,16,128]{2,1,0:T(8,128)(2,1)S(1)} %collective-permute-done.2.got_first, ...), custom_call_target="tpu_custom_call" | custom-call | flops 4194304 | bytes 4194304 | tf_op jit(solution)/shard_map/pallas_call | solution.py:743
  37.4 0.6 collective-permute-done.4.refs_2_
  38.0 0.0 copy-done.1
  38.0 0.0 copy-done.2
  38.0 5.5 %shard_map.73 = (f32[1040,128]{1,0:T(8,128)S(1)}, s16[16,3,16,128]{3,2,1,0:T(8,128)(2,1)S(1)}, f32[1608,128]{1,0:T(8,128)S(1)}, f32[1608,128]{1,0:T(8,128)S(1)},...) custom-call(s32[2]{0:T(128)S(1)} %pad_add_fusion.place.refs_0_, ...), custom_call_target="tpu_custom_call" | custom-call | tf_op jit(solution)/shard_map/pallas_call | solution.py:743
  43.5 12.2 %all_to_all.11.refs_1_ = s16[16,3,16,128]{3,2,1,0:T(8,128)(2,1)S(1)} all-to-all(s16[16,3,16,128]{3,2,1,0:T(8,128)(2,1)S(1)} %get-tuple-element.38), channel_id=1, replica_groups=mesh['gx'=8,'gy_chip'=2,'gy_core'=2] {'gx','gy_chip'}, dimensions={0} | all-to-all | bytes 393216 | tf_op jit(solution)/shard_map/all_to_all | solution.py:723
  55.8 0.0 collective-permute-start.5
  55.8 1.4 %collective-permute-done.5.refs_2_ = s16[16,3,16,128]{3,2,1,0:T(8,128)(2,1)S(1)} collective-permute-done((s16[16,3,16,128]{3,2,1,0:T(8,128)(2,1)S(1)}, s16[16,3,16,128]{3,2,1,0:T(8,128)(2,1)S(1)}, u32[]{:S(2)}, u32[]{:S(2)}) %collective-permute-start.5) | collective-permute-done | bytes 196640 | tf_op jit(solution)/shard_map/ppermute | solution.py:724
  57.2 5.1 %shard_map.74 = (f32[16,16,128]{2,1,0:T(8,128)}, f32[16,16,128]{2,1,0:T(8,128)}) custom-call(s32[2]{0:T(128)S(1)} %pad_add_fusion.place.refs_0_, s16[16,3,16,128]{3,2,1,0:T(8,128)(2,1)S(1)} %all_to_all.11.refs_1_, s16[16,3,16,128]{3,2,1,0:T(8,128)(2,1)S(1)} %collective-permute-done.5.refs_2_, f32[1040,128]{1,0:T(8,128)S(1)} %get-tuple-element.39.refs_3_, ...), custom_call_target="tpu_custom_call" | custom-call | tf_op jit(solution)/shard_map/pallas_call | solution.py:743
Async XLA Ops:
  2.5 6.5 %collective-permute-start = (bf16[18,16,128]{2,1,0:T(8,128)(2,1)S(1)}, bf16[18,16,128]{2,1,0:T(8,128)(2,1)S(1)}, u32[]{:S(2)}, u32[]{:S(2)}) collective-permute-start(bf16[18,16,128]{2,1,0:T(8,128)(2,1)S(1)} %get-tuple-element.23), channel_id=1, source_target_pairs={{4,8},{8,4},{12,16},{16,12},{20,24},{24,20},{5,9},{9,5},{13,17},{1... | collective-permute-start | bytes 221192 | tf_op jit(solution)/shard_map/ppermute | solution.py:719
  3.2 8.2 %collective-permute-start.1 = (bf16[18,16,128]{2,1,0:T(8,128)(2,1)S(1)}, bf16[18,16,128]{2,1,0:T(8,128)(2,1)S(1)}, u32[]{:S(2)}, u32[]{:S(2)}) collective-permute-start(bf16[18,16,128]{2,1,0:T(8,128)(2,1)S(1)} %get-tuple-element.24), channel_id=1, source_target_pairs={{0,4},{4,0},{8,12},{12,8},{16,20},{20,16},{24,28},{28,24},{1,5},{5... | collective-permute-start | bytes 221192 | tf_op jit(solution)/shard_map/ppermute | solution.py:719
  11.4 4.3 %copy-start = (bf16[256,128]{1,0:T(8,128)(2,1)S(1)}, bf16[256,128]{1,0:T(8,128)(2,1)}, u32[]{:S(2)}) copy-start(bf16[256,128]{1,0:T(8,128)(2,1)} %constant.30.clone.matrix.refs_7_.refs_11_) | copy-start | bytes 196612
  12.0 4.4 %collective-permute-start.2 = (bf16[26,16,128]{2,1,0:T(8,128)(2,1)S(1)}, bf16[26,16,128]{2,1,0:T(8,128)(2,1)S(1)}, u32[]{:S(2)}, u32[]{:S(2)}) collective-permute-start(bf16[26,16,128]{2,1,0:T(8,128)(2,1)S(1)} %get-tuple-element.28), channel_id=1, source_target_pairs={{1,2},{2,1},{5,6},{6,5},{9,10},{10,9},{13,14},{14,13},{17,18},{18,... | collective-permute-start | bytes 319496 | tf_op jit(solution)/shard_map/ppermute | solution.py:719
  12.7 3.9 %collective-permute-start.3 = (bf16[26,16,128]{2,1,0:T(8,128)(2,1)S(1)}, bf16[26,16,128]{2,1,0:T(8,128)(2,1)S(1)}, u32[]{:S(2)}, u32[]{:S(2)}) collective-permute-start(bf16[26,16,128]{2,1,0:T(8,128)(2,1)S(1)} %get-tuple-element.29), channel_id=1, source_target_pairs={{0,1},{1,0},{2,3},{3,2},{4,5},{5,4},{6,7},{7,6},{8,9},{9,8},{10,11... | collective-permute-start | bytes 319496 | tf_op jit(solution)/shard_map/ppermute | solution.py:719
  36.3 1.6 %copy-start.1 = (bf16[512,128]{1,0:T(8,128)(2,1)S(1)}, bf16[512,128]{1,0:T(8,128)(2,1)}, u32[]{:S(2)}) copy-start(bf16[512,128]{1,0:T(8,128)(2,1)} %constant.32.clone.refs_9_.refs_13_) | copy-start | bytes 393220
  36.3 1.6 %copy-start.2 = (bf16[512,128]{1,0:T(8,128)(2,1)S(1)}, bf16[512,128]{1,0:T(8,128)(2,1)}, u32[]{:S(2)}) copy-start(bf16[512,128]{1,0:T(8,128)(2,1)} %constant.31.clone.refs_8_.refs_12_) | copy-start | bytes 393220
  36.3 1.6 %collective-permute-start.4 = (s16[16,5,16,128]{3,2,1,0:T(8,128)(2,1)S(1)}, s16[16,5,16,128]{3,2,1,0:T(8,128)(2,1)S(1)}, u32[]{:S(2)}, u32[]{:S(2)}) collective-permute-start(s16[16,5,16,128]{3,2,1,0:T(8,128)(2,1)S(1)} %all_to_all.10.after.refs_1_), channel_id=1, source_target_pairs={{0,1},{1,0},{2,3},{3,2},{4,5},{5,4},{6,7},{7,6},{8,9},{9,8},{10,11... | collective-permute-start | bytes 983048 | tf_op jit(solution)/shard_map/ppermute | solution.py:724
  55.8 1.4 %collective-permute-start.5 = (s16[16,3,16,128]{3,2,1,0:T(8,128)(2,1)S(1)}, s16[16,3,16,128]{3,2,1,0:T(8,128)(2,1)S(1)}, u32[]{:S(2)}, u32[]{:S(2)}) collective-permute-start(s16[16,3,16,128]{3,2,1,0:T(8,128)(2,1)S(1)} %all_to_all.11.refs_1_), channel_id=1, source_target_pairs={{0,1},{1,0},{2,3},{3,2},{4,5},{5,4},{6,7},{7,6},{8,9},{9,8},{10,11... | collective-permute-start | bytes 589832 | tf_op jit(solution)/shard_map/ppermute | solution.py:724

commit v9 on v8

--- a/solution.py
+++ b/solution.py
@@ -692,15 +692,16 @@
         copy.start()
         return copy
 
-    for i in range(size_x):
-        solution_out[i] = iterate[pl.ds(8 + (HALO + i) * plane + HALO, size_y), :]
-    copies = [send(solution_out, solution_far, 0)]
+    copies = []
 
     def write(i, here, value):
+        solution_out[i] = here
         residual_out[i] = value
-        if (2 * i + 2) % size_x == 0:
-            half = pl.ds(i + 1 - size_x // 2, size_x // 2)
-            copies.append(send(residual_out.at[half], residual_far.at[half], 1 + (i + 1) * 2 // size_x))
+        if (4 * i + 4) % size_x == 0:
+            part = pl.ds(i + 1 - size_x // 4, size_x // 4)
+            number = (i + 1) * 4 // size_x - 1
+            copies.append(send(solution_out.at[part], solution_far.at[part], 2 * number))
+            copies.append(send(residual_out.at[part], residual_far.at[part], 2 * number + 1))
 
     finest_residual(iterate, field, count_x, size_x, size_y, write)
     for copy in copies:
@@ -859,7 +860,7 @@
         screen_two,
         screen_three,
         *mats,
-        copies=4,
+        copies=8,
         far_out=True,
     )
     return solution_own, residual_own

time: 62.5 us -> 62.6 us (level)
  no operation moved by 1% of the time
where the time goes in v9:
time: 62.6 us; the launch traced here: 62.3 us
  blocking collectives  30.9 us (49%)
  Pallas kernels  14.9 us (24%)
  starting transfers between devices  10.1 us (16%)
  waiting for transfers between devices  4.62 us (7%)
  other arithmetic  1.21 us (2%)
  between operations  0.7 us (1%)
    all_to_all x2, blocking collectives, gather(): near = lax.all_to_all(packet, ('gx', 'gy_chip'), 0, 0, tiled=True)  30.9 us
    pallas_call x7, Pallas kernels, call(): pl.pallas_call(kernel, out_shape=[jax.ShapeDtypeStruct(shape, dtype) for...  14.9 us
    ppermute x2, starting transfers between devices, exchange(): lax.ppermute(second, axis, pairs(0))  8.74 us
    ppermute x2, waiting for transfers between devices, exchange(): lax.ppermute(second, axis, pairs(0))  2.58 us
    ppermute x2, waiting for transfers between devices, gather(): return (near, lax.ppermute(near, 'gy_core', [(0, 1), (1, 0)]))  2.03 us
    ppermute x2, starting transfers between devices, exchange(): lax.ppermute(first, axis, pairs(1))  1.33 us
  transfers between devices with their start and end apart: 6, of which 4 were waited for; matrix products, arithmetic and copies ran while one was open for 0% of the time, Pallas kernels for 3%

profile of v9, /device:TPU:0, one launch (start us, length us, event | category | flops | bytes accessed | tf_op | source)
XLA Modules:
  0.0 62.3 jit_solution(6119318566176687276)
XLA Ops:
  0.6 0.1 pad_add_fusion.place.refs_0_
  0.7 1.1 %bitcast_add_fusion.words = s32[16,16,128]{2,1,0:T(8,128)S(1)} fusion(s32[3,16,16,128]{3,2,1,0:T(8,128)} %param.6, s32[16,16,128]{2,1,0:T(8,128)} %param.5), kind=kLoop, calls=%fused_computation | loop fusion | flops 327680 | bytes 655360 | tf_op jit(solution)/shard_map/add | solution.py:115
  1.9 0.7 %shard_map.68 = (bf16[18,16,128]{2,1,0:T(8,128)(2,1)S(1)}, bf16[18,16,128]{2,1,0:T(8,128)(2,1)S(1)}, bf16[16,16,128]{2,1,0:T(8,128)(2,1)S(1)}, bf16[16,16,128]{2,1,0:T(8,128)(2,1)S(1)}, bf16[2,16,128]{2,1,0:T(8,128)(2,1)S(1)}) custom-call(s32[2]{0:T(128)S(1)} %pad_add_fusion.place.refs_0_, s32[16,16,128]{2,1,0:T(8,128)S(1)} %bitcast_add_fusion.words), custom_call_target="tpu_custom_call" | custom-call | tf_op jit(solution)/shard_map/pallas_call | solution.py:744
  2.5 0.7 %collective-permute-start = (bf16[18,16,128]{2,1,0:T(8,128)(2,1)S(1)}, bf16[18,16,128]{2,1,0:T(8,128)(2,1)S(1)}, u32[]{:S(2)}, u32[]{:S(2)}) collective-permute-start(bf16[18,16,128]{2,1,0:T(8,128)(2,1)S(1)} %get-tuple-element.23), channel_id=1, source_target_pairs={{4,8},{8,4},{12,16},{16,12},{20,24},{24,20},{5,9},{9,5},{13,17},{1... | collective-permute-start | bytes 221192 | tf_op jit(solution)/shard_map/ppermute | solution.py:720
  3.2 5.8 %collective-permute-start.1 = (bf16[18,16,128]{2,1,0:T(8,128)(2,1)S(1)}, bf16[18,16,128]{2,1,0:T(8,128)(2,1)S(1)}, u32[]{:S(2)}, u32[]{:S(2)}) collective-permute-start(bf16[18,16,128]{2,1,0:T(8,128)(2,1)S(1)} %get-tuple-element.24), channel_id=1, source_target_pairs={{0,4},{4,0},{8,12},{12,8},{16,20},{20,16},{24,28},{28,24},{1,5},{5... | collective-permute-start | bytes 221192 | tf_op jit(solution)/shard_map/ppermute | solution.py:720
  9.0 0.0 collective-permute-done.got_first
  9.0 2.4 %collective-permute-done.1.got_second = bf16[18,16,128]{2,1,0:T(8,128)(2,1)S(1)} collective-permute-done((bf16[18,16,128]{2,1,0:T(8,128)(2,1)S(1)}, bf16[18,16,128]{2,1,0:T(8,128)(2,1)S(1)}, u32[]{:S(2)}, u32[]{:S(2)}) %collective-permute-start.1) | collective-permute-done | bytes 73760 | tf_op jit(solution)/shard_map/ppermute | solution.py:720
  11.4 0.0 copy-start
  11.4 0.6 %shard_map.69 = (bf16[26,16,128]{2,1,0:T(8,128)(2,1)S(1)}, bf16[26,16,128]{2,1,0:T(8,128)(2,1)S(1)}, bf16[32,16,128]{2,1,0:T(8,128)(2,1)S(1)}, bf16[32,16,128]{2,1,0:T(8,128)(2,1)S(1)}, f32[32,128]{1,0:T(8,128)S(1)}) custom-call(s32[2]{0:T(128)S(1)} %pad_add_fusion.place.refs_0_, bf16[18,16,128]{2,1,0:T(8,128)(2,1)S(1)} %collective-permute-done.got_first, ...), custom_call_target="tpu_custom_call" | custom-call | tf_op jit(solution)/shard_map/pallas_call | solution.py:744
  12.0 0.7 %collective-permute-start.2 = (bf16[26,16,128]{2,1,0:T(8,128)(2,1)S(1)}, bf16[26,16,128]{2,1,0:T(8,128)(2,1)S(1)}, u32[]{:S(2)}, u32[]{:S(2)}) collective-permute-start(bf16[26,16,128]{2,1,0:T(8,128)(2,1)S(1)} %get-tuple-element.28), channel_id=1, source_target_pairs={{1,2},{2,1},{5,6},{6,5},{9,10},{10,9},{13,14},{14,13},{17,18},{18,... | collective-permute-start | bytes 319496 | tf_op jit(solution)/shard_map/ppermute | solution.py:720
  12.7 2.9 %collective-permute-start.3 = (bf16[26,16,128]{2,1,0:T(8,128)(2,1)S(1)}, bf16[26,16,128]{2,1,0:T(8,128)(2,1)S(1)}, u32[]{:S(2)}, u32[]{:S(2)}) collective-permute-start(bf16[26,16,128]{2,1,0:T(8,128)(2,1)S(1)} %get-tuple-element.29), channel_id=1, source_target_pairs={{0,1},{1,0},{2,3},{3,2},{4,5},{5,4},{6,7},{7,6},{8,9},{9,8},{10,11... | collective-permute-start | bytes 319496 | tf_op jit(solution)/shard_map/ppermute | solution.py:720
  15.6 0.0 copy-done
  15.6 0.7 %shard_map.70 = (f32[32,16,128]{2,1,0:T(8,128)S(1)}, f32[32,128]{1,0:T(8,128)S(1)}) custom-call(s32[2]{0:T(128)S(1)} %pad_add_fusion.place.refs_0_, bf16[32,16,128]{2,1,0:T(8,128)(2,1)S(1)} %get-tuple-element.31.count_x.refs_6_, bf16[256,128]{1,0:T(8,128)(2,1)S(1)} %copy-done), custom_call_target="tpu_custom_call" | custom-call | flops 4194304 | bytes 4194304 | tf_op jit(solution)/shard_map/pallas_call | solution.py:744
  16.3 0.0 collective-permute-done.2.got_first
  16.4 0.2 collective-permute-done.3.got_second
  16.6 1.1 %shard_map.71 = s16[16,5,16,128]{3,2,1,0:T(8,128)(2,1)S(1)} custom-call(s32[2]{0:T(128)S(1)} %pad_add_fusion.place.refs_0_, bf16[26,16,128]{2,1,0:T(8,128)(2,1)S(1)} %collective-permute-done.2.got_first, bf16[26,16,128]{2,1,0:T(8,128)(2,1)S(1)} %collective-permute-done.3.got_second, bf16[32,16,128]{2,1,0:T(8,128)(2,1)S(1)} %get-tuple-element.30.part_x, ...), custom_call_target="tpu_custom_call" | custom-call | tf_op jit(solution)/shard_map/pallas_call | solution.py:744
  17.7 18.6 %all_to_all.10.after.refs_1_ = s16[16,5,16,128]{3,2,1,0:T(8,128)(2,1)S(1)} all-to-all(s16[16,5,16,128]{3,2,1,0:T(8,128)(2,1)S(1)} %shard_map.71), channel_id=1, replica_groups=mesh['gx'=8,'gy_chip'=2,'gy_core'=2] {'gx','gy_chip'}, dimensions={0} | all-to-all | bytes 655360 | tf_op jit(solution)/shard_map/all_to_all | solution.py:724
  36.3 0.0 copy-start.1
  36.3 0.0 copy-start.2
  36.3 0.0 collective-permute-start.4
  36.3 1.0 %shard_map.72 = (f32[1040,128]{1,0:T(8,128)S(1)}, f32[1040,128]{1,0:T(8,128)S(1)}, f32[1040,128]{1,0:T(8,128)S(1)}) custom-call(s32[2]{0:T(128)S(1)} %pad_add_fusion.place.refs_0_, s16[16,5,16,128]{3,2,1,0:T(8,128)(2,1)S(1)} %all_to_all.10.after.refs_1_, bf16[26,16,128]{2,1,0:T(8,128)(2,1)S(1)} %collective-permute-done.2.got_first, ...), custom_call_target="tpu_custom_call" | custom-call | flops 4194304 | bytes 4194304 | tf_op jit(solution)/shard_map/pallas_call | solution.py:744
  37.4 0.6 collective-permute-done.4.refs_2_
  38.0 0.0 copy-done.1
  38.0 0.0 copy-done.2
  38.0 5.5 %shard_map.73 = (f32[1040,128]{1,0:T(8,128)S(1)}, s16[16,3,16,128]{3,2,1,0:T(8,128)(2,1)S(1)}, f32[1608,128]{1,0:T(8,128)S(1)}, f32[1608,128]{1,0:T(8,128)S(1)},...) custom-call(s32[2]{0:T(128)S(1)} %pad_add_fusion.place.refs_0_, ...), custom_call_target="tpu_custom_call" | custom-call | tf_op jit(solution)/shard_map/pallas_call | solution.py:744
  43.5 12.2 %all_to_all.11.refs_1_ = s16[16,3,16,128]{3,2,1,0:T(8,128)(2,1)S(1)} all-to-all(s16[16,3,16,128]{3,2,1,0:T(8,128)(2,1)S(1)} %get-tuple-element.38), channel_id=1, replica_groups=mesh['gx'=8,'gy_chip'=2,'gy_core'=2] {'gx','gy_chip'}, dimensions={0} | all-to-all | bytes 393216 | tf_op jit(solution)/shard_map/all_to_all | solution.py:724
  55.8 0.0 collective-permute-start.5
  55.8 1.4 %collective-permute-done.5.refs_2_ = s16[16,3,16,128]{3,2,1,0:T(8,128)(2,1)S(1)} collective-permute-done((s16[16,3,16,128]{3,2,1,0:T(8,128)(2,1)S(1)}, s16[16,3,16,128]{3,2,1,0:T(8,128)(2,1)S(1)}, u32[]{:S(2)}, u32[]{:S(2)}) %collective-permute-start.5) | collective-permute-done | bytes 196640 | tf_op jit(solution)/shard_map/ppermute | solution.py:725
  57.2 5.1 %shard_map.74 = (f32[16,16,128]{2,1,0:T(8,128)}, f32[16,16,128]{2,1,0:T(8,128)}) custom-call(s32[2]{0:T(128)S(1)} %pad_add_fusion.place.refs_0_, s16[16,3,16,128]{3,2,1,0:T(8,128)(2,1)S(1)} %all_to_all.11.refs_1_, s16[16,3,16,128]{3,2,1,0:T(8,128)(2,1)S(1)} %collective-permute-done.5.refs_2_, f32[1040,128]{1,0:T(8,128)S(1)} %get-tuple-element.39.refs_3_, ...), custom_call_target="tpu_custom_call" | custom-call | tf_op jit(solution)/shard_map/pallas_call | solution.py:744
Async XLA Ops:
  2.5 6.5 %collective-permute-start = (bf16[18,16,128]{2,1,0:T(8,128)(2,1)S(1)}, bf16[18,16,128]{2,1,0:T(8,128)(2,1)S(1)}, u32[]{:S(2)}, u32[]{:S(2)}) collective-permute-start(bf16[18,16,128]{2,1,0:T(8,128)(2,1)S(1)} %get-tuple-element.23), channel_id=1, source_target_pairs={{4,8},{8,4},{12,16},{16,12},{20,24},{24,20},{5,9},{9,5},{13,17},{1... | collective-permute-start | bytes 221192 | tf_op jit(solution)/shard_map/ppermute | solution.py:720
  3.2 8.2 %collective-permute-start.1 = (bf16[18,16,128]{2,1,0:T(8,128)(2,1)S(1)}, bf16[18,16,128]{2,1,0:T(8,128)(2,1)S(1)}, u32[]{:S(2)}, u32[]{:S(2)}) collective-permute-start(bf16[18,16,128]{2,1,0:T(8,128)(2,1)S(1)} %get-tuple-element.24), channel_id=1, source_target_pairs={{0,4},{4,0},{8,12},{12,8},{16,20},{20,16},{24,28},{28,24},{1,5},{5... | collective-permute-start | bytes 221192 | tf_op jit(solution)/shard_map/ppermute | solution.py:720
  11.4 4.3 %copy-start = (bf16[256,128]{1,0:T(8,128)(2,1)S(1)}, bf16[256,128]{1,0:T(8,128)(2,1)}, u32[]{:S(2)}) copy-start(bf16[256,128]{1,0:T(8,128)(2,1)} %constant.30.clone.matrix.refs_7_.refs_11_) | copy-start | bytes 196612
  12.0 4.4 %collective-permute-start.2 = (bf16[26,16,128]{2,1,0:T(8,128)(2,1)S(1)}, bf16[26,16,128]{2,1,0:T(8,128)(2,1)S(1)}, u32[]{:S(2)}, u32[]{:S(2)}) collective-permute-start(bf16[26,16,128]{2,1,0:T(8,128)(2,1)S(1)} %get-tuple-element.28), channel_id=1, source_target_pairs={{1,2},{2,1},{5,6},{6,5},{9,10},{10,9},{13,14},{14,13},{17,18},{18,... | collective-permute-start | bytes 319496 | tf_op jit(solution)/shard_map/ppermute | solution.py:720
  12.7 3.9 %collective-permute-start.3 = (bf16[26,16,128]{2,1,0:T(8,128)(2,1)S(1)}, bf16[26,16,128]{2,1,0:T(8,128)(2,1)S(1)}, u32[]{:S(2)}, u32[]{:S(2)}) collective-permute-start(bf16[26,16,128]{2,1,0:T(8,128)(2,1)S(1)} %get-tuple-element.29), channel_id=1, source_target_pairs={{0,1},{1,0},{2,3},{3,2},{4,5},{5,4},{6,7},{7,6},{8,9},{9,8},{10,11... | collective-permute-start | bytes 319496 | tf_op jit(solution)/shard_map/ppermute | solution.py:720
  36.3 1.6 %copy-start.1 = (bf16[512,128]{1,0:T(8,128)(2,1)S(1)}, bf16[512,128]{1,0:T(8,128)(2,1)}, u32[]{:S(2)}) copy-start(bf16[512,128]{1,0:T(8,128)(2,1)} %constant.32.clone.refs_9_.refs_13_) | copy-start | bytes 393220
  36.3 1.6 %copy-start.2 = (bf16[512,128]{1,0:T(8,128)(2,1)S(1)}, bf16[512,128]{1,0:T(8,128)(2,1)}, u32[]{:S(2)}) copy-start(bf16[512,128]{1,0:T(8,128)(2,1)} %constant.31.clone.refs_8_.refs_12_) | copy-start | bytes 393220
  36.3 1.6 %collective-permute-start.4 = (s16[16,5,16,128]{3,2,1,0:T(8,128)(2,1)S(1)}, s16[16,5,16,128]{3,2,1,0:T(8,128)(2,1)S(1)}, u32[]{:S(2)}, u32[]{:S(2)}) collective-permute-start(s16[16,5,16,128]{3,2,1,0:T(8,128)(2,1)S(1)} %all_to_all.10.after.refs_1_), channel_id=1, source_target_pairs={{0,1},{1,0},{2,3},{3,2},{4,5},{5,4},{6,7},{7,6},{8,9},{9,8},{10,11... | collective-permute-start | bytes 983048 | tf_op jit(solution)/shard_map/ppermute | solution.py:725
  55.8 1.4 %collective-permute-start.5 = (s16[16,3,16,128]{3,2,1,0:T(8,128)(2,1)S(1)}, s16[16,3,16,128]{3,2,1,0:T(8,128)(2,1)S(1)}, u32[]{:S(2)}, u32[]{:S(2)}) collective-permute-start(s16[16,3,16,128]{3,2,1,0:T(8,128)(2,1)S(1)} %all_to_all.11.refs_1_), channel_id=1, source_target_pairs={{0,1},{1,0},{2,3},{3,2},{4,5},{5,4},{6,7},{7,6},{8,9},{9,8},{10,11... | collective-permute-start | bytes 589832 | tf_op jit(solution)/shard_map/ppermute | solution.py:725
